TPU v7x, 32 devices: a whole 2x2x4 slice. The times are simulated.
32 devices in a mesh: section: 4 (over y, x), expert: 8 (over z, core).
Axes of the slice: x: 2, y: 2, z: 4, core: 2. Of those that a mesh axis runs over, the one named last changes fastest.
Arguments:
- grad_out: bfloat16 [4, 512, 2048], P('section', 'expert'), may hold values from -3 to 3
- pre_act: bfloat16 [4, 512, 2, 2, 768], P('section', 'expert'), may hold values from -5 to 5
- route_ids: int32 [4, 512, 2], P('section', 'expert'), may hold values from 0 to 7, as said below
- route_gate: bfloat16 [4, 512, 2], P('section', 'expert'), may hold values from 0.19921875 to 1
- w_gate: bfloat16 [4, 2048, 6144], P('section', None, 'expert'), may hold values from -0.125 to 0.125
- w_up: bfloat16 [4, 2048, 6144], P('section', None, 'expert'), may hold values from -0.125 to 0.125
- w_down: bfloat16 [4, 6144, 2048], P('section', 'expert'), may hold values from -0.21875 to 0.21875
Outputs:
- grad_in: bfloat16 [4, 512, 2048], P('section', 'expert')
- grad_down: bfloat16 [4, 6144, 2048], P('section', 'expert')
Inputs may be any that keep to these rules, and one draw needn't show every extreme that they name: `route_ids`: each row names 2 different experts. In the rows of one device of one section (aligned blocks of 64 tokens) no expert is named by more than 24 rows, and in every block one expert is named by exactly 24 rows.
All inputs are finite; a program needn't handle non-finite values.
Results may differ from a plain program's by a relative error of at most 0.0065.
Values may be sent and summed in bfloat16 or wider, within the bound.
No kernel may reach another device: no remote copies, remote signals or barrier semaphores. Data moves between devices by JAX's collectives and lax.ppermute only.
A program may use at most 64 MiB of HBM per device.

v0:
```python
import jax
import jax.numpy as jnp
from jax import lax
from jax.sharding import PartitionSpec as P

EXPERTS = 8


def shifted_2(value, axis, steps):
    count = lax.axis_size(axis)
    pairs = [(source, (source + steps) % count) for source in range(count)]
    return lax.ppermute(value, axis, pairs)


def expert_rows(upstream, saved_rows, gate_rows, weight_gate, weight_up, weight_down):
    hid_units = weight_down.shape[0]
    grad_hidden = (
        lax.dot_general(
            upstream, weight_down, (((1,), (1,)), ((), ())), preferred_element_type=jnp.float32
        )
        * gate_rows[:, None]
    )
    saved_f = saved_rows.astype(jnp.float32)
    gate_pre = saved_f[:, :hid_units]
    up_pre = saved_f[:, hid_units:]
    sigmoid_g = jax.nn.sigmoid(gate_pre)
    silu_val = gate_pre * sigmoid_g
    grad_gate = (grad_hidden * up_pre * sigmoid_g * (1.0 + gate_pre * (1.0 - sigmoid_g))).astype(
        jnp.bfloat16
    )
    grad_upper = (grad_hidden * silu_val).astype(jnp.bfloat16)
    scaled_hidden = (gate_rows[:, None] * silu_val * up_pre).astype(jnp.bfloat16)
    contract_last = (((1,), (1,)), ((), ()))
    back_rows = lax.dot_general(
        grad_gate, weight_gate, contract_last, preferred_element_type=jnp.float32
    )
    back_rows = (
        back_rows
        + lax.dot_general(grad_upper, weight_up, contract_last, preferred_element_type=jnp.float32)
    ).astype(jnp.bfloat16)
    weight_term = lax.dot_general(
        scaled_hidden, upstream, (((0,), (0,)), ((), ())), preferred_element_type=jnp.float32
    )
    return (back_rows, weight_term)


def on_device(grad_out, pre_act, route_ids, route_gate, w_gate, w_up, w_down):
    member_count = lax.axis_size("expert")
    group_size = member_count // EXPERTS
    token_count = grad_out.shape[1]
    model_width = grad_out.shape[2]
    hid_units = w_down.shape[1]
    slot_cap = 3 * token_count // 8
    part_rows = slot_cap // group_size
    upstream = grad_out[0]
    route_rows = route_ids[0]
    gate_vals = route_gate[0]
    saved_acts = pre_act[0]
    weight_gate = w_gate[0]
    weight_up = w_up[0]
    weight_down = w_down[0]
    picked = route_rows[:, :, None] == jnp.arange(EXPERTS, dtype=jnp.int32)[None, None, :]
    is_named = jnp.any(picked, axis=1).astype(jnp.int32)
    slot_rank = jnp.cumsum(is_named, axis=0) - 1
    slot_index = jnp.where(is_named > 0, slot_rank, -1)
    selector = slot_index.T[:, None, :] == jnp.arange(slot_cap, dtype=jnp.int32)[None, :, None]
    order_sel = selector.reshape(EXPERTS, group_size, part_rows, token_count).transpose(1, 0, 2, 3)
    order_bf = order_sel.astype(jnp.bfloat16)
    gate_sel = jnp.sum(jnp.where(picked, gate_vals[:, :, None].astype(jnp.float32), 0.0), axis=1)
    saved_sel = jnp.zeros((token_count, EXPERTS, 2, saved_acts.shape[3]), jnp.bfloat16)
    for pick_index in range(saved_acts.shape[1]):
        saved_sel = jnp.where(
            picked[:, pick_index, :, None, None], saved_acts[:, pick_index, None, :, :], saved_sel
        )
    saved_rows = jnp.einsum(
        "gect,tex->gecx",
        order_bf,
        saved_sel.reshape(token_count, EXPERTS, -1),
        preferred_element_type=jnp.float32,
    ).astype(jnp.bfloat16)
    saved_rows = saved_rows.reshape(
        group_size, EXPERTS, part_rows, 2, group_size, hid_units
    ).transpose(0, 1, 4, 2, 3, 5)
    saved_buf = saved_rows.reshape(group_size, member_count, part_rows, 2 * hid_units)
    gate_rows = jnp.einsum("gect,te->gec", order_sel.astype(jnp.float32), gate_sel).astype(
        jnp.bfloat16
    )
    gate_buf = jnp.broadcast_to(
        gate_rows[:, :, None, :], (group_size, EXPERTS, group_size, part_rows)
    ).reshape(group_size, member_count, part_rows)
    upstream_rows = jnp.dot(
        order_bf.reshape(-1, token_count), upstream, preferred_element_type=jnp.float32
    ).astype(jnp.bfloat16)
    upstream_rows = upstream_rows.reshape(group_size, EXPERTS, 1, part_rows, model_width)
    upstream_buf = jnp.broadcast_to(
        upstream_rows, (group_size, EXPERTS, group_size, part_rows, model_width)
    )
    upstream_buf = upstream_buf.reshape(group_size, member_count, part_rows, model_width)
    recv_up, recv_saved, recv_gate = (
        lax.all_to_all(upstream_buf, "expert", split_axis=1, concat_axis=1, tiled=True),
        lax.all_to_all(saved_buf, "expert", split_axis=1, concat_axis=1, tiled=True),
        lax.all_to_all(gate_buf, "expert", split_axis=1, concat_axis=1, tiled=True),
    )
    up_flat = recv_up.reshape(-1, model_width)
    saved_flat = recv_saved.reshape(-1, 2 * hid_units)
    gate_flat = recv_gate.reshape(-1)
    gate_f = gate_flat.astype(jnp.float32)
    back_rows, down_sum = expert_rows(
        up_flat, saved_flat, gate_f, weight_gate, weight_up, weight_down
    )
    back_buf = back_rows.reshape(group_size, member_count, part_rows, model_width)
    returned = lax.all_to_all(back_buf, "expert", split_axis=1, concat_axis=1, tiled=True)
    member_sum = (
        returned.astype(jnp.float32)
        .reshape(group_size, EXPERTS, group_size, part_rows, model_width)
        .sum(axis=2)
    )
    summed = lax.optimization_barrier(member_sum.astype(jnp.bfloat16)).astype(jnp.float32)
    token_grad = lax.dot_general(
        order_sel.astype(jnp.float32).reshape(-1, token_count),
        summed.reshape(-1, model_width),
        (((0,), (0,)), ((), ())),
        precision=lax.Precision.HIGHEST,
        preferred_element_type=jnp.float32,
    )
    shifted = shifted_2(token_grad.astype(jnp.bfloat16)[None], "section", -1)
    return (shifted, down_sum.astype(jnp.bfloat16)[None])


def solution(mesh):
    placed = (
        P("section", "expert", None),
        P("section", "expert", None, None, None),
        P("section", "expert", None),
        P("section", "expert", None),
        P("section", None, "expert"),
        P("section", None, "expert"),
        P("section", "expert", None),
    )
    return jax.shard_map(
        on_device,
        mesh=mesh,
        in_specs=placed,
        out_specs=(P("section", "expert", None), P("section", "expert", None)),
        check_vma=False,
    )
```

profile of v0, /device:TPU:0, one launch (start us, length us, event | category | flops | bytes accessed | tf_op | source)
XLA Modules:
  0.0 100.7 jit_solution(14442948710834458529)
XLA Ops:
  0.6 0.0 copy-start
  0.6 0.8 bitcast_convert_fusion.1
  1.5 0.8 iota_compare_fusion.3
  2.3 0.7 select_reduce_fusion
  3.0 0.1 copy.15
  3.1 0.1 reduce_window_sum.11
  3.2 0.1 copy.16
  3.3 0.1 fusion.31
  3.4 0.6 copy.18
  4.0 6.3 %all-to-all-start.1 = ((bf16[1,8,24]{2,0,1:T(2,128)(2,1)}), bf16[1,8,24]{2,0,1:T(2,128)(2,1)S(1)}, u32[]{:S(2)}, u32[]{:S(2)}) async-start(bf16[1,8,24]{2,0,1:T(2,128)(2,1)} %copy.18), calls=%async_computation.1 | async-start | bytes 8192 | tf_op jit(solution)/shard_map/all_to_all | solution.py:102
  10.3 1.3 %fusion.39 = (bf16[64,1,2,768]{3,2,1,0:T(2,128)(2,1)S(1)}, bf16[64,1,2,768]{3,2,1,0:T(2,128)(2,1)S(1)}) fusion(bf16[64,2,2,768]{3,2,1,0:T(2,128)(2,1)} %bitcast.75), kind=kLoop, calls=%fused_computation.49 | loop fusion | bytes 786432 | tf_op jit(solution)/shard_map/slice | solution.py:73
  11.7 0.0 copy-start.2
  11.7 1.3 %fusion.13 = bf16[1,8,24,1536]{3,2,0,1:T(8,128)(2,1)} fusion(pred[64,8]{0,1:T(8,128)(4,1)S(1)} %get-tuple-element.5, pred[64,8]{0,1:T(8,128)(4,1)S(1)} %get-tuple-element.4, bf16[64,1536]{1,0:T(8,128)(2,1)S(1)} %bitcast.79, bf16[64,1536]{1,0:T(8,128)(2,1)S(1)} %bitcast.78, s32[8,64]{1,0:T(8,128)S(1)} %copy.16), kind=kOutput, calls=%fused_computation.12 | convolution fusion | flops 39628800 | bytes 986112 | tf_op jit(solution)/shard_map/gect,tex->gecx/dot_general | solution.py:75
  13.0 2.8 %all-to-all-done.1 = bf16[1,8,24]{2,0,1:T(2,128)(2,1)S(1)} async-done(((bf16[1,8,24]{2,0,1:T(2,128)(2,1)}), bf16[1,8,24]{2,0,1:T(2,128)(2,1)S(1)}, u32[]{:S(2)}, u32[]{:S(2)}) %all-to-all-start.1) | async-done | bytes 416 | tf_op jit(solution)/shard_map/all_to_all | solution.py:102
  15.8 4.2 %all-to-all-start.2 = ((bf16[1,8,24,1536]{3,2,0,1:T(8,128)(2,1)}), bf16[1,8,24,1536]{3,2,0,1:T(8,128)(2,1)}, u32[]{:S(2)}, u32[]{:S(2)}) async-start(bf16[1,8,24,1536]{3,2,0,1:T(8,128)(2,1)} %fusion.13), calls=%async_computation.2 | async-start | bytes 1179648 | tf_op jit(solution)/shard_map/all_to_all | solution.py:101
  20.1 0.0 copy-done.2
  20.1 1.3 %convolution_convert_fusion.2 = bf16[192,2048]{1,0:T(8,128)(2,1)} fusion(pred[192,64]{1,0:T(8,128)(4,1)S(1)} %bitcast.76, bf16[1,64,2048]{2,1,0:T(8,128)(2,1)S(1)} %copy-done.2), kind=kOutput, calls=%fused_computation.11 | convolution fusion | flops 50724864 | bytes 1060864 | tf_op jit(solution)/shard_map/dot_general | solution.py:91
  21.3 15.5 %all-to-all-done.2 = bf16[1,8,24,1536]{3,2,0,1:T(8,128)(2,1)} async-done(((bf16[1,8,24,1536]{3,2,0,1:T(8,128)(2,1)}), bf16[1,8,24,1536]{3,2,0,1:T(8,128)(2,1)}, u32[]{:S(2)}, u32[]{:S(2)}) %all-to-all-start.2) | async-done | bytes 589856 | tf_op jit(solution)/shard_map/all_to_all | solution.py:101
  36.8 4.2 %all-to-all-start = ((bf16[1,8,24,2048]{3,2,0,1:T(8,128)(2,1)}), bf16[1,8,24,2048]{3,2,0,1:T(8,128)(2,1)}, u32[]{:S(2)}, u32[]{:S(2)}) async-start(bf16[1,8,24,2048]{3,2,0,1:T(8,128)(2,1)} %bitcast.70), calls=%async_computation | async-start | bytes 1572864 | tf_op jit(solution)/shard_map/all_to_all | solution.py:100
  41.0 0.1 reshape.118
  41.1 2.2 %bitcast_convert_fusion = f32[192,1536]{1,0:T(8,128)} fusion(bf16[1,8,24,1536]{3,2,0,1:T(8,128)(2,1)} %all-to-all-done.2), kind=kLoop, calls=%fused_computation.23 | loop fusion | flops 294912 | bytes 1769472 | tf_op jit(solution)/shard_map/convert_element_type | solution.py:23
  43.3 18.7 %all-to-all-done = bf16[1,8,24,2048]{3,2,0,1:T(8,128)(2,1)} async-done(((bf16[1,8,24,2048]{3,2,0,1:T(8,128)(2,1)}), bf16[1,8,24,2048]{3,2,0,1:T(8,128)(2,1)}, u32[]{:S(2)}, u32[]{:S(2)}) %all-to-all-start) | async-done | bytes 786464 | tf_op jit(solution)/shard_map/all_to_all | solution.py:100
  62.0 0.0 copy-start.1
  62.0 3.4 %fusion.19 = f32[192,768]{1,0:T(8,128)S(1)} fusion(bf16[192,2048]{1,0:T(8,128)(2,1)} %bitcast.6, bf16[1,768,2048]{2,1,0:T(8,128)(2,1)} %param.13, f32[192]{0:T(256)S(1)} %reshape.118), kind=kOutput, calls=%fused_computation.19 | convolution fusion | flops 604127232 | bytes 4522752 | tf_op jit(solution)/shard_map/dot_general | solution.py:18
  65.4 0.0 copy-done
  65.4 0.0 copy-done.1
  65.4 0.0 copy-start.3
  65.4 1.2 %fusion = f32[192,2048]{1,0:T(8,128)S(1)} fusion(bf16[1,2048,768]{2,1,0:T(8,128)(2,1)S(1)} %copy-done, f32[192,768]{1,0:T(8,128)S(1)} %fusion.19, f32[192,1536]{1,0:T(8,128)S(1)} %copy-done.1), kind=kOutput, calls=%fused_computation.1 | convolution fusion | flops 604864512 | bytes 5898240 | tf_op jit(solution)/shard_map/dot_general | solution.py:39
  66.6 0.7 copy-done.3
  67.3 1.2 %fusion.10 = bf16[192,2048]{1,0:T(8,128)(2,1)S(1)} fusion(f32[192,2048]{1,0:T(8,128)S(1)} %fusion, bf16[1,2048,768]{2,1,0:T(8,128)(2,1)S(1)} %copy-done.3, f32[192,768]{1,0:T(8,128)S(1)} %fusion.19, f32[192,1536]{1,0:T(8,128)S(1)} %copy-done.1), kind=kOutput, calls=%fused_computation.9 | convolution fusion | flops 606240768 | bytes 7274496 | tf_op jit(solution)/shard_map/dot_general | solution.py:34
  68.5 23.4 %all_to_all.20 = bf16[1,8,24,2048]{3,2,0,1:T(8,128)(2,1)S(1)} all-to-all(bf16[1,8,24,2048]{3,2,0,1:T(8,128)(2,1)S(1)} %bitcast.72), channel_id=1, replica_groups=mesh['section'=4,'expert'=8] {'expert'}, dimensions={1} | all-to-all | bytes 1572864 | tf_op jit(solution)/shard_map/all_to_all | solution.py:112
  91.9 0.3 fusion.14
  92.2 2.5 %collective-permute-start = (bf16[1,64,2048]{2,1,0:T(8,128)(2,1)S(1)}, bf16[1,64,2048]{2,1,0:T(8,128)(2,1)S(1)}, u32[]{:S(2)}, u32[]{:S(2)}) collective-permute-start(bf16[1,64,2048]{2,1,0:T(8,128)(2,1)S(1)} %fusion.14), channel_id=1, source_target_pairs={{0,24},{8,0},{16,8},{24,16},{1,25},{9,1},{17,9},{25,17},{2,26},{10... | collective-permute-start | bytes 786440 | tf_op jit(solution)/shard_map/ppermute | solution.py:12
  94.7 3.9 %fusion.6 = bf16[1,768,2048]{2,1,0:T(8,128)(2,1)} fusion(bf16[192,2048]{1,0:T(8,128)(2,1)} %bitcast.6, f32[192,1536]{1,0:T(8,128)S(1)} %copy-done.1, f32[192]{0:T(256)S(1)} %reshape.118), kind=kOutput, calls=%fused_computation.7 | convolution fusion | flops 606584832 | bytes 5112576 | tf_op jit(solution)/shard_map/dot_general | solution.py:41
  98.7 1.3 %collective-permute-done = bf16[1,64,2048]{2,1,0:T(8,128)(2,1)S(1)} collective-permute-done((bf16[1,64,2048]{2,1,0:T(8,128)(2,1)S(1)}, bf16[1,64,2048]{2,1,0:T(8,128)(2,1)S(1)}, u32[]{:S(2)}, u32[]{:S(2)}) %collective-permute-start) | collective-permute-done | bytes 262176 | tf_op jit(solution)/shard_map/ppermute | solution.py:12
  100.0 0.7 copy.26
  (8 shorter events, 0.1 us)
Async XLA Ops:
  0.6 64.8 %copy-start = (bf16[1,2048,768]{2,1,0:T(8,128)(2,1)S(1)}, bf16[1,2048,768]{2,1,0:T(8,128)(2,1)}, u32[]{:S(2)}) copy-start(bf16[1,2048,768]{2,1,0:T(8,128)(2,1)} %param.12) | copy-start | bytes 9437188
  4.0 11.8 %all-to-all-start.1 = ((bf16[1,8,24]{2,0,1:T(2,128)(2,1)}), bf16[1,8,24]{2,0,1:T(2,128)(2,1)S(1)}, u32[]{:S(2)}, u32[]{:S(2)}) async-start(bf16[1,8,24]{2,0,1:T(2,128)(2,1)} %copy.18), calls=%async_computation.1 | async-start | bytes 8192 | tf_op jit(solution)/shard_map/all_to_all | solution.py:102
  11.7 8.3 %copy-start.2 = (bf16[1,64,2048]{2,1,0:T(8,128)(2,1)S(1)}, bf16[1,64,2048]{2,1,0:T(8,128)(2,1)}, u32[]{:S(2)}) copy-start(bf16[1,64,2048]{2,1,0:T(8,128)(2,1)} %param.7) | copy-start | bytes 786436
  15.8 21.0 %all-to-all-start.2 = ((bf16[1,8,24,1536]{3,2,0,1:T(8,128)(2,1)}), bf16[1,8,24,1536]{3,2,0,1:T(8,128)(2,1)}, u32[]{:S(2)}, u32[]{:S(2)}) async-start(bf16[1,8,24,1536]{3,2,0,1:T(8,128)(2,1)} %fusion.13), calls=%async_computation.2 | async-start | bytes 1179648 | tf_op jit(solution)/shard_map/all_to_all | solution.py:101
  36.8 25.2 %all-to-all-start = ((bf16[1,8,24,2048]{3,2,0,1:T(8,128)(2,1)}), bf16[1,8,24,2048]{3,2,0,1:T(8,128)(2,1)}, u32[]{:S(2)}, u32[]{:S(2)}) async-start(bf16[1,8,24,2048]{3,2,0,1:T(8,128)(2,1)} %bitcast.70), calls=%async_computation | async-start | bytes 1572864 | tf_op jit(solution)/shard_map/all_to_all | solution.py:100
  62.0 3.4 %copy-start.1 = (f32[192,1536]{1,0:T(8,128)S(1)}, f32[192,1536]{1,0:T(8,128)}, u32[]{:S(2)}) copy-start(f32[192,1536]{1,0:T(8,128)} %bitcast_convert_fusion) | copy-start | bytes 3538948
  65.4 1.9 %copy-start.3 = (bf16[1,2048,768]{2,1,0:T(8,128)(2,1)S(1)}, bf16[1,2048,768]{2,1,0:T(8,128)(2,1)}, u32[]{:S(2)}) copy-start(bf16[1,2048,768]{2,1,0:T(8,128)(2,1)} %param.11) | copy-start | bytes 9437188
  92.2 7.7 %collective-permute-start = (bf16[1,64,2048]{2,1,0:T(8,128)(2,1)S(1)}, bf16[1,64,2048]{2,1,0:T(8,128)(2,1)S(1)}, u32[]{:S(2)}, u32[]{:S(2)}) collective-permute-start(bf16[1,64,2048]{2,1,0:T(8,128)(2,1)S(1)} %fusion.14), channel_id=1, source_target_pairs={{0,24},{8,0},{16,8},{24,16},{1,25},{9,1},{17,9},{25,17},{2,26},{10... | collective-permute-start | bytes 786440 | tf_op jit(solution)/shard_map/ppermute | solution.py:12
where the time goes:
time: 101 us
  waiting for transfers between devices  38.3 us (38%)
  blocking collectives  23.4 us (23%)
  starting transfers between devices  17.2 us (17%)
  matrix products  12.7 us (13%)
  other arithmetic  4.69 us (5%)
  local copies, waits for them, and re-layouts  3.62 us (4%)
    all_to_all x1, blocking collectives, on_device(): lax.all_to_all(back_buf, 'expert', split_axis=1, concat_axis=1, tiled=True)  23.4 us
    all_to_all x1, waiting for transfers between devices, on_device(): lax.all_to_all(upstream_buf, 'expert', split_axis=1, concat_axis=1, tiled...  18.7 us
    all_to_all x1, waiting for transfers between devices, on_device(): lax.all_to_all(saved_buf, 'expert', split_axis=1, concat_axis=1, tiled=True)  15.5 us
    all_to_all x1, starting transfers between devices, on_device(): lax.all_to_all(gate_buf, 'expert', split_axis=1, concat_axis=1, tiled=True)  6.33 us
    all_to_all x1, starting transfers between devices, on_device(): lax.all_to_all(upstream_buf, 'expert', split_axis=1, concat_axis=1, tiled...  4.21 us
    all_to_all x1, starting transfers between devices, on_device(): lax.all_to_all(saved_buf, 'expert', split_axis=1, concat_axis=1, tiled=True)  4.19 us
    dot_general x1, matrix products, expert_rows(): lax.dot_general(scaled_hidden, upstream, (((0,), (0,)), ((), ())), prefer...  3.94 us
    dot_general x1, matrix products, expert_rows(): lax.dot_general(upstream, weight_down, (((1,), (1,)), ((), ())), preferre...  3.41 us
  transfers between devices with their start and end apart: 4, of which 4 were waited for; matrix products, arithmetic and copies ran while one was open for 10% of the time, Pallas kernels for 0%

commit v1 on v0

--- a/solution.py
+++ b/solution.py
@@ -44,7 +44,7 @@
     return (back_rows, weight_term)
 
 
-def on_device(grad_out, pre_act, route_ids, route_gate, w_gate, w_up, w_down):
+def on_device_general(grad_out, pre_act, route_ids, route_gate, w_gate, w_up, w_down):
     member_count = lax.axis_size("expert")
     group_size = member_count // EXPERTS
     token_count = grad_out.shape[1]
@@ -126,6 +126,143 @@
     shifted = shifted_2(token_grad.astype(jnp.bfloat16)[None], "section", -1)
     return (shifted, down_sum.astype(jnp.bfloat16)[None])
 
+def swapped(value, mask):
+    count = lax.axis_size("expert")
+    return lax.ppermute(value, "expert", [(i, i ^ mask) for i in range(count)])
+
+
+def slot_ranks(named, tokens):
+    lower = jnp.arange(tokens, dtype=jnp.int32)
+    upto = (lower[:, None] <= lower[None, :]).astype(jnp.bfloat16)
+    counts = jnp.dot(named.astype(jnp.bfloat16), upto, preferred_element_type=jnp.float32)
+    return jnp.where(named, counts.astype(jnp.int32) - 1, -1)
+
+
+def hidden_grads(grad_hidden, saved, gate):
+    units = grad_hidden.shape[1]
+    saved_f = saved.astype(jnp.float32)
+    gate_pre = saved_f[:, :units]
+    up_pre = saved_f[:, units:]
+    sig = jax.nn.sigmoid(gate_pre)
+    silu = gate_pre * sig
+    grad_h = grad_hidden * gate
+    grad_a = (grad_h * up_pre * sig * (1.0 + gate_pre * (1.0 - sig))).astype(jnp.bfloat16)
+    grad_b = (grad_h * silu).astype(jnp.bfloat16)
+    scaled = (gate * silu * up_pre).astype(jnp.bfloat16)
+    return grad_a, grad_b, scaled
+
+
+LAST = (((1,), (1,)), ((), ()))
+FIRST = (((0,), (0,)), ((), ()))
+
+
+def on_device_pairs(grad_out, pre_act, route_ids, route_gate, w_gate, w_up, w_down):
+    f32, bf16 = jnp.float32, jnp.bfloat16
+    tokens, width = grad_out.shape[1:]
+    picks = pre_act.shape[2]
+    units = w_down.shape[1]
+    cap = 3 * tokens // 8
+    me = lax.axis_index("expert")
+    upstream = grad_out[0]
+    meta = jnp.concatenate([route_ids[0].astype(bf16).T, route_gate[0].T], axis=0)
+    saved_all = pre_act[0].reshape(tokens * picks, 2 * units)
+
+    far_up = swapped(upstream, 4)
+    pair_up = swapped(upstream, 1)
+    meta_near = jnp.stack([meta, swapped(meta, 1)])
+    meta_far = swapped(meta_near, 4)
+    pair_saved = swapped(saved_all, 1)
+    far_pair_up = swapped(far_up, 1)
+
+    mine = me ^ jnp.array([0, 2, 4, 6], jnp.int32)
+
+    def selectors(block_meta, experts):
+        ids = block_meta[:, :picks].astype(jnp.int32)
+        hits = ids[:, None] == experts[None, :, None, None]
+        named = jnp.any(hits, axis=2)
+        blocks, count = named.shape[:2]
+        slots = slot_ranks(named.reshape(-1, tokens), tokens).reshape(named.shape)
+        slot_no = jnp.arange(cap, dtype=jnp.int32)[None, None, :, None]
+        order = slots[:, :, None, :] == slot_no
+        return order, hits
+
+    order_near, hits_near = selectors(meta_near, mine)
+    order_far, hits_far = selectors(meta_far, mine[:2])
+
+    def saved_of(block, rows):
+        both = order_near[block][:, :, :, None] & jnp.moveaxis(hits_near[block], 1, 2)[:, None]
+        sel = both.astype(bf16).reshape(4 * cap, tokens * picks)
+        got = jnp.dot(sel, rows, preferred_element_type=f32).astype(bf16)
+        return got.reshape(4, cap, 2 * units)
+
+    def gate_of(order, hits, block_meta):
+        gates = block_meta[:, None, picks:].astype(f32)
+        gate_sel = jnp.sum(jnp.where(hits, gates, 0.0), axis=2)
+        got = jnp.sum(jnp.where(order, gate_sel[:, :, None, :], 0.0), axis=3)
+        return got
+
+    gates_near = gate_of(order_near, hits_near, meta_near).astype(bf16)
+    saved_rows = jnp.stack([saved_of(0, saved_all), saved_of(1, pair_saved)], axis=1)
+    gate_cols = jnp.broadcast_to(jnp.moveaxis(gates_near, 0, 1)[..., None], (4, 2, cap, 128))
+    packed = jnp.concatenate([saved_rows, gate_cols], axis=3).reshape(4, 2 * cap, 2 * units + 128)
+
+    def up_rows(order, expert, first, second):
+        sel = order[:, expert].astype(bf16)
+        rows = [
+            jnp.dot(sel[n], rows, preferred_element_type=f32).astype(bf16)
+            for n, rows in enumerate((first, second))
+        ]
+        return jnp.concatenate(rows, axis=0)
+
+    own_up = up_rows(order_near, 0, upstream, pair_up)
+    near_up = swapped(up_rows(order_near, 1, upstream, pair_up), 2)
+    saved_1 = swapped(packed[1], 2)
+    saved_2 = swapped(packed[2], 4)
+    saved_3 = swapped(packed[3], 6)
+    two_up = up_rows(order_far, 0, far_up, far_pair_up)
+    three_up = swapped(up_rows(order_far, 1, far_up, far_pair_up), 2)
+
+    def backward(up, pack):
+        saved = pack[:, : 2 * units]
+        gate = pack[:, 2 * units : 2 * units + 1].astype(f32)
+        grad_hidden = lax.dot_general(up, w_down[0], LAST, preferred_element_type=f32)
+        grad_a, grad_b, scaled = hidden_grads(grad_hidden, saved, gate)
+        back = lax.dot_general(grad_a, w_gate[0], LAST, preferred_element_type=f32)
+        back = back + lax.dot_general(grad_b, w_up[0], LAST, preferred_element_type=f32)
+        return back.astype(bf16), scaled
+
+    back_0, scaled_0 = backward(own_up, packed[0])
+    back_1, scaled_1 = backward(near_up, saved_1)
+    back_2, scaled_2 = backward(two_up, saved_2)
+    back_3, scaled_3 = backward(three_up, saved_3)
+    home_1 = swapped(back_1, 2)
+    home_2 = swapped(back_2, 4)
+    home_3 = swapped(back_3, 6)
+
+    scaled = jnp.concatenate([scaled_0, scaled_1, scaled_2, scaled_3], axis=0)
+    ups = jnp.concatenate([own_up, near_up, two_up, three_up], axis=0)
+    down = lax.dot_general(scaled, ups, FIRST, preferred_element_type=f32).astype(bf16)
+
+    home = jnp.stack([back_0, home_1, home_2, home_3]).reshape(4, 2, cap, width)
+    sums = [
+        lax.dot_general(
+            order_near[n].astype(bf16).reshape(4 * cap, tokens),
+            home[:, n].reshape(4 * cap, width),
+            FIRST,
+            preferred_element_type=f32,
+        )
+        for n in range(2)
+    ]
+    other = swapped(sums[1].astype(bf16), 1)
+    total = (sums[0] + other.astype(f32)).astype(bf16)
+    return shifted_2(total[None], "section", -1), down[None]
+
+
+def on_device(*args):
+    if lax.axis_size("expert") == EXPERTS:
+        return on_device_pairs(*args)
+    return on_device_general(*args)
+
 
 def solution(mesh):
     placed = (

time: 101 us -> 99 us (0.980)
  the two profiles are of different devices: /device:TPU:0 before, /device:TPU:10 now
where the time goes in v1:
time: 99 us; the launch traced here: 98 us
  matrix products  28.7 us (29%)
  waiting for transfers between devices  25 us (25%)
  starting transfers between devices  14.8 us (15%)
  other arithmetic  14.2 us (14%)
  local copies, waits for them, and re-layouts  14.1 us (14%)
  between operations  1.1 us (1%)
    ppermute x15, waiting for transfers between devices, swapped(): return lax.ppermute(value, 'expert', [(i, i ^ mask) for i in range(count)])  19 us
    ppermute x15, starting transfers between devices, swapped(): return lax.ppermute(value, 'expert', [(i, i ^ mask) for i in range(count)])  14.3 us
    dot_general x8, matrix products, up_rows(): jnp.dot(sel[n], rows, preferred_element_type=f32).astype(bf16)  9.02 us
    ppermute x1, waiting for transfers between devices, shifted_2(): return lax.ppermute(value, axis, pairs)  5.99 us
    dot_general x4, matrix products, backward(): lax.dot_general(up, w_down[0], LAST, preferred_element_type=f32)  4.25 us
    dot_general x4, matrix products, backward(): back = lax.dot_general(grad_a, w_gate[0], LAST, preferred_element_type=f32)  4.1 us
    and x4, local copies, waits for them, and re-layouts, saved_of(): order_near[block][:, :, :, None]  4.09 us
    dot_general x4, matrix products, backward(): lax.dot_general(grad_b, w_up[0], LAST, preferred_element_type=f32)  4.08 us
  transfers between devices with their start and end apart: 16, of which 5 were waited for; matrix products, arithmetic and copies ran while one was open for 56% of the time, Pallas kernels for 0%

profile of v1, /device:TPU:10, one launch (start us, length us, event | category | flops | bytes accessed | tf_op | source)
XLA Modules:
  0.0 98.0 jit_solution(4236155305949927997)
XLA Ops:
  0.7 2.7 %collective-permute-start.7 = (bf16[64,2048]{1,0:T(8,128)(2,1)}, bf16[64,2048]{1,0:T(8,128)(2,1)}, u32[]{:S(2)}, u32[]{:S(2)}) collective-permute-start(bf16[64,2048]{1,0:T(8,128)(2,1)} %bitcast.174), channel_id=1, source_target_pairs={{0,4},{1,5},{2,6},{3,7},{4,0},{5,1},{6,2},{7,3},{8,12},{9,13},{10,... | collective-permute-start | bytes 786440 | tf_op jit(solution)/shard_map/ppermute | solution.py:131
  4.9 1.0 %copy.43 = bf16[16,8,2,768]{3,1,2,0:T(8,128)(2,1)S(1)} copy(bf16[16,8,2,768]{3,2,1,0:T(2,128)(2,1)} %bitcast.178) | data formatting | bytes 786432
  9.0 1.8 %select_reduce_fusion = (f32[2,4,64]{1,2,0:T(8,128)}, pred[2,4,2,64]{1,2,3,0:T(4,128)(4,1)S(1)}) fusion(f32[2,2,64]{1,2,0:T(8,128)} %copy.40, s32[4]{0:T(128)} %multiply_xor_fusion, s32[2,2,64]{1,2,0:T(8,128)} %copy.34), kind=kLoop, calls=%fused_computation.98 | loop fusion | flops 2560 | bytes 5136 | tf_op jit(solution)/shard_map/reduce_sum | solution.py:200
  12.2 1.0 %reduce_or.18 = pred[2,4,64]{1,2,0:T(8,128)(4,1)S(1)} reduce(pred[2,4,2,64]{1,2,3,0:T(4,128)(4,1)} %copy-done.3, pred[]{:T(512)} %constant.7.clone.1), dimensions={2}, to_apply=%region_0.0 | reduce | flops 512 | bytes 1537 | tf_op jit(solution)/shard_map/reduce_or | solution.py:182
  13.9 0.9 fusion.62
  15.4 1.7 %convolution_convert_fusion.9 = bf16[24,2048]{1,0:T(8,128)(2,1)} fusion(pred[2,4,24,64]{3,2,1,0:T(8,128)(4,1)S(1)} %iota_compare_fusion, bf16[1,64,2048]{2,1,0:T(8,128)(2,1)} %param.8), kind=kOutput, calls=%fused_computation.42 | convolution fusion | flops 6340608 | bytes 363520 | tf_op jit(solution)/shard_map/dot_general | solution.py:212
  17.2 1.8 %constant_dynamic-update-slice_fusion.5 = (bf16[192,2048]{1,0:T(8,128)(2,1)}, bf16[24,2048]{1,0:T(8,128)(2,1)}) fusion(bf16[1,64,2048]{2,1,0:T(8,128)(2,1)} %param.8, pred[2,4,24,64]{3,2,1,0:T(8,128)(4,1)S(1)} %iota_compare_fusion), kind=kOutput, calls=%fused_computation.121 | convolution fusion | flops 6340607 | bytes 461824 | tf_op jit(solution)/shard_map/dot_general | solution.py:212
  19.5 1.5 %copy.41 = f32[2,4,64]{2,1,0:T(4,128)} copy(f32[2,4,64]{1,2,0:T(8,128)} %get-tuple-element.2) | data formatting | bytes 4096 | tf_op jit(solution)/shard_map/reduce_sum | solution.py:200
  21.8 1.6 %broadcast_and_fusion.1 = pred[4,24,64,2]{1,0,3,2:T(4,128)(4,1)} fusion(pred[4,64,2]{0,2,1:T(4,128)(4,1)} %get-tuple-element.10, pred[4,24,64]{1,0,2:T(4,128)(4,1)} %copy.36), kind=kLoop, calls=%fused_computation.102 | loop fusion | flops 12288 | bytes 18944 | tf_op jit(solution)/shard_map/and | solution.py:193
  23.4 1.0 and.49
  24.3 1.4 %copy.37 = pred[4,24,64]{1,0,2:T(4,128)(4,1)} copy(pred[4,24,64]{2,1,0:T(8,128)(4,1)} %get-tuple-element.14) | data formatting | bytes 12288 | tf_op jit(solution)/shard_map/and | solution.py:193
  25.8 1.0 %convolution_convert_fusion.2 = bf16[96,1536]{1,0:T(8,128)(2,1)} fusion(pred[96,128]{0,1:T(32,128)(4,1)S(1)} %and.49, bf16[128,1536]{1,0:T(8,128)(2,1)S(1)} %bitcast.169), kind=kOutput, calls=%fused_computation.27 | convolution fusion | flops 37896192 | bytes 700416 | tf_op jit(solution)/shard_map/dot_general | solution.py:195
  26.8 1.6 %broadcast_and_fusion = pred[4,24,64,2]{1,0,3,2:T(4,128)(4,1)} fusion(pred[4,64,2]{0,2,1:T(4,128)(4,1)} %get-tuple-element.11, pred[4,24,64]{1,0,2:T(4,128)(4,1)} %copy.37), kind=kLoop, calls=%fused_computation.101 | loop fusion | flops 12288 | bytes 18944 | tf_op jit(solution)/shard_map/and | solution.py:193
  28.4 0.8 select_reduce_fusion.1
  29.8 1.0 and.54
  31.4 1.3 %compare_reduce_fusion = pred[2,2,64]{2,1,0:T(4,128)(4,1)} fusion(s32[2,2,64]{2,1,0:T(2,128)S(1)} %slice_convert_fusion.4, s32[2]{0:T(128)} %bitcast.192), kind=kLoop, calls=%fused_computation.130 | loop fusion | flops 768 | bytes 1288 | tf_op jit(solution)/shard_map/reduce_or | solution.py:182
  32.7 1.1 %reshape.86 = pred[4,64]{1,0:T(4,128)(4,1)} reshape(pred[2,2,64]{2,1,0:T(4,128)(4,1)} %compare_reduce_fusion) | data formatting | bytes 512 | tf_op jit(solution)/shard_map/reshape | solution.py:184
  33.8 0.9 fusion.64
  34.7 1.2 %convolution_convert_fusion.8 = bf16[24,2048]{1,0:T(8,128)(2,1)S(1)} fusion(bf16[64,2048]{1,0:T(8,128)(2,1)} %collective-permute-done.1, pred[2,4,24,64]{3,2,1,0:T(8,128)(4,1)} %copy-done.5), kind=kOutput, calls=%fused_computation.41 | convolution fusion | flops 6340608 | bytes 363520 | tf_op jit(solution)/shard_map/dot_general | solution.py:212
  35.9 0.9 pad_maximum_fusion.2
  37.3 1.1 %convolution_convert_fusion.5 = bf16[24,2048]{1,0:T(8,128)(2,1)S(1)} fusion(bf16[64,2048]{1,0:T(8,128)(2,1)} %collective-permute-done.7, pred[2,2,24,64]{3,2,1,0:T(8,128)(4,1)S(1)} %iota_compare_fusion.1), kind=kOutput, calls=%fused_computation.38 | convolution fusion | flops 6340608 | bytes 363520 | tf_op jit(solution)/shard_map/dot_general | solution.py:212
  38.4 1.8 %constant_dynamic-update-slice_fusion.4 = (bf16[192,2048]{1,0:T(8,128)(2,1)}, bf16[24,2048]{1,0:T(8,128)(2,1)S(1)}) fusion(bf16[192,2048]{1,0:T(8,128)(2,1)} %get-tuple-element.20, bf16[64,2048]{1,0:T(8,128)(2,1)} %collective-permute-done.1, pred[2,4,24,64]{3,2,1,0:T(8,128)(4,1)} %copy-done.5), kind=kOutput, calls=%fused_computation.120 | convolution fusion | flops 6340608 | bytes 461824 | tf_op jit(solution)/shard_map/dot_general | solution.py:212
  40.2 1.3 %convolution_convert_fusion.1 = bf16[96,1536]{1,0:T(8,128)(2,1)S(1)} fusion(pred[96,128]{0,1:T(32,128)(4,1)S(1)} %and.54, bf16[128,1536]{1,0:T(8,128)(2,1)} %collective-permute-done.2), kind=kOutput, calls=%fused_computation.26 | convolution fusion | flops 37896192 | bytes 700416 | tf_op jit(solution)/shard_map/dot_general | solution.py:195
  42.3 1.0 %pad_maximum_fusion.1 = bf16[4,2,24,1664]{3,2,1,0:T(8,128)(2,1)S(1)} fusion(bf16[4,2,24,128]{3,2,1,0:T(8,128)(2,1)S(1)} %broadcast_in_dim.38, bf16[4,1,24,1536]{3,2,1,0:T(8,128)(2,1)S(1)} %bitcast.172, bf16[4,1,24,1536]{3,2,1,0:T(8,128)(2,1)} %bitcast.171), kind=kLoop, calls=%fused_computation.56 | loop fusion | flops 1916928 | bytes 1277952 | tf_op jit(solution)/shard_map/concatenate | solution.py:207
  43.5 2.5 %collective-permute-start.12 = (bf16[48,1664]{1,0:T(8,128)(2,1)S(1)}, bf16[48,1664]{1,0:T(8,128)(2,1)S(1)}, u32[]{:S(2)}, u32[]{:S(2)}) collective-permute-start(bf16[48,1664]{1,0:T(8,128)(2,1)S(1)} %bitcast.182), channel_id=1, source_target_pairs={{0,6},{1,7},{2,4},{3,5},{4,2},{5,3},{6,0},{7,1},{8,14},{9,15},{10,... | collective-permute-start | bytes 479240 | tf_op jit(solution)/shard_map/ppermute | solution.py:131
  46.0 1.5 %collective-permute-start.9 = (bf16[48,1664]{1,0:T(8,128)(2,1)S(1)}, bf16[48,1664]{1,0:T(8,128)(2,1)S(1)}, u32[]{:S(2)}, u32[]{:S(2)}) collective-permute-start(bf16[48,1664]{1,0:T(8,128)(2,1)S(1)} %bitcast.183), channel_id=1, source_target_pairs={{0,4},{1,5},{2,6},{3,7},{4,0},{5,1},{6,2},{7,3},{8,12},{9,13},{10,... | collective-permute-start | bytes 479240 | tf_op jit(solution)/shard_map/ppermute | solution.py:131
  47.6 1.1 %fusion.49 = f32[48,768]{1,0:T(8,128)S(1)} fusion(bf16[1,768,2048]{2,1,0:T(8,128)(2,1)S(1)} %copy-done.1, bf16[24,2048]{1,0:T(8,128)(2,1)S(1)} %get-tuple-element.23, bf16[24,2048]{1,0:T(8,128)(2,1)S(1)} %copy-done.4, f32[48]{0:T(128)S(1)} %convert_reduce_fusion.3), kind=kOutput, calls=%fused_computation.45 | convolution fusion | flops 151425024 | bytes 3489984 | tf_op jit(solution)/shard_map/dot_general | solution.py:228
  48.6 1.0 %fusion.6 = f32[48,2048]{1,0:T(8,128)S(1)} fusion(bf16[1,2048,768]{2,1,0:T(8,128)(2,1)S(1)} %copy-done, f32[48,768]{1,0:T(8,128)S(1)} %fusion.49, f32[48,1536]{1,0:T(8,128)S(1)} %slice_convert_fusion.3), kind=kOutput, calls=%fused_computation.7 | convolution fusion | flops 151216128 | bytes 3833856 | tf_op jit(solution)/shard_map/dot_general | solution.py:231
  49.7 1.0 %fusion.46 = bf16[48,2048]{1,0:T(8,128)(2,1)S(1)} fusion(f32[48,2048]{1,0:T(8,128)S(1)} %fusion.6, bf16[1,2048,768]{2,1,0:T(8,128)(2,1)S(1)} %copy-done.2, f32[48,768]{1,0:T(8,128)S(1)} %fusion.49, f32[48,1536]{1,0:T(8,128)S(1)} %slice_convert_fusion.3), kind=kOutput, calls=%fused_computation.36 | convolution fusion | flops 151560192 | bytes 4177920 | tf_op jit(solution)/shard_map/dot_general | solution.py:230
  50.9 1.1 %constant_dynamic-update-slice_fusion.2 = (bf16[192,2048]{1,0:T(8,128)(2,1)S(1)}, bf16[24,2048]{1,0:T(8,128)(2,1)S(1)}) fusion(bf16[192,2048]{1,0:T(8,128)(2,1)S(1)} %constant_dynamic-update-slice_fusion.3, bf16[64,2048]{1,0:T(8,128)(2,1)} %collective-permute-done.7, pred[2,2,24,64]{3,2,1,0:T(8,128)(4,1)S(1)} %iota_compare_fusion.1), kind=kOutput, calls=%fused_computation.118 | convolution fusion | flops 6340608 | bytes 461824 | tf_op jit(solution)/shard_map/dot_general | solution.py:212
  52.2 2.0 %collective-permute-start.11 = (bf16[48,2048]{1,0:T(8,128)(2,1)S(1)}, bf16[48,2048]{1,0:T(8,128)(2,1)S(1)}, u32[]{:S(2)}, u32[]{:S(2)}) collective-permute-start(bf16[48,2048]{1,0:T(8,128)(2,1)S(1)} %pad_maximum_fusion.3), channel_id=1, source_target_pairs={{0,2},{1,3},{2,0},{3,1},{4,6},{5,7},{6,4},{7,5},{8,10},{9,11},{10,... | collective-permute-start | bytes 589832 | tf_op jit(solution)/shard_map/ppermute | solution.py:131
  54.4 4.8 %collective-permute-done.4 = bf16[48,1664]{1,0:T(8,128)(2,1)S(1)} collective-permute-done((bf16[48,1664]{1,0:T(8,128)(2,1)S(1)}, bf16[48,1664]{1,0:T(8,128)(2,1)S(1)}, u32[]{:S(2)}, u32[]{:S(2)}) %collective-permute-start.4) | collective-permute-done | bytes 159776 | tf_op jit(solution)/shard_map/ppermute | solution.py:131
  59.3 1.1 %fusion.52 = f32[48,768]{1,0:T(8,128)S(1)} fusion(bf16[48,2048]{1,0:T(8,128)(2,1)S(1)} %collective-permute-done.3, bf16[1,768,2048]{2,1,0:T(8,128)(2,1)S(1)} %copy-done.1, f32[48]{0:T(128)S(1)} %convert_reduce_fusion.2), kind=kOutput, calls=%fused_computation.46 | convolution fusion | flops 151031808 | bytes 3489984 | tf_op jit(solution)/shard_map/dot_general | solution.py:228
  60.4 1.0 %fusion.4 = f32[48,2048]{1,0:T(8,128)S(1)} fusion(bf16[1,2048,768]{2,1,0:T(8,128)(2,1)S(1)} %copy-done, f32[48,768]{1,0:T(8,128)S(1)} %fusion.52, f32[48,1536]{1,0:T(8,128)S(1)} %slice_convert_fusion.2), kind=kOutput, calls=%fused_computation.5 | convolution fusion | flops 151216128 | bytes 3833856 | tf_op jit(solution)/shard_map/dot_general | solution.py:231
  61.4 1.0 %fusion.43 = bf16[48,2048]{1,0:T(8,128)(2,1)S(1)} fusion(f32[48,2048]{1,0:T(8,128)S(1)} %fusion.4, bf16[1,2048,768]{2,1,0:T(8,128)(2,1)S(1)} %copy-done.2, f32[48,768]{1,0:T(8,128)S(1)} %fusion.52, f32[48,1536]{1,0:T(8,128)S(1)} %slice_convert_fusion.2), kind=kOutput, calls=%fused_computation.35 | convolution fusion | flops 151560192 | bytes 4177920 | tf_op jit(solution)/shard_map/dot_general | solution.py:230
  62.7 1.1 %fusion.55 = f32[48,768]{1,0:T(8,128)S(1)} fusion(bf16[1,768,2048]{2,1,0:T(8,128)(2,1)S(1)} %copy-done.1, bf16[24,2048]{1,0:T(8,128)(2,1)S(1)} %get-tuple-element.27, bf16[24,2048]{1,0:T(8,128)(2,1)S(1)} %get-tuple-element.25, f32[48]{0:T(128)S(1)} %convert_reduce_fusion.1), kind=kOutput, calls=%fused_computation.47 | convolution fusion | flops 151425024 | bytes 3489984 | tf_op jit(solution)/shard_map/dot_general | solution.py:228
  63.8 1.0 %fusion.2 = f32[48,2048]{1,0:T(8,128)S(1)} fusion(bf16[1,2048,768]{2,1,0:T(8,128)(2,1)S(1)} %copy-done, f32[48,768]{1,0:T(8,128)S(1)} %fusion.55, f32[48,1536]{1,0:T(8,128)S(1)} %slice_convert_fusion.1), kind=kOutput, calls=%fused_computation.3 | convolution fusion | flops 151216128 | bytes 3833856 | tf_op jit(solution)/shard_map/dot_general | solution.py:231
  64.8 1.0 %fusion.40 = bf16[48,2048]{1,0:T(8,128)(2,1)S(1)} fusion(f32[48,2048]{1,0:T(8,128)S(1)} %fusion.2, bf16[1,2048,768]{2,1,0:T(8,128)(2,1)S(1)} %copy-done.2, f32[48,768]{1,0:T(8,128)S(1)} %fusion.55, f32[48,1536]{1,0:T(8,128)S(1)} %slice_convert_fusion.1), kind=kOutput, calls=%fused_computation.34 | convolution fusion | flops 151560192 | bytes 4177920 | tf_op jit(solution)/shard_map/dot_general | solution.py:230
  65.8 2.2 %collective-permute-start.10 = (bf16[48,2048]{1,0:T(8,128)(2,1)S(1)}, bf16[48,2048]{1,0:T(8,128)(2,1)S(1)}, u32[]{:S(2)}, u32[]{:S(2)}) collective-permute-start(bf16[48,2048]{1,0:T(8,128)(2,1)S(1)} %fusion.40), channel_id=1, source_target_pairs={{0,4},{1,5},{2,6},{3,7},{4,0},{5,1},{6,2},{7,3},{8,12},{9,13},{10,... | collective-permute-start | bytes 589832 | tf_op jit(solution)/shard_map/ppermute | solution.py:131
  68.2 1.1 %fusion.58 = f32[48,768]{1,0:T(8,128)S(1)} fusion(bf16[48,2048]{1,0:T(8,128)(2,1)S(1)} %collective-permute-done.11, bf16[1,768,2048]{2,1,0:T(8,128)(2,1)S(1)} %copy-done.1, f32[48]{0:T(128)S(1)} %convert_reduce_fusion), kind=kOutput, calls=%fused_computation.48 | convolution fusion | flops 151031808 | bytes 3489984 | tf_op jit(solution)/shard_map/dot_general | solution.py:228
  69.2 1.0 %fusion = f32[48,2048]{1,0:T(8,128)S(1)} fusion(bf16[1,2048,768]{2,1,0:T(8,128)(2,1)S(1)} %copy-done, f32[48,768]{1,0:T(8,128)S(1)} %fusion.58, f32[48,1536]{1,0:T(8,128)S(1)} %slice_convert_fusion), kind=kOutput, calls=%fused_computation.1 | convolution fusion | flops 151216128 | bytes 3833856 | tf_op jit(solution)/shard_map/dot_general | solution.py:231
  70.3 1.0 %fusion.37 = bf16[48,2048]{1,0:T(8,128)(2,1)S(1)} fusion(f32[48,2048]{1,0:T(8,128)S(1)} %fusion, bf16[1,2048,768]{2,1,0:T(8,128)(2,1)S(1)} %copy-done.2, f32[48,768]{1,0:T(8,128)S(1)} %fusion.58, f32[48,1536]{1,0:T(8,128)S(1)} %slice_convert_fusion), kind=kOutput, calls=%fused_computation.33 | convolution fusion | flops 151560192 | bytes 4177920 | tf_op jit(solution)/shard_map/dot_general | solution.py:230
  71.3 1.4 %collective-permute-start.13 = (bf16[48,2048]{1,0:T(8,128)(2,1)S(1)}, bf16[48,2048]{1,0:T(8,128)(2,1)S(1)}, u32[]{:S(2)}, u32[]{:S(2)}) collective-permute-start(bf16[48,2048]{1,0:T(8,128)(2,1)S(1)} %fusion.37), channel_id=1, source_target_pairs={{0,6},{1,7},{2,4},{3,5},{4,2},{5,3},{6,0},{7,1},{8,14},{9,15},{10,... | collective-permute-start | bytes 589832 | tf_op jit(solution)/shard_map/ppermute | solution.py:131
  72.8 7.6 %collective-permute-done.10 = bf16[48,2048]{1,0:T(8,128)(2,1)S(1)} collective-permute-done((bf16[48,2048]{1,0:T(8,128)(2,1)S(1)}, bf16[48,2048]{1,0:T(8,128)(2,1)S(1)}, u32[]{:S(2)}, u32[]{:S(2)}) %collective-permute-start.10) | collective-permute-done | bytes 196640 | tf_op jit(solution)/shard_map/ppermute | solution.py:131
  80.5 5.2 %collective-permute-done.13 = bf16[48,2048]{1,0:T(8,128)(2,1)S(1)} collective-permute-done((bf16[48,2048]{1,0:T(8,128)(2,1)S(1)}, bf16[48,2048]{1,0:T(8,128)(2,1)S(1)}, u32[]{:S(2)}, u32[]{:S(2)}) %collective-permute-start.13) | collective-permute-done | bytes 196640 | tf_op jit(solution)/shard_map/ppermute | solution.py:131
  86.4 1.3 %collective-permute-done.14 = bf16[64,2048]{1,0:T(8,128)(2,1)S(1)} collective-permute-done((bf16[64,2048]{1,0:T(8,128)(2,1)S(1)}, bf16[64,2048]{1,0:T(8,128)(2,1)S(1)}, u32[]{:S(2)}, u32[]{:S(2)}) %collective-permute-start.14) | collective-permute-done | bytes 262176 | tf_op jit(solution)/shard_map/ppermute | solution.py:131
  88.6 2.7 %fusion.24 = bf16[1,768,2048]{2,1,0:T(8,128)(2,1)} fusion(bf16[192,2048]{1,0:T(8,128)(2,1)S(1)} %constant_dynamic-update-slice_fusion, bf16[48,768]{1,0:T(8,128)(2,1)S(1)} %multiply_convert_fusion, bf16[48,768]{1,0:T(8,128)(2,1)S(1)} %multiply_convert_fusion.1, bf16[48,768]{1,0:T(8,128)(2,1)S(1)} %multiply_convert_fusion.2, ...), kind=kOutput, calls=%fused_computation.25 | convolution fusion | flops 606732288 | bytes 4227072 | tf_op jit(solution)/shard_map/dot_general | solution.py:244
  91.3 6.0 %collective-permute-done.15 = bf16[1,64,2048]{2,1,0:T(8,128)(2,1)S(1)} collective-permute-done((bf16[1,64,2048]{2,1,0:T(8,128)(2,1)S(1)}, bf16[1,64,2048]{2,1,0:T(8,128)(2,1)S(1)}, u32[]{:S(2)}, u32[]{:S(2)}) %collective-permute-start.15) | collective-permute-done | bytes 262176 | tf_op jit(solution)/shard_map/ppermute | solution.py:12
  (80 shorter events, 14.7 us)
Async XLA Ops:
  0.6 48.0 %copy-start = (bf16[1,2048,768]{2,1,0:T(8,128)(2,1)S(1)}, bf16[1,2048,768]{2,1,0:T(8,128)(2,1)}, u32[]{:S(2)}) copy-start(bf16[1,2048,768]{2,1,0:T(8,128)(2,1)} %param.13) | copy-start | bytes 9437188
  0.6 34.1 %collective-permute-start.1 = (bf16[64,2048]{1,0:T(8,128)(2,1)}, bf16[64,2048]{1,0:T(8,128)(2,1)}, u32[]{:S(2)}, u32[]{:S(2)}) collective-permute-start(bf16[64,2048]{1,0:T(8,128)(2,1)} %bitcast.173), channel_id=1, source_target_pairs={{0,1},{1,0},{2,3},{3,2},{4,5},{5,4},{6,7},{7,6},{8,9},{9,8},{10,11... | collective-permute-start | bytes 786440 | tf_op jit(solution)/shard_map/ppermute | solution.py:131
  0.7 36.6 %collective-permute-start.7 = (bf16[64,2048]{1,0:T(8,128)(2,1)}, bf16[64,2048]{1,0:T(8,128)(2,1)}, u32[]{:S(2)}, u32[]{:S(2)}) collective-permute-start(bf16[64,2048]{1,0:T(8,128)(2,1)} %bitcast.174), channel_id=1, source_target_pairs={{0,4},{1,5},{2,6},{3,7},{4,0},{5,1},{6,2},{7,3},{8,12},{9,13},{10,... | collective-permute-start | bytes 786440 | tf_op jit(solution)/shard_map/ppermute | solution.py:131
  4.7 2.2 %collective-permute-start = (bf16[4,64]{1,0:T(4,128)(2,1)S(1)}, bf16[4,64]{1,0:T(4,128)(2,1)S(1)}, u32[]{:S(2)}, u32[]{:S(2)}) collective-permute-start(bf16[4,64]{1,0:T(4,128)(2,1)S(1)} %get-tuple-element.18), channel_id=1, source_target_pairs={{0,1},{1,0},{2,3},{3,2},{4,5},{5,4},{6,7},{7,6},{8,9},{9,8},{10,11... | collective-permute-start | bytes 1544 | tf_op jit(solution)/shard_map/ppermute | solution.py:131
  5.9 34.3 %collective-permute-start.2 = (bf16[128,1536]{1,0:T(8,128)(2,1)S(1)}, bf16[128,1536]{1,0:T(8,128)(2,1)}, u32[]{:S(2)}, u32[]{:S(2)}) collective-permute-start(bf16[128,1536]{1,0:T(8,128)(2,1)S(1)} %bitcast.168), channel_id=1, source_target_pairs={{0,1},{1,0},{2,3},{3,2},{4,5},{5,4},{6,7},{7,6},{8,9},{9,8},{10,11... | collective-permute-start | bytes 1179656 | tf_op jit(solution)/shard_map/ppermute | solution.py:131
  10.9 0.6 copy-start.3
  14.8 4.2 %copy-start.8 = (s32[8,64]{1,0:T(8,128)}, s32[8,64]{1,0:T(8,128)S(1)}, u32[]{:S(2)}) copy-start(s32[8,64]{1,0:T(8,128)S(1)} %fusion.62) | copy-start | bytes 6148
  14.8 2.4 %copy-start.5 = (pred[2,4,24,64]{3,2,1,0:T(8,128)(4,1)}, pred[2,4,24,64]{3,2,1,0:T(8,128)(4,1)S(1)}, u32[]{:S(2)}) copy-start(pred[2,4,24,64]{3,2,1,0:T(8,128)(4,1)S(1)} %iota_compare_fusion) | copy-start | bytes 36868
  19.0 11.8 %collective-permute-start.6 = (bf16[2,4,64]{2,1,0:T(4,128)(2,1)}, bf16[2,4,64]{2,1,0:T(4,128)(2,1)}, u32[]{:S(2)}, u32[]{:S(2)}) collective-permute-start(bf16[2,4,64]{2,1,0:T(4,128)(2,1)} %pad_maximum_fusion.4), channel_id=1, source_target_pairs={{0,4},{1,5},{2,6},{3,7},{4,0},{5,1},{6,2},{7,3},{8,12},{9,13},{10,... | collective-permute-start | bytes 3080 | tf_op jit(solution)/shard_map/ppermute | solution.py:131
  33.8 13.8 %copy-start.1 = (bf16[1,768,2048]{2,1,0:T(8,128)(2,1)S(1)}, bf16[1,768,2048]{2,1,0:T(8,128)(2,1)}, u32[]{:S(2)}) copy-start(bf16[1,768,2048]{2,1,0:T(8,128)(2,1)} %param.14) | copy-start | bytes 9437188
  33.8 13.8 %copy-start.4 = (bf16[24,2048]{1,0:T(8,128)(2,1)S(1)}, bf16[24,2048]{1,0:T(8,128)(2,1)}, u32[]{:S(2)}) copy-start(bf16[24,2048]{1,0:T(8,128)(2,1)} %get-tuple-element.21) | copy-start | bytes 294916
  36.8 14.0 %collective-permute-start.3 = (bf16[48,2048]{1,0:T(8,128)(2,1)S(1)}, bf16[48,2048]{1,0:T(8,128)(2,1)S(1)}, u32[]{:S(2)}, u32[]{:S(2)}) collective-permute-start(bf16[48,2048]{1,0:T(8,128)(2,1)S(1)} %pad_maximum_fusion.2), channel_id=1, source_target_pairs={{0,2},{1,3},{2,0},{3,1},{4,6},{5,7},{6,4},{7,5},{8,10},{9,11},{10,... | collective-permute-start | bytes 589832 | tf_op jit(solution)/shard_map/ppermute | solution.py:131
  37.3 14.7 %collective-permute-start.8 = (bf16[64,2048]{1,0:T(8,128)(2,1)}, bf16[64,2048]{1,0:T(8,128)(2,1)S(1)}, u32[]{:S(2)}, u32[]{:S(2)}) collective-permute-start(bf16[64,2048]{1,0:T(8,128)(2,1)} %collective-permute-done.7), channel_id=1, source_target_pairs={{0,1},{1,0},{2,3},{3,2},{4,5},{5,4},{6,7},{7,6},{8,9},{9,8},{10,11... | collective-permute-start | bytes 786440 | tf_op jit(solution)/shard_map/ppermute | solution.py:131
  43.5 24.5 %collective-permute-start.12 = (bf16[48,1664]{1,0:T(8,128)(2,1)S(1)}, bf16[48,1664]{1,0:T(8,128)(2,1)S(1)}, u32[]{:S(2)}, u32[]{:S(2)}) collective-permute-start(bf16[48,1664]{1,0:T(8,128)(2,1)S(1)} %bitcast.182), channel_id=1, source_target_pairs={{0,6},{1,7},{2,4},{3,5},{4,2},{5,3},{6,0},{7,1},{8,14},{9,15},{10,... | collective-permute-start | bytes 479240 | tf_op jit(solution)/shard_map/ppermute | solution.py:131
  46.0 16.5 %collective-permute-start.9 = (bf16[48,1664]{1,0:T(8,128)(2,1)S(1)}, bf16[48,1664]{1,0:T(8,128)(2,1)S(1)}, u32[]{:S(2)}, u32[]{:S(2)}) collective-permute-start(bf16[48,1664]{1,0:T(8,128)(2,1)S(1)} %bitcast.183), channel_id=1, source_target_pairs={{0,4},{1,5},{2,6},{3,7},{4,0},{5,1},{6,2},{7,3},{8,12},{9,13},{10,... | collective-permute-start | bytes 479240 | tf_op jit(solution)/shard_map/ppermute | solution.py:131
  47.5 11.7 %collective-permute-start.4 = (bf16[48,1664]{1,0:T(8,128)(2,1)S(1)}, bf16[48,1664]{1,0:T(8,128)(2,1)S(1)}, u32[]{:S(2)}, u32[]{:S(2)}) collective-permute-start(bf16[48,1664]{1,0:T(8,128)(2,1)S(1)} %bitcast.184), channel_id=1, source_target_pairs={{0,2},{1,3},{2,0},{3,1},{4,6},{5,7},{6,4},{7,5},{8,10},{9,11},{10,... | collective-permute-start | bytes 479240 | tf_op jit(solution)/shard_map/ppermute | solution.py:131
  47.6 2.1 %copy-start.2 = (bf16[1,2048,768]{2,1,0:T(8,128)(2,1)S(1)}, bf16[1,2048,768]{2,1,0:T(8,128)(2,1)}, u32[]{:S(2)}) copy-start(bf16[1,2048,768]{2,1,0:T(8,128)(2,1)} %param.12) | copy-start | bytes 9437188
  49.7 1.1 %copy-start.9 = (bf16[192,2048]{1,0:T(8,128)(2,1)S(1)}, bf16[192,2048]{1,0:T(8,128)(2,1)}, u32[]{:S(2)}) copy-start(bf16[192,2048]{1,0:T(8,128)(2,1)} %get-tuple-element.22) | copy-start | bytes 2359300
  52.2 16.0 %collective-permute-start.11 = (bf16[48,2048]{1,0:T(8,128)(2,1)S(1)}, bf16[48,2048]{1,0:T(8,128)(2,1)S(1)}, u32[]{:S(2)}, u32[]{:S(2)}) collective-permute-start(bf16[48,2048]{1,0:T(8,128)(2,1)S(1)} %pad_maximum_fusion.3), channel_id=1, source_target_pairs={{0,2},{1,3},{2,0},{3,1},{4,6},{5,7},{6,4},{7,5},{8,10},{9,11},{10,... | collective-permute-start | bytes 589832 | tf_op jit(solution)/shard_map/ppermute | solution.py:131
  62.5 10.4 %collective-permute-start.5 = (bf16[48,2048]{1,0:T(8,128)(2,1)S(1)}, bf16[48,2048]{1,0:T(8,128)(2,1)S(1)}, u32[]{:S(2)}, u32[]{:S(2)}) collective-permute-start(bf16[48,2048]{1,0:T(8,128)(2,1)S(1)} %fusion.43), channel_id=1, source_target_pairs={{0,2},{1,3},{2,0},{3,1},{4,6},{5,7},{6,4},{7,5},{8,10},{9,11},{10,... | collective-permute-start | bytes 589832 | tf_op jit(solution)/shard_map/ppermute | solution.py:131
  65.8 14.6 %collective-permute-start.10 = (bf16[48,2048]{1,0:T(8,128)(2,1)S(1)}, bf16[48,2048]{1,0:T(8,128)(2,1)S(1)}, u32[]{:S(2)}, u32[]{:S(2)}) collective-permute-start(bf16[48,2048]{1,0:T(8,128)(2,1)S(1)} %fusion.40), channel_id=1, source_target_pairs={{0,4},{1,5},{2,6},{3,7},{4,0},{5,1},{6,2},{7,3},{8,12},{9,13},{10,... | collective-permute-start | bytes 589832 | tf_op jit(solution)/shard_map/ppermute | solution.py:131
  70.3 15.6 %copy-start.7 = (pred[1,4,24,64]{3,2,1,0:T(8,128)(4,1)S(1)}, pred[1,4,24,64]{3,2,1,0:T(8,128)(4,1)}, u32[]{:S(2)}) copy-start(pred[1,4,24,64]{3,2,1,0:T(8,128)(4,1)} %get-tuple-element.12) | copy-start | bytes 18436
  71.3 16.4 %copy-start.6 = (pred[1,4,24,64]{3,2,1,0:T(8,128)(4,1)S(1)}, pred[1,4,24,64]{3,2,1,0:T(8,128)(4,1)}, u32[]{:S(2)}) copy-start(pred[1,4,24,64]{3,2,1,0:T(8,128)(4,1)} %get-tuple-element.15) | copy-start | bytes 18436
  71.3 14.3 %collective-permute-start.13 = (bf16[48,2048]{1,0:T(8,128)(2,1)S(1)}, bf16[48,2048]{1,0:T(8,128)(2,1)S(1)}, u32[]{:S(2)}, u32[]{:S(2)}) collective-permute-start(bf16[48,2048]{1,0:T(8,128)(2,1)S(1)} %fusion.37), channel_id=1, source_target_pairs={{0,6},{1,7},{2,4},{3,5},{4,2},{5,3},{6,0},{7,1},{8,14},{9,15},{10,... | collective-permute-start | bytes 589832 | tf_op jit(solution)/shard_map/ppermute | solution.py:131
  86.1 1.6 %collective-permute-start.14 = (bf16[64,2048]{1,0:T(8,128)(2,1)S(1)}, bf16[64,2048]{1,0:T(8,128)(2,1)S(1)}, u32[]{:S(2)}, u32[]{:S(2)}) collective-permute-start(bf16[64,2048]{1,0:T(8,128)(2,1)S(1)} %convolution_convert_fusion.3), channel_id=1, source_target_pairs={{0,1},{1,0},{2,3},{3,2},{4,5},{5,4},{6,7},{7,6},{8,9},{9,8},{10,11... | collective-permute-start | bytes 786440 | tf_op jit(solution)/shard_map/ppermute | solution.py:131
  88.0 9.3 %collective-permute-start.15 = (bf16[1,64,2048]{2,1,0:T(8,128)(2,1)S(1)}, bf16[1,64,2048]{2,1,0:T(8,128)(2,1)S(1)}, u32[]{:S(2)}, u32[]{:S(2)}) collective-permute-start(bf16[1,64,2048]{2,1,0:T(8,128)(2,1)S(1)} %fusion.72), channel_id=1, source_target_pairs={{0,24},{8,0},{16,8},{24,16},{1,25},{9,1},{17,9},{25,17},{2,26},{10... | collective-permute-start | bytes 786440 | tf_op jit(solution)/shard_map/ppermute | solution.py:12

commit v2 on v0

--- a/solution.py
+++ b/solution.py
@@ -1,6 +1,8 @@
 import jax
 import jax.numpy as jnp
 from jax import lax
+from jax.experimental import pallas as pl
+from jax.experimental.pallas import tpu as pltpu
 from jax.sharding import PartitionSpec as P
 
 EXPERTS = 8
@@ -44,7 +46,7 @@
     return (back_rows, weight_term)
 
 
-def on_device(grad_out, pre_act, route_ids, route_gate, w_gate, w_up, w_down):
+def on_device_general(grad_out, pre_act, route_ids, route_gate, w_gate, w_up, w_down):
     member_count = lax.axis_size("expert")
     group_size = member_count // EXPERTS
     token_count = grad_out.shape[1]
@@ -127,6 +129,191 @@
     return (shifted, down_sum.astype(jnp.bfloat16)[None])
 
 
+LAST = (((1,), (1,)), ((), ()))
+FIRST = (((0,), (0,)), ((), ()))
+F32 = jnp.float32
+BF16 = jnp.bfloat16
+GATE_LANES = 128
+
+
+def swapped(value, mask):
+    count = lax.axis_size("expert")
+    return lax.ppermute(value, "expert", [(i, i ^ mask) for i in range(count)])
+
+
+def slot_order(own_meta, pair_meta, experts, cap):
+    lanes = own_meta.shape[1]
+    lane = lax.broadcasted_iota(jnp.int32, (8, lanes), 1)
+    first = lane < lanes // 2
+    packed = jnp.where(first, own_meta[...], pair_meta[...])
+    ids = jnp.right_shift(packed.astype(jnp.int32), 1)
+    gates = packed - 2.0 * ids.astype(F32)
+    row = lax.broadcasted_iota(jnp.int32, (8, lanes), 0)
+    wanted = jnp.bitwise_xor(lax.axis_index("expert"), 2 * row)
+    hit_0 = ids[0:1] == wanted
+    hit_1 = ids[1:2] == wanted
+    named = jnp.where(jnp.logical_or(hit_0, hit_1), 1.0, 0.0)
+    gate = jnp.where(hit_0, gates[0:1], jnp.where(hit_1, gates[1:2], 0.0))
+    before = lax.broadcasted_iota(jnp.int32, (lanes, lanes), 0)
+    after = lax.broadcasted_iota(jnp.int32, (lanes, lanes), 1)
+    half = lanes // 2
+    same = (before < half) == (after < half)
+    upto = jnp.where(jnp.logical_and(before <= after, same), 1.0, 0.0).astype(BF16)
+    counts = jnp.dot(named.astype(BF16), upto, preferred_element_type=F32)
+    slots = jnp.where(named > 0.5, counts.astype(jnp.int32) - 1, -1)
+    slot_no = lax.broadcasted_iota(jnp.int32, (cap, lanes), 0)
+    in_first = lax.broadcasted_iota(jnp.int32, (cap, lanes), 1) < half
+    rows = []
+    for e in range(experts):
+        match = jnp.where(slots[e : e + 1] == slot_no, 1.0, 0.0)
+        rows.append(jnp.where(in_first, match, 0.0))
+        rows.append(jnp.where(in_first, 0.0, match))
+    return rows, jnp.where(hit_0, 1.0, 0.0), jnp.where(hit_1, 1.0, 0.0), gate
+
+
+def near_kernel(
+    own_meta, pair_meta, own_up, pair_up, own_saved, pair_saved,
+    up_0, up_1, pack_0, pack_1, pack_2, pack_3, order_out,
+):
+    cap = up_0.shape[0] // 2
+    wide = own_saved.shape[2]
+    rows, hit_0, hit_1, gate = slot_order(own_meta, pair_meta, 4, cap)
+    order = jnp.concatenate(rows, axis=0)
+    order_bf = order.astype(BF16)
+    order_out[...] = order_bf
+    ups = jnp.concatenate([own_up[...], pair_up[...]], axis=0)
+    picked = jnp.dot(order_bf[: 4 * cap], ups, preferred_element_type=F32)
+    up_0[...] = picked[: 2 * cap].astype(BF16)
+    up_1[...] = picked[2 * cap :].astype(BF16)
+    sel_0 = jnp.concatenate([rows[n] * hit_0[n // 2 : n // 2 + 1] for n in range(8)], axis=0)
+    sel_1 = jnp.concatenate([rows[n] * hit_1[n // 2 : n // 2 + 1] for n in range(8)], axis=0)
+    sel = jnp.concatenate([sel_0.astype(BF16), sel_1.astype(BF16)], axis=1)
+    saved = jnp.concatenate([own_saved[0], pair_saved[0], own_saved[1], pair_saved[1]], axis=0)
+    got = jnp.dot(sel, saved, preferred_element_type=F32)
+    gate_rows = jnp.concatenate(
+        [jnp.sum(rows[n] * gate[n // 2 : n // 2 + 1], axis=1, keepdims=True) for n in range(8)],
+        axis=0,
+    )
+    gate_cols = jnp.broadcast_to(gate_rows, (8 * cap, GATE_LANES))
+    for n, pack in enumerate((pack_0, pack_1, pack_2, pack_3)):
+        part = slice(2 * cap * n, 2 * cap * (n + 1))
+        pack[:, :wide] = got[part].astype(BF16)
+        pack[:, wide:] = gate_cols[part].astype(BF16)
+
+
+def far_kernel(own_meta, pair_meta, own_up, pair_up, up_2, up_3):
+    cap = up_2.shape[0] // 2
+    rows = slot_order(own_meta, pair_meta, 2, cap)[0]
+    order = jnp.concatenate(rows, axis=0).astype(BF16)
+    ups = jnp.concatenate([own_up[...], pair_up[...]], axis=0)
+    picked = jnp.dot(order, ups, preferred_element_type=F32)
+    up_2[...] = picked[: 2 * cap].astype(BF16)
+    up_3[...] = picked[2 * cap :].astype(BF16)
+
+
+def local_call(kernel, outs, args, flops):
+    moved = sum(a.size * a.dtype.itemsize for a in args)
+    moved += sum(o.size * o.dtype.itemsize for o in outs)
+    whole = pl.BlockSpec(memory_space=pltpu.VMEM)
+    return pl.pallas_call(
+        kernel,
+        out_shape=outs,
+        in_specs=[whole] * len(args),
+        out_specs=[whole] * len(outs),
+        compiler_params=pltpu.CompilerParams(vmem_limit_bytes=24 * 1024 * 1024),
+        cost_estimate=pl.CostEstimate(flops=flops, bytes_accessed=moved, transcendentals=0),
+    )(*args)
+
+
+def hidden_grads(grad_hidden, saved, gate):
+    units = grad_hidden.shape[1]
+    saved_f = saved.astype(F32)
+    gate_pre = saved_f[:, :units]
+    up_pre = saved_f[:, units:]
+    sig = jax.nn.sigmoid(gate_pre)
+    silu = gate_pre * sig
+    grad_h = grad_hidden * gate
+    grad_a = (grad_h * up_pre * sig * (1.0 + gate_pre * (1.0 - sig))).astype(BF16)
+    grad_b = (grad_h * silu).astype(BF16)
+    scaled = (gate * silu * up_pre).astype(BF16)
+    return grad_a, grad_b, scaled
+
+
+def on_device_pairs(grad_out, pre_act, route_ids, route_gate, w_gate, w_up, w_down):
+    tokens, width = grad_out.shape[1:]
+    units = w_down.shape[1]
+    wide = 2 * units
+    cap = 3 * tokens // 8
+    upstream = grad_out[0]
+
+    meta = (2 * route_ids[0]).astype(F32) + route_gate[0].astype(F32)
+    meta = jnp.concatenate([meta.T, meta.T], axis=1)
+    meta = jnp.pad(meta, ((0, 8 - meta.shape[0]), (0, 0)))
+    saved_all = pre_act[0].transpose(1, 0, 2, 3).reshape(-1, tokens, wide)
+
+    far_up = swapped(upstream, 4)
+    far_meta = swapped(meta, 4)
+    pair_up = swapped(upstream, 1)
+    pair_meta = swapped(meta, 1)
+    pair_saved = swapped(saved_all, 1)
+    far_pair_up = swapped(far_up, 1)
+    far_pair_meta = swapped(far_meta, 1)
+
+    up_shape = jax.ShapeDtypeStruct((2 * cap, width), BF16)
+    pack_shape = jax.ShapeDtypeStruct((2 * cap, wide + GATE_LANES), BF16)
+    order_shape = jax.ShapeDtypeStruct((8 * cap, 2 * tokens), BF16)
+    own_rows, near_rows, pack_0, pack_1, pack_2, pack_3, order = local_call(
+        near_kernel,
+        [up_shape] * 2 + [pack_shape] * 4 + [order_shape],
+        (meta, pair_meta, upstream, pair_up, saved_all, pair_saved),
+        2 * 8 * cap * 4 * tokens * (width + wide),
+    )
+    near_rows = swapped(near_rows, 2)
+    pack_2 = swapped(pack_2, 4)
+    pack_3 = swapped(pack_3, 6)
+    pack_1 = swapped(pack_1, 2)
+    two_rows, three_rows = local_call(
+        far_kernel,
+        [up_shape] * 2,
+        (far_meta, far_pair_meta, far_up, far_pair_up),
+        2 * 4 * cap * 2 * tokens * width,
+    )
+    three_rows = swapped(three_rows, 2)
+
+    def backward(up, pack):
+        saved = pack[:, :wide]
+        gate = pack[:, wide : wide + 1].astype(F32)
+        grad_hidden = lax.dot_general(up, w_down[0], LAST, preferred_element_type=F32)
+        grad_a, grad_b, scaled = hidden_grads(grad_hidden, saved, gate)
+        back = lax.dot_general(grad_a, w_gate[0], LAST, preferred_element_type=F32)
+        back = back + lax.dot_general(grad_b, w_up[0], LAST, preferred_element_type=F32)
+        return back.astype(BF16), scaled
+
+    close_up = jnp.concatenate([own_rows, near_rows], axis=0)
+    back_close, scaled_close = backward(close_up, jnp.concatenate([pack_0, pack_1], axis=0))
+    back_2, scaled_2 = backward(two_rows, pack_2)
+    back_3, scaled_3 = backward(three_rows, pack_3)
+    home_2 = swapped(back_2, 4)
+    home_3 = swapped(back_3, 6)
+    home_1 = swapped(back_close[2 * cap :], 2)
+
+    scaled = jnp.concatenate([scaled_close, scaled_2, scaled_3], axis=0)
+    ups = jnp.concatenate([close_up, two_rows, three_rows], axis=0)
+    down = lax.dot_general(scaled, ups, FIRST, preferred_element_type=F32).astype(BF16)
+
+    home = jnp.concatenate([back_close[: 2 * cap], home_1, home_2, home_3], axis=0)
+    sums = lax.dot_general(order, home, FIRST, preferred_element_type=F32)
+    other = swapped(sums[tokens:].astype(BF16), 1)
+    total = (sums[:tokens] + other.astype(F32)).astype(BF16)
+    return shifted_2(total[None], "section", -1), down[None]
+
+
+def on_device(*args):
+    if lax.axis_size("expert") == EXPERTS:
+        return on_device_pairs(*args)
+    return on_device_general(*args)
+
+
 def solution(mesh):
     placed = (
         P("section", "expert", None),

time: 101 us -> 69.5 us (0.69)
  blocking collectives: 23.4 us -> 0 us
  waiting for transfers between devices: 38.3 us -> 31.1 us
  other arithmetic: 4.69 us -> 1.53 us
  starting transfers between devices: 17.2 us -> 19 us
    all_to_all x3 -> x0, waiting for transfers between devices: 37 us -> none  [the longest x1 18.7 us: on_device(): lax.all_to_all(upstream_buf, 'expert', split_axis=1, concat_axis=1, tiled...]
    ppermute x0 -> x16, waiting for transfers between devices: none -> 28 us  [swapped(): return lax.ppermute(value, 'expert', [(i, i ^ mask) for i in range(count)])]
    all_to_all x1 -> x0, blocking collectives: 23.4 us -> none  [on_device(): lax.all_to_all(back_buf, 'expert', split_axis=1, concat_axis=1, tiled=True)]
    ppermute x0 -> x16, starting transfers between devices: none -> 16.5 us  [swapped(): return lax.ppermute(value, 'expert', [(i, i ^ mask) for i in range(count)])]
    all_to_all x3 -> x0, starting transfers between devices: 14.7 us -> none  [the longest x1 6.33 us: on_device(): lax.all_to_all(gate_buf, 'expert', split_axis=1, concat_axis=1, tiled=True)]
    convert_element_type x5 -> x6, other arithmetic: 3.05 us -> 0.38 us  [the longest x3 0.29 us: hidden_grads(): scaled = (gate * silu * up_pre).astype(BF16)]
    ppermute x1, waiting for transfers between devices: 1.3 us -> 3.1 us  [shifted_2(): return lax.ppermute(value, axis, pairs)]
    reshape x0 -> x2, local copies, waits for them, and re-layouts: none -> 1.44 us  [on_device_pairs(): saved_all = pre_act[0].transpose(1, 0, 2, 3).reshape(-1, tokens, wide)]
  transfers between devices with their start and end apart: 4 -> 17, of which waited for: 4 -> 7; matrix products, arithmetic and copies ran while one was open for 10% -> 20% of each run, Pallas kernels for 0% -> 1%
where the time goes in v2:
time: 69.5 us; the launch traced here: 69.3 us
  waiting for transfers between devices  31.1 us (45%)
  starting transfers between devices  19 us (27%)
  matrix products  12.5 us (18%)
  local copies, waits for them, and re-layouts  3.2 us (5%)
  other arithmetic  1.53 us (2%)
  Pallas kernels  0.97 us (1%)
  between operations  0.9 us (1%)
    ppermute x16, waiting for transfers between devices, swapped(): return lax.ppermute(value, 'expert', [(i, i ^ mask) for i in range(count)])  28 us
    ppermute x16, starting transfers between devices, swapped(): return lax.ppermute(value, 'expert', [(i, i ^ mask) for i in range(count)])  16.5 us
    dot_general x3, matrix products, backward(): lax.dot_general(up, w_down[0], LAST, preferred_element_type=F32)  3.23 us
    dot_general x3, matrix products, backward(): back = lax.dot_general(grad_a, w_gate[0], LAST, preferred_element_type=F32)  3.16 us
    dot_general x3, matrix products, backward(): lax.dot_general(grad_b, w_up[0], LAST, preferred_element_type=F32)  3.12 us
    ppermute x1, waiting for transfers between devices, shifted_2(): return lax.ppermute(value, axis, pairs)  3.1 us
    dot_general x1, matrix products, on_device_pairs(): lax.dot_general(scaled, ups, FIRST, preferred_element_type=F32).astype(BF16)  2.69 us
    ppermute x1, starting transfers between devices, shifted_2(): return lax.ppermute(value, axis, pairs)  2.52 us
  transfers between devices with their start and end apart: 17, of which 7 were waited for; matrix products, arithmetic and copies ran while one was open for 20% of the time, Pallas kernels for 1%

profile of v2, /device:TPU:0, one launch (start us, length us, event | category | flops | bytes accessed | tf_op | source)
XLA Modules:
  0.0 69.3 jit_solution(12390960402984745969)
XLA Ops:
  0.6 0.0 copy-start
  0.6 1.4 %reshape.16 = bf16[2,64,1536]{2,0,1:T(2,128)(2,1)S(1)} reshape(bf16[2,64,2,768]{3,2,0,1:T(2,128)(2,1)} %bitcast.59) | data formatting | bytes 786432 | tf_op jit(solution)/shard_map/reshape | solution.py:252
  2.1 0.5 collective-permute-start.2
  2.6 3.7 %collective-permute-start.8 = (bf16[64,2048]{1,0:T(8,128)(2,1)}, bf16[64,2048]{1,0:T(8,128)(2,1)S(1)}, u32[]{:S(2)}, u32[]{:S(2)}) collective-permute-start(bf16[64,2048]{1,0:T(8,128)(2,1)} %bitcast.56), channel_id=1, source_target_pairs={{0,4},{1,5},{2,6},{3,7},{4,0},{5,1},{6,2},{7,3},{8,12},{9,13},{10,... | collective-permute-start | bytes 786440 | tf_op jit(solution)/shard_map/ppermute | solution.py:141
  6.3 0.2 collective-permute-start.1
  6.4 0.7 %add_bitcast_fusion = f32[2,64]{1,0:T(2,128)S(1)} fusion(bf16[1,64,2]{1,2,0:T(2,128)(2,1)} %param.10, s32[1,64,2]{1,2,0:T(2,128)} %param.9), kind=kLoop, calls=%fused_computation.84 | loop fusion | flops 512 | bytes 1280 | tf_op jit(solution)/shard_map/transpose | solution.py:250
  7.1 0.1 select_maximum_fusion.own_meta
  7.2 0.3 collective-permute-start.6
  7.5 0.2 collective-permute-start
  7.6 11.5 %collective-permute-done.6.own_meta = f32[8,128]{1,0:T(8,128)S(1)} collective-permute-done((f32[8,128]{1,0:T(8,128)S(1)}, f32[8,128]{1,0:T(8,128)S(1)}, u32[]{:S(2)}, u32[]{:S(2)}) %collective-permute-start.6) | collective-permute-done | bytes 4128 | tf_op jit(solution)/shard_map/ppermute | solution.py:141
  19.2 0.5 collective-permute-start.9
  19.7 0.9 %copy-done.1 = bf16[1,64,2048]{2,1,0:T(8,128)(2,1)S(1)} copy-done((bf16[1,64,2048]{2,1,0:T(8,128)(2,1)S(1)}, bf16[1,64,2048]{2,1,0:T(8,128)(2,1)}, u32[]{:S(2)}) %copy-start.1) | copy-done | bytes 262168
  20.7 0.6 shard_map.86
  21.2 0.9 %collective-permute-start.4 = (bf16[48,1664]{1,0:T(8,128)(2,1)S(1)}, bf16[48,1664]{1,0:T(8,128)(2,1)S(1)}, u32[]{:S(2)}, u32[]{:S(2)}) collective-permute-start(bf16[48,1664]{1,0:T(8,128)(2,1)S(1)} %get-tuple-element.15), channel_id=1, source_target_pairs={{0,2},{1,3},{2,0},{3,1},{4,6},{5,7},{6,4},{7,5},{8,10},{9,11},{10,... | collective-permute-start | bytes 479240 | tf_op jit(solution)/shard_map/ppermute | solution.py:141
  22.1 3.3 %collective-permute-start.10 = (bf16[48,1664]{1,0:T(8,128)(2,1)S(1)}, bf16[48,1664]{1,0:T(8,128)(2,1)S(1)}, u32[]{:S(2)}, u32[]{:S(2)}) collective-permute-start(bf16[48,1664]{1,0:T(8,128)(2,1)S(1)} %get-tuple-element.17), channel_id=1, source_target_pairs={{0,4},{1,5},{2,6},{3,7},{4,0},{5,1},{6,2},{7,3},{8,12},{9,13},{10,... | collective-permute-start | bytes 479240 | tf_op jit(solution)/shard_map/ppermute | solution.py:141
  25.4 0.3 collective-permute-start.13
  25.7 0.4 collective-permute-start.3
  26.1 0.4 shard_map.87
  26.5 1.8 %collective-permute-start.12 = (bf16[48,2048]{1,0:T(8,128)(2,1)S(1)}, bf16[48,2048]{1,0:T(8,128)(2,1)S(1)}, u32[]{:S(2)}, u32[]{:S(2)}) collective-permute-start(bf16[48,2048]{1,0:T(8,128)(2,1)S(1)} %get-tuple-element.18), channel_id=1, source_target_pairs={{0,2},{1,3},{2,0},{3,1},{4,6},{5,7},{6,4},{7,5},{8,10},{9,11},{10,... | collective-permute-start | bytes 589832 | tf_op jit(solution)/shard_map/ppermute | solution.py:141
  28.3 2.9 %collective-permute-done.4 = bf16[48,1664]{1,0:T(8,128)(2,1)S(1)} collective-permute-done((bf16[48,1664]{1,0:T(8,128)(2,1)S(1)}, bf16[48,1664]{1,0:T(8,128)(2,1)S(1)}, u32[]{:S(2)}, u32[]{:S(2)}) %collective-permute-start.4) | collective-permute-done | bytes 159776 | tf_op jit(solution)/shard_map/ppermute | solution.py:141
  31.2 6.1 %collective-permute-done.10 = bf16[48,1664]{1,0:T(8,128)(2,1)S(1)} collective-permute-done((bf16[48,1664]{1,0:T(8,128)(2,1)S(1)}, bf16[48,1664]{1,0:T(8,128)(2,1)S(1)}, u32[]{:S(2)}, u32[]{:S(2)}) %collective-permute-start.10) | collective-permute-done | bytes 159776 | tf_op jit(solution)/shard_map/ppermute | solution.py:141
  37.3 0.1 convert_reduce_fusion.2
  37.4 1.1 %fusion.40 = f32[48,768]{1,0:T(8,128)S(1)} fusion(bf16[48,2048]{1,0:T(8,128)(2,1)S(1)} %get-tuple-element.16, bf16[1,768,2048]{2,1,0:T(8,128)(2,1)S(1)} %copy-done.2, f32[48]{0:T(128)S(1)} %convert_reduce_fusion.2), kind=kOutput, calls=%fused_computation.27 | convolution fusion | flops 151031808 | bytes 3489984 | tf_op jit(solution)/shard_map/dot_general | solution.py:286
  38.6 1.0 %fusion.2 = f32[48,2048]{1,0:T(8,128)S(1)} fusion(bf16[1,2048,768]{2,1,0:T(8,128)(2,1)S(1)} %copy-done, f32[48,768]{1,0:T(8,128)S(1)} %fusion.40, f32[48,1536]{1,0:T(8,128)S(1)} %slice_convert_fusion.3), kind=kOutput, calls=%fused_computation.3 | convolution fusion | flops 151216128 | bytes 3833856 | tf_op jit(solution)/shard_map/dot_general | solution.py:289
  39.6 1.0 %fusion.34 = bf16[48,2048]{1,0:T(8,128)(2,1)S(1)} fusion(f32[48,2048]{1,0:T(8,128)S(1)} %fusion.2, bf16[1,2048,768]{2,1,0:T(8,128)(2,1)S(1)} %copy-done.3, f32[48,768]{1,0:T(8,128)S(1)} %fusion.40, f32[48,1536]{1,0:T(8,128)S(1)} %slice_convert_fusion.3), kind=kOutput, calls=%fused_computation.25 | convolution fusion | flops 151560192 | bytes 4177920 | tf_op jit(solution)/shard_map/dot_general | solution.py:288
  40.6 0.1 collective-permute-start.11
  40.8 0.1 convert_reduce_fusion.1
  40.9 0.1 convert_reduce_fusion
  41.0 1.1 %fusion.37 = f32[96,768]{1,0:T(8,128)S(1)} fusion(bf16[1,768,2048]{2,1,0:T(8,128)(2,1)S(1)} %copy-done.2, bf16[48,2048]{1,0:T(8,128)(2,1)S(1)} %collective-permute-done.3, bf16[48,2048]{1,0:T(8,128)(2,1)S(1)} %get-tuple-element.12, f32[96]{0:T(128)S(1)} %convert_reduce_fusion), kind=kOutput, calls=%fused_computation.26 | convolution fusion | flops 302850048 | bytes 3834240 | tf_op jit(solution)/shard_map/dot_general | solution.py:286
  42.1 1.1 %fusion.4 = f32[96,2048]{1,0:T(8,128)S(1)} fusion(bf16[1,2048,768]{2,1,0:T(8,128)(2,1)S(1)} %copy-done, f32[96,768]{1,0:T(8,128)S(1)} %fusion.37, f32[96,1536]{1,0:T(8,128)S(1)} %slice_convert_fusion.1), kind=kOutput, calls=%fused_computation.5 | convolution fusion | flops 302432256 | bytes 4521984 | tf_op jit(solution)/shard_map/dot_general | solution.py:289
  43.2 1.1 %fusion.22 = bf16[96,2048]{1,0:T(8,128)(2,1)S(1)} fusion(f32[96,2048]{1,0:T(8,128)S(1)} %fusion.4, bf16[1,2048,768]{2,1,0:T(8,128)(2,1)S(1)} %copy-done.3, f32[96,768]{1,0:T(8,128)S(1)} %fusion.37, f32[96,1536]{1,0:T(8,128)S(1)} %slice_convert_fusion.1), kind=kOutput, calls=%fused_computation.21 | convolution fusion | flops 303120384 | bytes 5210112 | tf_op jit(solution)/shard_map/dot_general | solution.py:288
  44.3 3.0 %collective-permute-start.5 = (bf16[48,2048]{1,0:T(8,128)(2,1)S(1)}, bf16[48,2048]{1,0:T(8,128)(2,1)S(1)}, u32[]{:S(2)}, u32[]{:S(2)}) collective-permute-start(bf16[48,2048]{1,0:T(8,128)(2,1)S(1)} %get-tuple-element.21), channel_id=1, source_target_pairs={{0,2},{1,3},{2,0},{3,1},{4,6},{5,7},{6,4},{7,5},{8,10},{9,11},{10,... | collective-permute-start | bytes 589832 | tf_op jit(solution)/shard_map/ppermute | solution.py:141
  47.4 1.1 %fusion.43 = f32[48,768]{1,0:T(8,128)S(1)} fusion(bf16[48,2048]{1,0:T(8,128)(2,1)S(1)} %collective-permute-done.12, bf16[1,768,2048]{2,1,0:T(8,128)(2,1)S(1)} %copy-done.2, f32[48]{0:T(128)S(1)} %convert_reduce_fusion.1), kind=kOutput, calls=%fused_computation.28 | convolution fusion | flops 151031808 | bytes 3489984 | tf_op jit(solution)/shard_map/dot_general | solution.py:286
  48.4 1.0 %fusion = f32[48,2048]{1,0:T(8,128)S(1)} fusion(bf16[1,2048,768]{2,1,0:T(8,128)(2,1)S(1)} %copy-done, f32[48,768]{1,0:T(8,128)S(1)} %fusion.43, f32[48,1536]{1,0:T(8,128)S(1)} %slice_convert_fusion.2), kind=kOutput, calls=%fused_computation.1 | convolution fusion | flops 151216128 | bytes 3833856 | tf_op jit(solution)/shard_map/dot_general | solution.py:289
  49.5 1.0 %fusion.31 = bf16[48,2048]{1,0:T(8,128)(2,1)S(1)} fusion(f32[48,2048]{1,0:T(8,128)S(1)} %fusion, bf16[1,2048,768]{2,1,0:T(8,128)(2,1)S(1)} %copy-done.3, f32[48,768]{1,0:T(8,128)S(1)} %fusion.43, f32[48,1536]{1,0:T(8,128)S(1)} %slice_convert_fusion.2), kind=kOutput, calls=%fused_computation.24 | convolution fusion | flops 151560192 | bytes 4177920 | tf_op jit(solution)/shard_map/dot_general | solution.py:288
  50.5 1.4 %collective-permute-start.14 = (bf16[48,2048]{1,0:T(8,128)(2,1)S(1)}, bf16[48,2048]{1,0:T(8,128)(2,1)S(1)}, u32[]{:S(2)}, u32[]{:S(2)}) collective-permute-start(bf16[48,2048]{1,0:T(8,128)(2,1)S(1)} %fusion.31), channel_id=1, source_target_pairs={{0,6},{1,7},{2,4},{3,5},{4,2},{5,3},{6,0},{7,1},{8,14},{9,15},{10,... | collective-permute-start | bytes 589832 | tf_op jit(solution)/shard_map/ppermute | solution.py:141
  52.0 0.8 %collective-permute-done.5 = bf16[48,2048]{1,0:T(8,128)(2,1)S(1)} collective-permute-done((bf16[48,2048]{1,0:T(8,128)(2,1)S(1)}, bf16[48,2048]{1,0:T(8,128)(2,1)S(1)}, u32[]{:S(2)}, u32[]{:S(2)}) %collective-permute-start.5) | collective-permute-done | bytes 196640 | tf_op jit(solution)/shard_map/ppermute | solution.py:141
  52.8 5.4 %collective-permute-done.14 = bf16[48,2048]{1,0:T(8,128)(2,1)S(1)} collective-permute-done((bf16[48,2048]{1,0:T(8,128)(2,1)S(1)}, bf16[48,2048]{1,0:T(8,128)(2,1)S(1)}, u32[]{:S(2)}, u32[]{:S(2)}) %collective-permute-start.14) | collective-permute-done | bytes 196640 | tf_op jit(solution)/shard_map/ppermute | solution.py:141
  58.2 0.3 fusion.46
  58.5 0.1 collective-permute-start.15
  58.6 0.1 multiply_convert_fusion.6
  58.7 0.1 multiply_convert_fusion
  58.8 1.3 %collective-permute-done.15 = bf16[64,2048]{1,0:T(8,128)(2,1)S(1)} collective-permute-done((bf16[64,2048]{1,0:T(8,128)(2,1)S(1)}, bf16[64,2048]{1,0:T(8,128)(2,1)S(1)}, u32[]{:S(2)}, u32[]{:S(2)}) %collective-permute-start.15) | collective-permute-done | bytes 262176 | tf_op jit(solution)/shard_map/ppermute | solution.py:141
  60.2 2.5 %collective-permute-start.16 = (bf16[1,64,2048]{2,1,0:T(8,128)(2,1)S(1)}, bf16[1,64,2048]{2,1,0:T(8,128)(2,1)S(1)}, u32[]{:S(2)}, u32[]{:S(2)}) collective-permute-start(bf16[1,64,2048]{2,1,0:T(8,128)(2,1)S(1)} %fusion.71), channel_id=1, source_target_pairs={{0,24},{8,0},{16,8},{24,16},{1,25},{9,1},{17,9},{25,17},{2,26},{10... | collective-permute-start | bytes 786440 | tf_op jit(solution)/shard_map/ppermute | solution.py:14
  62.7 0.1 multiply_convert_fusion.5
  62.8 2.7 %fusion.18 = bf16[1,768,2048]{2,1,0:T(8,128)(2,1)} fusion(bf16[48,2048]{1,0:T(8,128)(2,1)S(1)} %collective-permute-done.12, bf16[48,2048]{1,0:T(8,128)(2,1)S(1)} %get-tuple-element.16, bf16[48,2048]{1,0:T(8,128)(2,1)S(1)} %collective-permute-done.3, bf16[48,2048]{1,0:T(8,128)(2,1)S(1)} %get-tuple-element.12, ...), kind=kOutput, calls=%fused_computation.19 | convolution fusion | flops 609583104 | bytes 4227072 | tf_op jit(solution)/shard_map/dot_general | solution.py:302
  65.5 3.1 %collective-permute-done.16 = bf16[1,64,2048]{2,1,0:T(8,128)(2,1)S(1)} collective-permute-done((bf16[1,64,2048]{2,1,0:T(8,128)(2,1)S(1)}, bf16[1,64,2048]{2,1,0:T(8,128)(2,1)S(1)}, u32[]{:S(2)}, u32[]{:S(2)}) %collective-permute-start.16) | collective-permute-done | bytes 262176 | tf_op jit(solution)/shard_map/ppermute | solution.py:14
  68.6 0.7 %copy.14 = bf16[1,64,2048]{2,1,0:T(8,128)(2,1)} copy(bf16[1,64,2048]{2,1,0:T(8,128)(2,1)S(1)} %collective-permute-done.16) | data formatting | bytes 524288
  (26 shorter events, 0.3 us)
Async XLA Ops:
  0.6 37.9 %copy-start = (bf16[1,2048,768]{2,1,0:T(8,128)(2,1)S(1)}, bf16[1,2048,768]{2,1,0:T(8,128)(2,1)}, u32[]{:S(2)}) copy-start(bf16[1,2048,768]{2,1,0:T(8,128)(2,1)} %param.12) | copy-start | bytes 9437188
  2.1 17.6 %collective-permute-start.2 = (bf16[2,64,1536]{2,1,0:T(8,128)(2,1)S(1)}, bf16[2,64,1536]{2,1,0:T(8,128)(2,1)S(1)}, u32[]{:S(2)}, u32[]{:S(2)}) collective-permute-start(bf16[2,64,1536]{2,1,0:T(8,128)(2,1)S(1)} %copy.11.own_saved), channel_id=1, source_target_pairs={{0,1},{1,0},{2,3},{3,2},{4,5},{5,4},{6,7},{7,6},{8,9},{9,8},{10,11... | collective-permute-start | bytes 1179656 | tf_op jit(solution)/shard_map/ppermute | solution.py:141
  2.6 16.6 %collective-permute-start.8 = (bf16[64,2048]{1,0:T(8,128)(2,1)}, bf16[64,2048]{1,0:T(8,128)(2,1)S(1)}, u32[]{:S(2)}, u32[]{:S(2)}) collective-permute-start(bf16[64,2048]{1,0:T(8,128)(2,1)} %bitcast.56), channel_id=1, source_target_pairs={{0,4},{1,5},{2,6},{3,7},{4,0},{5,1},{6,2},{7,3},{8,12},{9,13},{10,... | collective-permute-start | bytes 786440 | tf_op jit(solution)/shard_map/ppermute | solution.py:141
  6.3 13.4 %collective-permute-start.1 = (bf16[64,2048]{1,0:T(8,128)(2,1)}, bf16[64,2048]{1,0:T(8,128)(2,1)S(1)}, u32[]{:S(2)}, u32[]{:S(2)}) collective-permute-start(bf16[64,2048]{1,0:T(8,128)(2,1)} %bitcast.57), channel_id=1, source_target_pairs={{0,1},{1,0},{2,3},{3,2},{4,5},{5,4},{6,7},{7,6},{8,9},{9,8},{10,11... | collective-permute-start | bytes 786440 | tf_op jit(solution)/shard_map/ppermute | solution.py:141
  7.2 12.0 %collective-permute-start.6 = (f32[8,128]{1,0:T(8,128)S(1)}, f32[8,128]{1,0:T(8,128)S(1)}, u32[]{:S(2)}, u32[]{:S(2)}) collective-permute-start(f32[8,128]{1,0:T(8,128)S(1)} %select_maximum_fusion.own_meta), channel_id=1, source_target_pairs={{0,4},{1,5},{2,6},{3,7},{4,0},{5,1},{6,2},{7,3},{8,12},{9,13},{10,... | collective-permute-start | bytes 12296 | tf_op jit(solution)/shard_map/ppermute | solution.py:141
  7.5 12.2 %collective-permute-start = (f32[8,128]{1,0:T(8,128)S(1)}, f32[8,128]{1,0:T(8,128)S(1)}, u32[]{:S(2)}, u32[]{:S(2)}) collective-permute-start(f32[8,128]{1,0:T(8,128)S(1)} %select_maximum_fusion.own_meta), channel_id=1, source_target_pairs={{0,1},{1,0},{2,3},{3,2},{4,5},{5,4},{6,7},{7,6},{8,9},{9,8},{10,11... | collective-permute-start | bytes 12296 | tf_op jit(solution)/shard_map/ppermute | solution.py:141
  19.2 6.5 %collective-permute-start.7 = (f32[8,128]{1,0:T(8,128)S(1)}, f32[8,128]{1,0:T(8,128)S(1)}, u32[]{:S(2)}, u32[]{:S(2)}) collective-permute-start(f32[8,128]{1,0:T(8,128)S(1)} %collective-permute-done.6.own_meta), channel_id=1, source_target_pairs={{0,1},{1,0},{2,3},{3,2},{4,5},{5,4},{6,7},{7,6},{8,9},{9,8},{10,11... | collective-permute-start | bytes 12296 | tf_op jit(solution)/shard_map/ppermute | solution.py:141
  19.2 6.9 %collective-permute-start.9 = (bf16[64,2048]{1,0:T(8,128)(2,1)S(1)}, bf16[64,2048]{1,0:T(8,128)(2,1)S(1)}, u32[]{:S(2)}, u32[]{:S(2)}) collective-permute-start(bf16[64,2048]{1,0:T(8,128)(2,1)S(1)} %collective-permute-done.8.own_up), channel_id=1, source_target_pairs={{0,1},{1,0},{2,3},{3,2},{4,5},{5,4},{6,7},{7,6},{8,9},{9,8},{10,11... | collective-permute-start | bytes 786440 | tf_op jit(solution)/shard_map/ppermute | solution.py:141
  19.7 1.0 %copy-start.1 = (bf16[1,64,2048]{2,1,0:T(8,128)(2,1)S(1)}, bf16[1,64,2048]{2,1,0:T(8,128)(2,1)}, u32[]{:S(2)}) copy-start(bf16[1,64,2048]{2,1,0:T(8,128)(2,1)} %param.7) | copy-start | bytes 786436
  20.7 16.8 %copy-start.2 = (bf16[1,768,2048]{2,1,0:T(8,128)(2,1)S(1)}, bf16[1,768,2048]{2,1,0:T(8,128)(2,1)}, u32[]{:S(2)}) copy-start(bf16[1,768,2048]{2,1,0:T(8,128)(2,1)} %param.13) | copy-start | bytes 9437188
  21.2 9.9 %collective-permute-start.4 = (bf16[48,1664]{1,0:T(8,128)(2,1)S(1)}, bf16[48,1664]{1,0:T(8,128)(2,1)S(1)}, u32[]{:S(2)}, u32[]{:S(2)}) collective-permute-start(bf16[48,1664]{1,0:T(8,128)(2,1)S(1)} %get-tuple-element.15), channel_id=1, source_target_pairs={{0,2},{1,3},{2,0},{3,1},{4,6},{5,7},{6,4},{7,5},{8,10},{9,11},{10,... | collective-permute-start | bytes 479240 | tf_op jit(solution)/shard_map/ppermute | solution.py:141
  22.1 15.2 %collective-permute-start.10 = (bf16[48,1664]{1,0:T(8,128)(2,1)S(1)}, bf16[48,1664]{1,0:T(8,128)(2,1)S(1)}, u32[]{:S(2)}, u32[]{:S(2)}) collective-permute-start(bf16[48,1664]{1,0:T(8,128)(2,1)S(1)} %get-tuple-element.17), channel_id=1, source_target_pairs={{0,4},{1,5},{2,6},{3,7},{4,0},{5,1},{6,2},{7,3},{8,12},{9,13},{10,... | collective-permute-start | bytes 479240 | tf_op jit(solution)/shard_map/ppermute | solution.py:141
  25.4 15.3 %collective-permute-start.13 = (bf16[48,1664]{1,0:T(8,128)(2,1)S(1)}, bf16[48,1664]{1,0:T(8,128)(2,1)S(1)}, u32[]{:S(2)}, u32[]{:S(2)}) collective-permute-start(bf16[48,1664]{1,0:T(8,128)(2,1)S(1)} %get-tuple-element.19), channel_id=1, source_target_pairs={{0,6},{1,7},{2,4},{3,5},{4,2},{5,3},{6,0},{7,1},{8,14},{9,15},{10,... | collective-permute-start | bytes 479240 | tf_op jit(solution)/shard_map/ppermute | solution.py:141
  25.7 15.2 %collective-permute-start.3 = (bf16[48,2048]{1,0:T(8,128)(2,1)S(1)}, bf16[48,2048]{1,0:T(8,128)(2,1)S(1)}, u32[]{:S(2)}, u32[]{:S(2)}) collective-permute-start(bf16[48,2048]{1,0:T(8,128)(2,1)S(1)} %get-tuple-element.13), channel_id=1, source_target_pairs={{0,2},{1,3},{2,0},{3,1},{4,6},{5,7},{6,4},{7,5},{8,10},{9,11},{10,... | collective-permute-start | bytes 589832 | tf_op jit(solution)/shard_map/ppermute | solution.py:141
  26.5 20.9 %collective-permute-start.12 = (bf16[48,2048]{1,0:T(8,128)(2,1)S(1)}, bf16[48,2048]{1,0:T(8,128)(2,1)S(1)}, u32[]{:S(2)}, u32[]{:S(2)}) collective-permute-start(bf16[48,2048]{1,0:T(8,128)(2,1)S(1)} %get-tuple-element.18), channel_id=1, source_target_pairs={{0,2},{1,3},{2,0},{3,1},{4,6},{5,7},{6,4},{7,5},{8,10},{9,11},{10,... | collective-permute-start | bytes 589832 | tf_op jit(solution)/shard_map/ppermute | solution.py:141
  37.4 2.2 %copy-start.3 = (bf16[1,2048,768]{2,1,0:T(8,128)(2,1)S(1)}, bf16[1,2048,768]{2,1,0:T(8,128)(2,1)}, u32[]{:S(2)}) copy-start(bf16[1,2048,768]{2,1,0:T(8,128)(2,1)} %param.11) | copy-start | bytes 9437188
  40.6 11.3 %collective-permute-start.11 = (bf16[48,2048]{1,0:T(8,128)(2,1)S(1)}, bf16[48,2048]{1,0:T(8,128)(2,1)S(1)}, u32[]{:S(2)}, u32[]{:S(2)}) collective-permute-start(bf16[48,2048]{1,0:T(8,128)(2,1)S(1)} %fusion.34), channel_id=1, source_target_pairs={{0,4},{1,5},{2,6},{3,7},{4,0},{5,1},{6,2},{7,3},{8,12},{9,13},{10,... | collective-permute-start | bytes 589832 | tf_op jit(solution)/shard_map/ppermute | solution.py:141
  44.3 8.5 %collective-permute-start.5 = (bf16[48,2048]{1,0:T(8,128)(2,1)S(1)}, bf16[48,2048]{1,0:T(8,128)(2,1)S(1)}, u32[]{:S(2)}, u32[]{:S(2)}) collective-permute-start(bf16[48,2048]{1,0:T(8,128)(2,1)S(1)} %get-tuple-element.21), channel_id=1, source_target_pairs={{0,2},{1,3},{2,0},{3,1},{4,6},{5,7},{6,4},{7,5},{8,10},{9,11},{10,... | collective-permute-start | bytes 589832 | tf_op jit(solution)/shard_map/ppermute | solution.py:141
  50.5 7.6 %collective-permute-start.14 = (bf16[48,2048]{1,0:T(8,128)(2,1)S(1)}, bf16[48,2048]{1,0:T(8,128)(2,1)S(1)}, u32[]{:S(2)}, u32[]{:S(2)}) collective-permute-start(bf16[48,2048]{1,0:T(8,128)(2,1)S(1)} %fusion.31), channel_id=1, source_target_pairs={{0,6},{1,7},{2,4},{3,5},{4,2},{5,3},{6,0},{7,1},{8,14},{9,15},{10,... | collective-permute-start | bytes 589832 | tf_op jit(solution)/shard_map/ppermute | solution.py:141
  58.5 1.6 %collective-permute-start.15 = (bf16[64,2048]{1,0:T(8,128)(2,1)S(1)}, bf16[64,2048]{1,0:T(8,128)(2,1)S(1)}, u32[]{:S(2)}, u32[]{:S(2)}) collective-permute-start(bf16[64,2048]{1,0:T(8,128)(2,1)S(1)} %slice.126), channel_id=1, source_target_pairs={{0,1},{1,0},{2,3},{3,2},{4,5},{5,4},{6,7},{7,6},{8,9},{9,8},{10,11... | collective-permute-start | bytes 786440 | tf_op jit(solution)/shard_map/ppermute | solution.py:141
  60.2 8.4 %collective-permute-start.16 = (bf16[1,64,2048]{2,1,0:T(8,128)(2,1)S(1)}, bf16[1,64,2048]{2,1,0:T(8,128)(2,1)S(1)}, u32[]{:S(2)}, u32[]{:S(2)}) collective-permute-start(bf16[1,64,2048]{2,1,0:T(8,128)(2,1)S(1)} %fusion.71), channel_id=1, source_target_pairs={{0,24},{8,0},{16,8},{24,16},{1,25},{9,1},{17,9},{25,17},{2,26},{10... | collective-permute-start | bytes 786440 | tf_op jit(solution)/shard_map/ppermute | solution.py:14

commit v3 on v0

--- a/solution.py
+++ b/solution.py
@@ -1,6 +1,10 @@
+import functools
+
 import jax
 import jax.numpy as jnp
 from jax import lax
+from jax.experimental import pallas as pl
+from jax.experimental.pallas import tpu as pltpu
 from jax.sharding import PartitionSpec as P
 
 EXPERTS = 8
@@ -44,7 +48,7 @@
     return (back_rows, weight_term)
 
 
-def on_device(grad_out, pre_act, route_ids, route_gate, w_gate, w_up, w_down):
+def on_device_general(grad_out, pre_act, route_ids, route_gate, w_gate, w_up, w_down):
     member_count = lax.axis_size("expert")
     group_size = member_count // EXPERTS
     token_count = grad_out.shape[1]
@@ -127,6 +131,334 @@
     return (shifted, down_sum.astype(jnp.bfloat16)[None])
 
 
+LAST = (((1,), (1,)), ((), ()))
+FIRST = (((0,), (0,)), ((), ()))
+F32 = jnp.float32
+BF16 = jnp.bfloat16
+GATE_LANES = 128
+SUM_COST = 8 * 1024 * 1024
+OWN_LIMIT = 44
+
+
+def swapped(value, mask):
+    count = lax.axis_size("expert")
+    return lax.ppermute(value, "expert", [(i, i ^ mask) for i in range(count)])
+
+
+def slot_order(ids, gates, masks, cap):
+    lanes = ids.shape[1]
+    half = lanes // 2
+    row = lax.broadcasted_iota(jnp.int32, (8, lanes), 0)
+    wanted = jnp.full((8, lanes), masks[0], jnp.int32)
+    for n in range(1, len(masks)):
+        wanted = jnp.where(row == n, masks[n], wanted)
+    wanted = jnp.bitwise_xor(lax.axis_index("expert"), wanted)
+    hit_0 = ids[0:1] == wanted
+    hit_1 = ids[1:2] == wanted
+    named = jnp.where(jnp.logical_or(hit_0, hit_1), 1.0, 0.0)
+    gate = jnp.where(hit_0, gates[0:1], jnp.where(hit_1, gates[1:2], 0.0))
+    before = lax.broadcasted_iota(jnp.int32, (lanes, lanes), 0)
+    after = lax.broadcasted_iota(jnp.int32, (lanes, lanes), 1)
+    same = (before < half) == (after < half)
+    upto = jnp.where(jnp.logical_and(before <= after, same), 1.0, 0.0).astype(BF16)
+    counts = jnp.dot(named.astype(BF16), upto, preferred_element_type=F32)
+    slots = jnp.where(named > 0.5, counts.astype(jnp.int32) - 1, -1)
+    slot_no = lax.broadcasted_iota(jnp.int32, (cap, lanes), 0)
+    in_first = lax.broadcasted_iota(jnp.int32, (cap, lanes), 1) < half
+    rows = []
+    for n in range(len(masks)):
+        match = jnp.where(slots[n : n + 1] == slot_no, 1.0, 0.0)
+        rows.append(jnp.where(in_first, match, 0.0))
+        rows.append(jnp.where(in_first, 0.0, match))
+    return rows, jnp.where(hit_0, 1.0, 0.0), jnp.where(hit_1, 1.0, 0.0), gate
+
+
+def gate_columns(rows, gate):
+    found = [
+        jnp.sum(row * gate[n // 2 : n // 2 + 1], axis=1, keepdims=True)
+        for n, row in enumerate(rows)
+    ]
+    found = jnp.concatenate(found, axis=0)
+    return jnp.broadcast_to(found, (found.shape[0], GATE_LANES)).astype(BF16)
+
+
+def near_kernel(
+    own_ids, own_gate, own_up, own_act, pair_ids, pair_gate, pair_up, pair_act,
+    routes, up_0, up_1, saved_0, saved_1, saved_2, saved_3, gate_0, acts,
+):
+    tokens = own_up.shape[0]
+    cap, width = up_0.shape[0] // 2, up_0.shape[1]
+    units = own_act.shape[3]
+    wide = 2 * units
+    ids = jnp.concatenate([own_ids[...], pair_ids[...]], axis=1)
+    gates = jnp.concatenate([own_gate[...].astype(F32), pair_gate[...].astype(F32)], axis=1)
+    picks = ids.shape[0]
+    named = jnp.concatenate([ids.astype(F32), gates], axis=0)
+    rest = jnp.zeros((routes.shape[0] - 2 * picks, routes.shape[1]), F32)
+    named = jnp.concatenate([named, rest], axis=0)
+    routes[...] = named.astype(BF16)
+    saved_2[:, wide:] = named.astype(BF16)
+    rows, hit_0, hit_1, gate = slot_order(ids, gates, (0, 2, 4, 6), cap)
+    order_bf = jnp.concatenate(rows, axis=0).astype(BF16)
+    gates = gate_columns(rows[:4], gate)
+    gate_0[...] = gates[: 2 * cap]
+    up_1[:, width:] = gates[2 * cap :]
+    sel_0 = jnp.concatenate([rows[n] * hit_0[n // 2 : n // 2 + 1] for n in range(8)], axis=0)
+    sel_1 = jnp.concatenate([rows[n] * hit_1[n // 2 : n // 2 + 1] for n in range(8)], axis=0)
+    sel = jnp.concatenate([sel_0.astype(BF16), sel_1.astype(BF16)], axis=1)
+    ups = jnp.concatenate([own_up[...], pair_up[...]], axis=0)
+    picked = jnp.dot(order_bf[: 4 * cap], ups, preferred_element_type=F32)
+    up_0[...] = picked[: 2 * cap].astype(BF16)
+    up_1[:, :width] = picked[2 * cap :].astype(BF16)
+    for block, act in enumerate((own_act, pair_act)):
+        for pick in range(picks):
+            low = (2 * pick + block) * tokens
+            for side in range(2):
+                part = act[:, pick, side, :]
+                acts[low : low + tokens, side * units : (side + 1) * units] = part
+    got = jnp.dot(sel, acts[...], preferred_element_type=F32)
+    for n, out in enumerate((saved_0, saved_1, saved_2, saved_3)):
+        out[:, :wide] = got[2 * cap * n : 2 * cap * (n + 1)].astype(BF16)
+
+
+def read_routes(routes):
+    named = routes.astype(F32)
+    return named[:2].astype(jnp.int32), named[2:4]
+
+
+def far_kernel(saved_2, both_up, up_2, up_3, gate_2):
+    cap, width = up_2.shape[0] // 2, up_2.shape[1]
+    tokens = both_up.shape[0] // 2
+    ids, gates = read_routes(saved_2[:, saved_2.shape[1] - 2 * tokens :])
+    rows, _, _, gate = slot_order(ids, gates, (0, 2), cap)
+    order = jnp.concatenate(rows, axis=0)
+    odd = lax.axis_index("expert") % 2 == 1
+    order = jnp.where(odd, pltpu.roll(order, tokens, 1), order).astype(BF16)
+    picked = jnp.dot(order, both_up[...], preferred_element_type=F32)
+    gates = gate_columns(rows, gate)
+    up_2[...] = picked[: 2 * cap].astype(BF16)
+    up_3[:, :width] = picked[2 * cap :].astype(BF16)
+    up_3[:, width:] = gates[2 * cap :]
+    gate_2[...] = gates[: 2 * cap]
+
+
+def through_expert(up, saved, gate, w_down, w_gate, w_up):
+    grad_hidden = lax.dot_general(up, w_down[...], LAST, preferred_element_type=F32)
+    grad_a, grad_b, scaled = hidden_grads(grad_hidden, saved, gate[:, :1].astype(F32))
+    back = lax.dot_general(grad_a, w_gate[...], LAST, preferred_element_type=F32)
+    back = back + lax.dot_general(grad_b, w_up[...], LAST, preferred_element_type=F32)
+    return back.astype(BF16), scaled
+
+
+def own_kernel(
+    up, saved, gate, w_down, w_gate, w_up,
+    back_out, scaled_out, down_here, gate_here, up_here, arrived,
+):
+    moves = ((w_down, down_here), (w_gate, gate_here), (w_up, up_here))
+    copies = [pltpu.make_async_copy(a, b, arrived.at[n]) for n, (a, b) in enumerate(moves)]
+    for copy in copies:
+        copy.start()
+    copies[0].wait()
+    grad_hidden = lax.dot_general(up[...], down_here[...], LAST, preferred_element_type=F32)
+    grad_a, grad_b, scaled = hidden_grads(grad_hidden, saved[...], gate[:, :1].astype(F32))
+    scaled_out[...] = scaled
+    copies[1].wait()
+    back = lax.dot_general(grad_a, gate_here[...], LAST, preferred_element_type=F32)
+    copies[2].wait()
+    back = back + lax.dot_general(grad_b, up_here[...], LAST, preferred_element_type=F32)
+    back_out[...] = back.astype(BF16)
+
+
+def chunk_kernel(count, *refs):
+    ups, saveds, gates = refs[:count], refs[count : 2 * count], refs[2 * count : 3 * count]
+    w_down, w_gate, w_up = refs[3 * count : 3 * count + 3]
+    backs, scaled_out = refs[3 * count + 3 : -1], refs[-1]
+    width, units = w_gate.shape[0], w_gate.shape[1]
+    each = ups[0].shape[0]
+    up = jnp.concatenate([ref[:, :width] for ref in ups], axis=0)
+    saved = jnp.concatenate([ref[:, : 2 * units] for ref in saveds], axis=0)
+    gate = jnp.concatenate([ref[:, ref.shape[1] - GATE_LANES :] for ref in gates], axis=0)
+    back, scaled_out[...] = through_expert(up, saved, gate, w_down, w_gate, w_up)
+    for n, out in enumerate(backs):
+        out[...] = back[n * each : (n + 1) * each]
+
+
+def down_kernel(scaled_a, scaled_b, scaled_c, up_a, up_b, up_c, up_d, out):
+    scaled = jnp.concatenate([scaled_a[...], scaled_b[...], scaled_c[...]], axis=0)
+    ups = jnp.concatenate([up_a[...], up_b[...], up_c[...], up_d[...]], axis=0)
+    out[...] = lax.dot_general(scaled, ups, FIRST, preferred_element_type=F32).astype(BF16)
+
+
+def sum_kernel(routes, rows_0, rows_1, rows_2, own, other):
+    tokens = own.shape[0]
+    ids, gates = read_routes(routes[...])
+    order = slot_order(ids, gates, (0, 2, 4), rows_0.shape[0] // 2)[0]
+    order = jnp.concatenate(order, axis=0).astype(BF16)
+    rows = jnp.concatenate([rows_0[...], rows_1[...], rows_2[...]], axis=0)
+    back = lax.dot_general(order, rows, FIRST, preferred_element_type=F32)
+    own[...] = back[:tokens]
+    other[...] = back[tokens:].astype(BF16)
+
+
+def last_kernel(routes, own, other, rows_6, rows_7, out):
+    tokens, cap = own.shape[0], rows_6.shape[0] // 2
+    ids, gates = read_routes(routes[...])
+    order = slot_order(ids, gates, (6, 7), cap)[0]
+    order = jnp.concatenate([order[0], order[2]], axis=0).astype(BF16)
+    rows = [rows_6[...].astype(F32)[:cap], rows_7[...].astype(F32)[cap:]]
+    rows = jnp.concatenate(rows, axis=0).astype(BF16)
+    back = lax.dot_general(order, rows, FIRST, preferred_element_type=F32)
+    out[...] = (own[...] + other[...].astype(F32) + back[:tokens]).astype(BF16)
+
+
+def local_call(kernel, outs, args, scratch=(), cost=0, limit=28, **blocks):
+    whole = pl.BlockSpec(memory_space=pltpu.VMEM)
+    if not blocks:
+        blocks["in_specs"] = [whole] * len(args)
+        blocks["out_specs"] = [whole] * len(outs)
+    return pl.pallas_call(
+        kernel,
+        out_shape=outs,
+        scratch_shapes=scratch,
+        compiler_params=pltpu.CompilerParams(vmem_limit_bytes=limit * 1024 * 1024),
+        cost_estimate=pl.CostEstimate(flops=0, bytes_accessed=cost, transcendentals=0),
+        **blocks,
+    )(*args)
+
+
+def hidden_grads(grad_hidden, saved, gate):
+    units = grad_hidden.shape[1]
+    saved_f = saved.astype(F32)
+    gate_pre = saved_f[:, :units]
+    up_pre = saved_f[:, units:]
+    sig = 1.0 / (1.0 + jnp.exp(-gate_pre))
+    silu = gate_pre * sig
+    grad_h = grad_hidden * gate
+    grad_a = (grad_h * up_pre * sig * (1.0 + gate_pre * (1.0 - sig))).astype(BF16)
+    grad_b = (grad_h * silu).astype(BF16)
+    scaled = (gate * silu * up_pre).astype(BF16)
+    return grad_a, grad_b, scaled
+
+
+def after(value, *others):
+    return lax.optimization_barrier((value,) + others)[0]
+
+
+def before_section(value, mask):
+    sections, count = lax.axis_size("section"), lax.axis_size("expert")
+    pairs = [
+        (s * count + e, (s + sections - 1) % sections * count + (e ^ mask))
+        for s in range(sections)
+        for e in range(count)
+    ]
+    return lax.ppermute(value, ("section", "expert"), pairs)
+
+
+def on_device_pairs(grad_out, pre_act, route_ids, route_gate, w_gate, w_up, w_down):
+    tokens, width = grad_out.shape[1:]
+    units = w_down.shape[1]
+    wide = 2 * units
+    cap = 3 * tokens // 8
+    upstream = grad_out[0]
+
+    def shape(rows, lanes):
+        return jax.ShapeDtypeStruct((rows, lanes), BF16)
+
+    up, act = grad_out[0], pre_act[0]
+    ids, gate = route_ids[0].T, route_gate[0].T
+    far_up = swapped(up, 4)
+    routes, own_rows, near_rows, saved_0, saved_1, saved_2, saved_3, gate_0 = local_call(
+        near_kernel,
+        [shape(2 * cap, 2 * tokens)]
+        + [shape(2 * cap, width), shape(2 * cap, width + GATE_LANES)]
+        + [shape(2 * cap, wide + (2 * tokens if n == 2 else 0)) for n in range(4)]
+        + [shape(2 * cap, GATE_LANES)],
+        (ids, gate, up, act, swapped(ids, 1), swapped(gate, 1), swapped(up, 1), swapped(act, 1)),
+        [pltpu.VMEM((4 * tokens, wide), BF16)],
+    )
+    near_rows = swapped(near_rows, 2)
+    saved_2 = swapped(saved_2, 4)
+    saved_1 = swapped(saved_1, 2)
+    vmem, hbm = (pl.BlockSpec(memory_space=space) for space in (pltpu.VMEM, pltpu.HBM))
+    weights = (w_down[0], w_gate[0], w_up[0])
+    back_0, scaled_0, *weights = local_call(
+        own_kernel,
+        [shape(2 * cap, width), shape(2 * cap, units)] + [shape(*w.shape) for w in weights],
+        (own_rows, saved_0, gate_0, *weights),
+        [pltpu.SemaphoreType.DMA((3,))],
+        limit=OWN_LIMIT,
+        in_specs=[vmem] * 3 + [hbm] * 3,
+        out_specs=[vmem] * 5,
+    )
+    next_routes = before_section(routes, 0)
+    far_up = after(far_up, back_0, next_routes)
+    far_both = lax.all_gather(
+        far_up, "expert", axis=0, tiled=True, axis_index_groups=[[i, i + 1] for i in range(0, 8, 2)]
+    )
+    saved_3 = swapped(after(saved_3, far_up), 6)
+    two_rows, three_rows, gate_2 = local_call(
+        far_kernel,
+        [shape(2 * cap, width), shape(2 * cap, width + GATE_LANES), shape(2 * cap, GATE_LANES)],
+        (saved_2, far_both),
+    )
+    three_rows = swapped(three_rows, 2)
+    home_0 = before_section(back_0, 0)
+    saved_1 = after(saved_1, two_rows)
+    back_1, back_2, scaled_12 = local_call(
+        functools.partial(chunk_kernel, 2),
+        [shape(2 * cap, width)] * 2 + [shape(4 * cap, units)],
+        (near_rows, two_rows, saved_1, saved_2, near_rows, gate_2, *weights),
+    )
+    saved_3 = after(saved_3, back_2, home_0)
+    back_3, scaled_3 = local_call(
+        functools.partial(chunk_kernel, 1),
+        [shape(2 * cap, width), shape(2 * cap, units)],
+        (three_rows, saved_3, three_rows, *weights),
+    )
+    home_2 = before_section(back_2, 4)
+    home_1 = before_section(back_1, 2)
+    home_3 = before_section(back_3, 6)
+    parts = 4
+
+    def columns(array):
+        return pl.BlockSpec((array.shape[0], width // parts), lambda n: (0, n))
+
+    def every(array):
+        return pl.BlockSpec(array.shape, lambda n: (0, 0))
+
+    scaled = (scaled_0, scaled_12, scaled_3)
+    ups = (own_rows, near_rows, two_rows, three_rows)
+    (down,) = local_call(
+        down_kernel,
+        [shape(units, width)],
+        scaled + ups,
+        grid=(parts,),
+        in_specs=[every(a) for a in scaled] + [columns(a) for a in ups],
+        out_specs=[pl.BlockSpec((units, width // parts), lambda n: (0, n))],
+    )
+    home_2 = after(home_2, down)
+    summed, other = local_call(
+        sum_kernel,
+        [jax.ShapeDtypeStruct((tokens, width), F32), shape(tokens, width)],
+        (next_routes, home_0, home_1, home_2),
+        cost=SUM_COST,
+    )
+    other = swapped(other, 1)
+    home_3 = after(home_3, summed)
+    (total,) = local_call(
+        last_kernel,
+        [shape(tokens, width)],
+        (next_routes, summed, other, home_3, swapped(home_3, 1)),
+    )
+    return total[None], down[None]
+
+
+def on_device(*args):
+    if lax.axis_size("expert") == EXPERTS:
+        return on_device_pairs(*args)
+    return on_device_general(*args)
+
+
 def solution(mesh):
     placed = (
         P("section", "expert", None),

time: 101 us -> 58.5 us (0.58)
  the two profiles are of different devices: /device:TPU:0 before, /device:TPU:3 now
where the time goes in v3:
time: 58.5 us; the launch traced here: 58.3 us
  starting transfers between devices  27.7 us (47%)
  Pallas kernels  20.5 us (35%)
  blocking collectives  3.77 us (6%)
  local copies, waits for them, and re-layouts  3.27 us (6%)
  waiting for transfers between devices  2.36 us (4%)
  between operations  0.75 us (1%)
    pallas_call x8, Pallas kernels, local_call(): pl.pallas_call(kernel, out_shape=outs, scratch_shapes=scratch, compiler_p...  20.5 us
    ppermute x12, starting transfers between devices, swapped(): return lax.ppermute(value, 'expert', [(i, i ^ mask) for i in range(count)])  13.9 us
    ppermute x5, starting transfers between devices, before_section(): return lax.ppermute(value, ('section', 'expert'), pairs)  13.8 us
    all_gather x1, blocking collectives, on_device_pairs(): lax.all_gather(far_up, 'expert', axis=0, tiled=True, axis_index_groups=[[...  3.77 us
    unnamed x8, local copies, waits for them, and re-layouts  3.27 us
    ppermute x12, waiting for transfers between devices, swapped(): return lax.ppermute(value, 'expert', [(i, i ^ mask) for i in range(count)])  2.35 us
  transfers between devices with their start and end apart: 17, of which 2 were waited for; matrix products, arithmetic and copies ran while one was open for 0% of the time, Pallas kernels for 33%

profile of v3, /device:TPU:3, one launch (start us, length us, event | category | flops | bytes accessed | tf_op | source)
XLA Modules:
  0.0 58.3 jit_solution(3532653289481937123)
XLA Ops:
  0.6 0.7 %collective-permute-start.3 = (bf16[64,2,2,768]{3,2,1,0:T(2,128)(2,1)}, bf16[64,2,2,768]{3,2,1,0:T(2,128)(2,1)S(1)}, u32[]{:S(2)}, u32[]{:S(2)}) collective-permute-start(bf16[64,2,2,768]{3,2,1,0:T(2,128)(2,1)} %bitcast.13), channel_id=1, source_target_pairs={{0,1},{1,0},{2,3},{3,2},{4,5},{5,4},{6,7},{7,6},{8,9},{9,8},{10,11... | collective-permute-start | bytes 1179656 | tf_op jit(solution)/shard_map/ppermute | solution.py:145
  1.4 0.1 collective-permute-start.2
  1.4 2.3 %collective-permute-start.8 = (bf16[64,2048]{1,0:T(8,128)(2,1)}, bf16[64,2048]{1,0:T(8,128)(2,1)S(1)}, u32[]{:S(2)}, u32[]{:S(2)}) collective-permute-start(bf16[64,2048]{1,0:T(8,128)(2,1)} %bitcast.16), channel_id=1, source_target_pairs={{0,4},{1,5},{2,6},{3,7},{4,0},{5,1},{6,2},{7,3},{8,12},{9,13},{10,... | collective-permute-start | bytes 786440 | tf_op jit(solution)/shard_map/ppermute | solution.py:145
  3.8 0.7 %collective-permute-start = (s32[2,64]{1,0:T(2,128)}, s32[2,64]{1,0:T(2,128)S(1)}, u32[]{:S(2)}, u32[]{:S(2)}) collective-permute-start(s32[2,64]{1,0:T(2,128)} %bitcast.18), channel_id=1, source_target_pairs={{0,1},{1,0},{2,3},{3,2},{4,5},{5,4},{6,7},{7,6},{8,9},{9,8},{10,11... | collective-permute-start | bytes 1544 | tf_op jit(solution)/shard_map/ppermute | solution.py:145
  4.5 0.0 collective-permute-start.1
  4.5 1.3 %collective-permute-done.1.pair_gate = bf16[2,64]{1,0:T(2,128)(2,1)S(1)} collective-permute-done((bf16[2,64]{1,0:T(2,128)(2,1)}, bf16[2,64]{1,0:T(2,128)(2,1)S(1)}, u32[]{:S(2)}, u32[]{:S(2)}) %collective-permute-start.1) | collective-permute-done | bytes 288 | tf_op jit(solution)/shard_map/ppermute | solution.py:145
  5.7 0.0 collective-permute-done.pair_ids
  5.7 0.0 collective-permute-done.2.pair_up
  5.7 0.0 collective-permute-done.3.pair_act
  5.7 0.0 copy-start
  5.8 1.0 %copy-done = bf16[1,64,2,2,768]{4,3,2,1,0:T(2,128)(2,1)S(1)} copy-done((bf16[1,64,2,2,768]{4,3,2,1,0:T(2,128)(2,1)S(1)}, bf16[1,64,2,2,768]{4,3,2,1,0:T(2,128)(2,1)}, u32[]{:S(2)}) %copy-start) | copy-done | bytes 393240
  6.7 0.9 %copy-done.1 = bf16[1,64,2048]{2,1,0:T(8,128)(2,1)S(1)} copy-done((bf16[1,64,2048]{2,1,0:T(8,128)(2,1)S(1)}, bf16[1,64,2048]{2,1,0:T(8,128)(2,1)}, u32[]{:S(2)}) %copy-start.1) | copy-done | bytes 262168
  7.7 0.7 %copy-done.2 = s32[1,64,2]{1,2,0:T(2,128)S(1)} copy-done((s32[1,64,2]{1,2,0:T(2,128)S(1)}, s32[1,64,2]{1,2,0:T(2,128)}, u32[]{:S(2)}) %copy-start.2) | copy-done | bytes 536
  8.4 0.7 %copy-done.3 = bf16[1,64,2]{1,2,0:T(2,128)(2,1)S(1)} copy-done((bf16[1,64,2]{1,2,0:T(2,128)(2,1)S(1)}, bf16[1,64,2]{1,2,0:T(2,128)(2,1)}, u32[]{:S(2)}) %copy-start.3) | copy-done | bytes 280
  9.0 2.3 %shard_map.86 = (bf16[48,128]{1,0:T(8,128)(2,1)S(1)}, bf16[48,2048]{1,0:T(8,128)(2,1)S(1)}, bf16[48,2176]{1,0:T(8,128)(2,1)S(1)}, bf16[48,1536]{1,0:T(8,128)(2,1...) custom-call(s32[2,64]{1,0:T(2,128)S(1)} %bitcast.19, ...), custom_call_target="tpu_custom_call" | custom-call | tf_op jit(solution)/shard_map/pallas_call | solution.py:319
  11.4 0.1 collective-permute-start.7
  11.5 0.3 collective-permute-start.4
  11.7 1.3 %collective-permute-start.9 = (bf16[48,1536]{1,0:T(8,128)(2,1)S(1)}, bf16[48,1536]{1,0:T(8,128)(2,1)S(1)}, u32[]{:S(2)}, u32[]{:S(2)}) collective-permute-start(bf16[48,1536]{1,0:T(8,128)(2,1)S(1)} %get-tuple-element.40), channel_id=1, source_target_pairs={{0,2},{1,3},{2,0},{3,1},{4,6},{5,7},{6,4},{7,5},{8,10},{9,11},{10,... | collective-permute-start | bytes 442376 | tf_op jit(solution)/shard_map/ppermute | solution.py:145
  13.0 0.2 collective-permute-start.6
  13.2 6.1 %shard_map.87 = (bf16[48,2048]{1,0:T(8,128)(2,1)S(1)}, bf16[48,768]{1,0:T(8,128)(2,1)S(1)}, bf16[768,2048]{1,0:T(8,128)(2,1)S(1)}, bf16[2048,768]{1,0:T(8,128)(2,1)S(1)}, bf16[2048,768]{1,0:T(8,128)(2,1)S(1)}) custom-call(bf16[48,2048]{1,0:T(8,128)(2,1)S(1)} %get-tuple-element.32.up.up_a, bf16[48,1536]{1,0:T(8,128)(2,1)S(1)} %get-tuple-element.33.saved, ...), custom_call_target="tpu_custom_call" | custom-call | tf_op jit(solution)/shard_map/pallas_call | solution.py:319
  19.3 0.0 collective-permute-done.8
  19.3 0.0 collective-permute-done.4.routes
  19.3 3.8 %all_gather.3.both_up = bf16[128,2048]{1,0:T(8,128)(2,1)S(1)} all-gather(bf16[64,2048]{1,0:T(8,128)(2,1)S(1)} %collective-permute-done.8), channel_id=1, replica_groups={{0,1},{2,3},{4,5},{6,7},{8,9},{10,11},{12,13},{14,15},{16,17},{18,19},{..., dimensions={0}, use_global_device_ids=true | all-gather | bytes 786432 | tf_op jit(solution)/shard_map/all_gather | solution.py:395
  23.1 0.0 collective-permute-done.7.saved_2.refs_3_
  23.1 0.5 shard_map.88
  23.6 0.7 %collective-permute-start.12 = (bf16[48,2176]{1,0:T(8,128)(2,1)S(1)}, bf16[48,2176]{1,0:T(8,128)(2,1)S(1)}, u32[]{:S(2)}, u32[]{:S(2)}) collective-permute-start(bf16[48,2176]{1,0:T(8,128)(2,1)S(1)} %get-tuple-element.50), channel_id=1, source_target_pairs={{0,2},{1,3},{2,0},{3,1},{4,6},{5,7},{6,4},{7,5},{8,10},{9,11},{10,... | collective-permute-start | bytes 626696 | tf_op jit(solution)/shard_map/ppermute | solution.py:145
  24.3 2.2 %collective-permute-start.5 = (bf16[48,2048]{1,0:T(8,128)(2,1)S(1)}, bf16[48,2048]{1,0:T(8,128)(2,1)S(1)}, u32[]{:S(2)}, u32[]{:S(2)}) collective-permute-start(bf16[48,2048]{1,0:T(8,128)(2,1)S(1)} %get-tuple-element.35), channel_id=1, source_target_pairs={{0,24},{1,25},{2,26},{3,27},{4,28},{5,29},{6,30},{7,31},{8,0},{9,1... | collective-permute-start | bytes 589832 | tf_op jit(solution)/shard_map/ppermute | solution.py:354
  26.5 2.2 %collective-permute-start.13 = (bf16[48,1536]{1,0:T(8,128)(2,1)S(1)}, bf16[48,1536]{1,0:T(8,128)(2,1)S(1)}, u32[]{:S(2)}, u32[]{:S(2)}) collective-permute-start(bf16[48,1536]{1,0:T(8,128)(2,1)S(1)} %get-tuple-element.52), channel_id=1, source_target_pairs={{0,6},{1,7},{2,4},{3,5},{4,2},{5,3},{6,0},{7,1},{8,14},{9,15},{10,... | collective-permute-start | bytes 442376 | tf_op jit(solution)/shard_map/ppermute | solution.py:145
  28.7 0.0 collective-permute-done.9.refs_2_
  28.7 0.0 collective-permute-done.6.refs_0_.refs_4_.up_b
  28.7 3.5 %shard_map.89 = (bf16[48,2048]{1,0:T(8,128)(2,1)S(1)}, bf16[48,2048]{1,0:T(8,128)(2,1)S(1)}, bf16[96,768]{1,0:T(8,128)(2,1)S(1)}) custom-call(bf16[48,2176]{1,0:T(8,128)(2,1)S(1)} %collective-permute-done.6.refs_0_.refs_4_.up_b, bf16[48,2048]{1,0:T(8,128)(2,1)S(1)} %get-tuple-element.39.refs_1_.up_c, bf16[48,1536]{1,0:T(8,128)(2,1)S(1)} %collective-permute-done.9.refs_2_, ...), custom_call_target="tpu_custom_call" | custom-call | tf_op jit(solution)/shard_map/pallas_call | solution.py:319
  32.1 3.5 %collective-permute-start.11 = (bf16[48,2048]{1,0:T(8,128)(2,1)S(1)}, bf16[48,2048]{1,0:T(8,128)(2,1)S(1)}, u32[]{:S(2)}, u32[]{:S(2)}) collective-permute-start(bf16[48,2048]{1,0:T(8,128)(2,1)S(1)} %get-tuple-element.47), channel_id=1, source_target_pairs={{0,28},{1,29},{2,30},{3,31},{4,24},{5,25},{6,26},{7,27},{8,4},{9,5... | collective-permute-start | bytes 589832 | tf_op jit(solution)/shard_map/ppermute | solution.py:354
  35.7 1.2 %collective-permute-start.10 = (bf16[48,2048]{1,0:T(8,128)(2,1)S(1)}, bf16[48,2048]{1,0:T(8,128)(2,1)S(1)}, u32[]{:S(2)}, u32[]{:S(2)}) collective-permute-start(bf16[48,2048]{1,0:T(8,128)(2,1)S(1)} %get-tuple-element.46), channel_id=1, source_target_pairs={{0,26},{1,27},{2,24},{3,25},{4,30},{5,31},{6,28},{7,29},{8,2},{9,3... | collective-permute-start | bytes 589832 | tf_op jit(solution)/shard_map/ppermute | solution.py:354
  36.9 0.0 collective-permute-done.13.refs_1_
  36.9 0.0 collective-permute-done.5.rows_0
  36.9 0.0 collective-permute-done.12.refs_0_.refs_2_.up_d
  36.9 3.3 %shard_map.90 = (bf16[48,2048]{1,0:T(8,128)(2,1)S(1)}, bf16[48,768]{1,0:T(8,128)(2,1)S(1)}) custom-call(bf16[48,2176]{1,0:T(8,128)(2,1)S(1)} %collective-permute-done.12.refs_0_.refs_2_.up_d, bf16[48,1536]{1,0:T(8,128)(2,1)S(1)} %collective-permute-done.13.refs_1_, bf16[48,2176]{1,0:T(8,128)(2,1)S(1)} %collective-permute-done.12.refs_0_.refs_2_.up_d, ...), custom_call_target="tpu_custom_call" | custom-call | tf_op jit(solution)/shard_map/pallas_call | solution.py:319
  40.2 6.6 %collective-permute-start.15 = (bf16[48,2048]{1,0:T(8,128)(2,1)S(1)}, bf16[48,2048]{1,0:T(8,128)(2,1)S(1)}, u32[]{:S(2)}, u32[]{:S(2)}) collective-permute-start(bf16[48,2048]{1,0:T(8,128)(2,1)S(1)} %get-tuple-element.58), channel_id=1, source_target_pairs={{0,30},{1,31},{2,28},{3,29},{4,26},{5,27},{6,24},{7,25},{8,6},{9,7... | collective-permute-start | bytes 589832 | tf_op jit(solution)/shard_map/ppermute | solution.py:354
  46.8 3.2 %shard_map.91 = bf16[768,2048]{1,0:T(8,128)(2,1)} custom-call(bf16[48,768]{1,0:T(8,128)(2,1)S(1)} %get-tuple-element.48.scaled_a, bf16[96,768]{1,0:T(8,128)(2,1)S(1)} %get-tuple-element.49.scaled_b, bf16[48,768]{1,0:T(8,128)(2,1)S(1)} %get-tuple-element.54.scaled_c, bf16[48,2048]{1,0:T(8,128)(2,1)S(1)} %get-tuple-element.32.up.up_a, ...), custom_call_target="tpu_custom_call" | custom-call | tf_op jit(solution)/shard_map/pallas_call | solution.py:319
  50.1 0.0 collective-permute-done.11.rows_2
  50.1 0.0 collective-permute-done.10.rows_1
  50.1 0.5 shard_map.92
  50.6 1.1 %collective-permute-start.14 = (bf16[64,2048]{1,0:T(8,128)(2,1)S(1)}, bf16[64,2048]{1,0:T(8,128)(2,1)S(1)}, u32[]{:S(2)}, u32[]{:S(2)}) collective-permute-start(bf16[64,2048]{1,0:T(8,128)(2,1)S(1)} %get-tuple-element.57), channel_id=1, source_target_pairs={{0,1},{1,0},{2,3},{3,2},{4,5},{5,4},{6,7},{7,6},{8,9},{9,8},{10,11... | collective-permute-start | bytes 786440 | tf_op jit(solution)/shard_map/ppermute | solution.py:145
  51.7 0.0 collective-permute-done.15.rows_6
  51.7 4.4 %collective-permute-start.16 = (bf16[48,2048]{1,0:T(8,128)(2,1)S(1)}, bf16[48,2048]{1,0:T(8,128)(2,1)S(1)}, u32[]{:S(2)}, u32[]{:S(2)}) collective-permute-start(bf16[48,2048]{1,0:T(8,128)(2,1)S(1)} %collective-permute-done.15.rows_6), channel_id=1, source_target_pairs={{0,1},{1,0},{2,3},{3,2},{4,5},{5,4},{6,7},{7,6},{8,9},{9,8},{10,11... | collective-permute-start | bytes 589832 | tf_op jit(solution)/shard_map/ppermute | solution.py:145
  56.1 0.0 collective-permute-done.14.other
  56.1 1.1 %collective-permute-done.16.rows_7 = bf16[48,2048]{1,0:T(8,128)(2,1)S(1)} collective-permute-done((bf16[48,2048]{1,0:T(8,128)(2,1)S(1)}, bf16[48,2048]{1,0:T(8,128)(2,1)S(1)}, u32[]{:S(2)}, u32[]{:S(2)}) %collective-permute-start.16) | collective-permute-done | bytes 196640 | tf_op jit(solution)/shard_map/ppermute | solution.py:145
  57.1 1.2 %shard_map.93 = bf16[64,2048]{1,0:T(8,128)(2,1)} custom-call(bf16[48,128]{1,0:T(8,128)(2,1)S(1)} %collective-permute-done.4.routes, f32[64,2048]{1,0:T(8,128)S(1)} %get-tuple-element.56.own, bf16[64,2048]{1,0:T(8,128)(2,1)S(1)} %collective-permute-done.14.other, bf16[48,2048]{1,0:T(8,128)(2,1)S(1)} %collective-permute-done.15.rows_6, ...), custom_call_target="tpu_custom_call" | custom-call | tf_op jit(solution)/shard_map/pallas_call | solution.py:319
  (3 shorter events, 0.0 us)
Async XLA Ops:
  0.6 5.1 %collective-permute-start.3 = (bf16[64,2,2,768]{3,2,1,0:T(2,128)(2,1)}, bf16[64,2,2,768]{3,2,1,0:T(2,128)(2,1)S(1)}, u32[]{:S(2)}, u32[]{:S(2)}) collective-permute-start(bf16[64,2,2,768]{3,2,1,0:T(2,128)(2,1)} %bitcast.13), channel_id=1, source_target_pairs={{0,1},{1,0},{2,3},{3,2},{4,5},{5,4},{6,7},{7,6},{8,9},{9,8},{10,11... | collective-permute-start | bytes 1179656 | tf_op jit(solution)/shard_map/ppermute | solution.py:145
  1.4 4.4 %collective-permute-start.2 = (bf16[64,2048]{1,0:T(8,128)(2,1)}, bf16[64,2048]{1,0:T(8,128)(2,1)S(1)}, u32[]{:S(2)}, u32[]{:S(2)}) collective-permute-start(bf16[64,2048]{1,0:T(8,128)(2,1)} %bitcast.15), channel_id=1, source_target_pairs={{0,1},{1,0},{2,3},{3,2},{4,5},{5,4},{6,7},{7,6},{8,9},{9,8},{10,11... | collective-permute-start | bytes 786440 | tf_op jit(solution)/shard_map/ppermute | solution.py:145
  1.4 17.9 %collective-permute-start.8 = (bf16[64,2048]{1,0:T(8,128)(2,1)}, bf16[64,2048]{1,0:T(8,128)(2,1)S(1)}, u32[]{:S(2)}, u32[]{:S(2)}) collective-permute-start(bf16[64,2048]{1,0:T(8,128)(2,1)} %bitcast.16), channel_id=1, source_target_pairs={{0,4},{1,5},{2,6},{3,7},{4,0},{5,1},{6,2},{7,3},{8,12},{9,13},{10,... | collective-permute-start | bytes 786440 | tf_op jit(solution)/shard_map/ppermute | solution.py:145
  3.8 2.0 %collective-permute-start = (s32[2,64]{1,0:T(2,128)}, s32[2,64]{1,0:T(2,128)S(1)}, u32[]{:S(2)}, u32[]{:S(2)}) collective-permute-start(s32[2,64]{1,0:T(2,128)} %bitcast.18), channel_id=1, source_target_pairs={{0,1},{1,0},{2,3},{3,2},{4,5},{5,4},{6,7},{7,6},{8,9},{9,8},{10,11... | collective-permute-start | bytes 1544 | tf_op jit(solution)/shard_map/ppermute | solution.py:145
  4.5 1.3 %collective-permute-start.1 = (bf16[2,64]{1,0:T(2,128)(2,1)}, bf16[2,64]{1,0:T(2,128)(2,1)S(1)}, u32[]{:S(2)}, u32[]{:S(2)}) collective-permute-start(bf16[2,64]{1,0:T(2,128)(2,1)} %bitcast.20), channel_id=1, source_target_pairs={{0,1},{1,0},{2,3},{3,2},{4,5},{5,4},{6,7},{7,6},{8,9},{9,8},{10,11... | collective-permute-start | bytes 776 | tf_op jit(solution)/shard_map/ppermute | solution.py:145
  5.7 1.0 %copy-start = (bf16[1,64,2,2,768]{4,3,2,1,0:T(2,128)(2,1)S(1)}, bf16[1,64,2,2,768]{4,3,2,1,0:T(2,128)(2,1)}, u32[]{:S(2)}) copy-start(bf16[1,64,2,2,768]{4,3,2,1,0:T(2,128)(2,1)} %param.8) | copy-start | bytes 1179652
  6.7 0.9 %copy-start.1 = (bf16[1,64,2048]{2,1,0:T(8,128)(2,1)S(1)}, bf16[1,64,2048]{2,1,0:T(8,128)(2,1)}, u32[]{:S(2)}) copy-start(bf16[1,64,2048]{2,1,0:T(8,128)(2,1)} %param.7) | copy-start | bytes 786436
  7.7 0.7 %copy-start.2 = (s32[1,64,2]{1,2,0:T(2,128)S(1)}, s32[1,64,2]{1,2,0:T(2,128)}, u32[]{:S(2)}) copy-start(s32[1,64,2]{1,2,0:T(2,128)} %param.9) | copy-start | bytes 1540
  8.4 0.7 %copy-start.3 = (bf16[1,64,2]{1,2,0:T(2,128)(2,1)S(1)}, bf16[1,64,2]{1,2,0:T(2,128)(2,1)}, u32[]{:S(2)}) copy-start(bf16[1,64,2]{1,2,0:T(2,128)(2,1)} %param.10) | copy-start | bytes 772
  11.4 11.8 %collective-permute-start.7 = (bf16[48,1664]{1,0:T(8,128)(2,1)S(1)}, bf16[48,1664]{1,0:T(8,128)(2,1)S(1)}, u32[]{:S(2)}, u32[]{:S(2)}) collective-permute-start(bf16[48,1664]{1,0:T(8,128)(2,1)S(1)} %get-tuple-element.37), channel_id=1, source_target_pairs={{0,4},{1,5},{2,6},{3,7},{4,0},{5,1},{6,2},{7,3},{8,12},{9,13},{10,... | collective-permute-start | bytes 479240 | tf_op jit(solution)/shard_map/ppermute | solution.py:145
  11.5 7.9 %collective-permute-start.4 = (bf16[48,128]{1,0:T(8,128)(2,1)S(1)}, bf16[48,128]{1,0:T(8,128)(2,1)S(1)}, u32[]{:S(2)}, u32[]{:S(2)}) collective-permute-start(bf16[48,128]{1,0:T(8,128)(2,1)S(1)} %get-tuple-element.31), channel_id=1, source_target_pairs={{0,24},{1,25},{2,26},{3,27},{4,28},{5,29},{6,30},{7,31},{8,0},{9,1... | collective-permute-start | bytes 36872 | tf_op jit(solution)/shard_map/ppermute | solution.py:354
  11.7 16.9 %collective-permute-start.9 = (bf16[48,1536]{1,0:T(8,128)(2,1)S(1)}, bf16[48,1536]{1,0:T(8,128)(2,1)S(1)}, u32[]{:S(2)}, u32[]{:S(2)}) collective-permute-start(bf16[48,1536]{1,0:T(8,128)(2,1)S(1)} %get-tuple-element.40), channel_id=1, source_target_pairs={{0,2},{1,3},{2,0},{3,1},{4,6},{5,7},{6,4},{7,5},{8,10},{9,11},{10,... | collective-permute-start | bytes 442376 | tf_op jit(solution)/shard_map/ppermute | solution.py:145
  13.0 15.6 %collective-permute-start.6 = (bf16[48,2176]{1,0:T(8,128)(2,1)S(1)}, bf16[48,2176]{1,0:T(8,128)(2,1)S(1)}, u32[]{:S(2)}, u32[]{:S(2)}) collective-permute-start(bf16[48,2176]{1,0:T(8,128)(2,1)S(1)} %get-tuple-element.36), channel_id=1, source_target_pairs={{0,2},{1,3},{2,0},{3,1},{4,6},{5,7},{6,4},{7,5},{8,10},{9,11},{10,... | collective-permute-start | bytes 626696 | tf_op jit(solution)/shard_map/ppermute | solution.py:145
  23.6 13.3 %collective-permute-start.12 = (bf16[48,2176]{1,0:T(8,128)(2,1)S(1)}, bf16[48,2176]{1,0:T(8,128)(2,1)S(1)}, u32[]{:S(2)}, u32[]{:S(2)}) collective-permute-start(bf16[48,2176]{1,0:T(8,128)(2,1)S(1)} %get-tuple-element.50), channel_id=1, source_target_pairs={{0,2},{1,3},{2,0},{3,1},{4,6},{5,7},{6,4},{7,5},{8,10},{9,11},{10,... | collective-permute-start | bytes 626696 | tf_op jit(solution)/shard_map/ppermute | solution.py:145
  24.3 12.6 %collective-permute-start.5 = (bf16[48,2048]{1,0:T(8,128)(2,1)S(1)}, bf16[48,2048]{1,0:T(8,128)(2,1)S(1)}, u32[]{:S(2)}, u32[]{:S(2)}) collective-permute-start(bf16[48,2048]{1,0:T(8,128)(2,1)S(1)} %get-tuple-element.35), channel_id=1, source_target_pairs={{0,24},{1,25},{2,26},{3,27},{4,28},{5,29},{6,30},{7,31},{8,0},{9,1... | collective-permute-start | bytes 589832 | tf_op jit(solution)/shard_map/ppermute | solution.py:354
  26.5 10.4 %collective-permute-start.13 = (bf16[48,1536]{1,0:T(8,128)(2,1)S(1)}, bf16[48,1536]{1,0:T(8,128)(2,1)S(1)}, u32[]{:S(2)}, u32[]{:S(2)}) collective-permute-start(bf16[48,1536]{1,0:T(8,128)(2,1)S(1)} %get-tuple-element.52), channel_id=1, source_target_pairs={{0,6},{1,7},{2,4},{3,5},{4,2},{5,3},{6,0},{7,1},{8,14},{9,15},{10,... | collective-permute-start | bytes 442376 | tf_op jit(solution)/shard_map/ppermute | solution.py:145
  32.1 17.9 %collective-permute-start.11 = (bf16[48,2048]{1,0:T(8,128)(2,1)S(1)}, bf16[48,2048]{1,0:T(8,128)(2,1)S(1)}, u32[]{:S(2)}, u32[]{:S(2)}) collective-permute-start(bf16[48,2048]{1,0:T(8,128)(2,1)S(1)} %get-tuple-element.47), channel_id=1, source_target_pairs={{0,28},{1,29},{2,30},{3,31},{4,24},{5,25},{6,26},{7,27},{8,4},{9,5... | collective-permute-start | bytes 589832 | tf_op jit(solution)/shard_map/ppermute | solution.py:354
  35.7 14.4 %collective-permute-start.10 = (bf16[48,2048]{1,0:T(8,128)(2,1)S(1)}, bf16[48,2048]{1,0:T(8,128)(2,1)S(1)}, u32[]{:S(2)}, u32[]{:S(2)}) collective-permute-start(bf16[48,2048]{1,0:T(8,128)(2,1)S(1)} %get-tuple-element.46), channel_id=1, source_target_pairs={{0,26},{1,27},{2,24},{3,25},{4,30},{5,31},{6,28},{7,29},{8,2},{9,3... | collective-permute-start | bytes 589832 | tf_op jit(solution)/shard_map/ppermute | solution.py:354
  40.2 11.5 %collective-permute-start.15 = (bf16[48,2048]{1,0:T(8,128)(2,1)S(1)}, bf16[48,2048]{1,0:T(8,128)(2,1)S(1)}, u32[]{:S(2)}, u32[]{:S(2)}) collective-permute-start(bf16[48,2048]{1,0:T(8,128)(2,1)S(1)} %get-tuple-element.58), channel_id=1, source_target_pairs={{0,30},{1,31},{2,28},{3,29},{4,26},{5,27},{6,24},{7,25},{8,6},{9,7... | collective-permute-start | bytes 589832 | tf_op jit(solution)/shard_map/ppermute | solution.py:354
  50.6 5.5 %collective-permute-start.14 = (bf16[64,2048]{1,0:T(8,128)(2,1)S(1)}, bf16[64,2048]{1,0:T(8,128)(2,1)S(1)}, u32[]{:S(2)}, u32[]{:S(2)}) collective-permute-start(bf16[64,2048]{1,0:T(8,128)(2,1)S(1)} %get-tuple-element.57), channel_id=1, source_target_pairs={{0,1},{1,0},{2,3},{3,2},{4,5},{5,4},{6,7},{7,6},{8,9},{9,8},{10,11... | collective-permute-start | bytes 786440 | tf_op jit(solution)/shard_map/ppermute | solution.py:145
  51.7 5.5 %collective-permute-start.16 = (bf16[48,2048]{1,0:T(8,128)(2,1)S(1)}, bf16[48,2048]{1,0:T(8,128)(2,1)S(1)}, u32[]{:S(2)}, u32[]{:S(2)}) collective-permute-start(bf16[48,2048]{1,0:T(8,128)(2,1)S(1)} %collective-permute-done.15.rows_6), channel_id=1, source_target_pairs={{0,1},{1,0},{2,3},{3,2},{4,5},{5,4},{6,7},{7,6},{8,9},{9,8},{10,11... | collective-permute-start | bytes 589832 | tf_op jit(solution)/shard_map/ppermute | solution.py:145

commit v4 on v3

--- a/solution.py
+++ b/solution.py
@@ -1,5 +1,3 @@
-import functools
-
 import jax
 import jax.numpy as jnp
 from jax import lax
@@ -136,8 +134,10 @@
 F32 = jnp.float32
 BF16 = jnp.bfloat16
 GATE_LANES = 128
-SUM_COST = 8 * 1024 * 1024
+SUM_COST = 0
+FACTORS_COST = 0
 OWN_LIMIT = 44
+K0_COST = 10 ** 10
 
 
 def swapped(value, mask):
@@ -145,7 +145,19 @@
     return lax.ppermute(value, "expert", [(i, i ^ mask) for i in range(count)])
 
 
-def slot_order(ids, gates, masks, cap):
+def earlier_tokens(lanes):
+    half = lanes // 2
+    before = lax.broadcasted_iota(jnp.int32, (lanes, lanes), 0)
+    after = lax.broadcasted_iota(jnp.int32, (lanes, lanes), 1)
+    same = (before < half) == (after < half)
+    return jnp.where(jnp.logical_and(before <= after, same), 1.0, 0.0).astype(BF16)
+
+
+def earlier_kernel(out):
+    out[...] = earlier_tokens(out.shape[0])
+
+
+def slot_order(ids, gates, masks, cap, upto=None):
     lanes = ids.shape[1]
     half = lanes // 2
     row = lax.broadcasted_iota(jnp.int32, (8, lanes), 0)
@@ -157,10 +169,8 @@
     hit_1 = ids[1:2] == wanted
     named = jnp.where(jnp.logical_or(hit_0, hit_1), 1.0, 0.0)
     gate = jnp.where(hit_0, gates[0:1], jnp.where(hit_1, gates[1:2], 0.0))
-    before = lax.broadcasted_iota(jnp.int32, (lanes, lanes), 0)
-    after = lax.broadcasted_iota(jnp.int32, (lanes, lanes), 1)
-    same = (before < half) == (after < half)
-    upto = jnp.where(jnp.logical_and(before <= after, same), 1.0, 0.0).astype(BF16)
+    if upto is None:
+        upto = earlier_tokens(lanes)
     counts = jnp.dot(named.astype(BF16), upto, preferred_element_type=F32)
     slots = jnp.where(named > 0.5, counts.astype(jnp.int32) - 1, -1)
     slot_no = lax.broadcasted_iota(jnp.int32, (cap, lanes), 0)
@@ -183,8 +193,8 @@
 
 
 def near_kernel(
-    own_ids, own_gate, own_up, own_act, pair_ids, pair_gate, pair_up, pair_act,
-    routes, up_0, up_1, saved_0, saved_1, saved_2, saved_3, gate_0, acts,
+    upto, own_ids, own_gate, own_up, own_act, pair_ids, pair_gate, pair_up, pair_act,
+    up_0, near, saved_0, saved_2, saved_3, gate_0, acts,
 ):
     tokens = own_up.shape[0]
     cap, width = up_0.shape[0] // 2, up_0.shape[1]
@@ -194,22 +204,21 @@
     gates = jnp.concatenate([own_gate[...].astype(F32), pair_gate[...].astype(F32)], axis=1)
     picks = ids.shape[0]
     named = jnp.concatenate([ids.astype(F32), gates], axis=0)
-    rest = jnp.zeros((routes.shape[0] - 2 * picks, routes.shape[1]), F32)
+    rest = jnp.zeros((2 * cap - 2 * picks, ids.shape[1]), F32)
     named = jnp.concatenate([named, rest], axis=0)
-    routes[...] = named.astype(BF16)
     saved_2[:, wide:] = named.astype(BF16)
-    rows, hit_0, hit_1, gate = slot_order(ids, gates, (0, 2, 4, 6), cap)
+    rows, hit_0, hit_1, gate = slot_order(ids, gates, (0, 2, 4, 6), cap, upto[...])
     order_bf = jnp.concatenate(rows, axis=0).astype(BF16)
     gates = gate_columns(rows[:4], gate)
     gate_0[...] = gates[: 2 * cap]
-    up_1[:, width:] = gates[2 * cap :]
+    near[:, width : width + GATE_LANES] = gates[2 * cap :]
     sel_0 = jnp.concatenate([rows[n] * hit_0[n // 2 : n // 2 + 1] for n in range(8)], axis=0)
     sel_1 = jnp.concatenate([rows[n] * hit_1[n // 2 : n // 2 + 1] for n in range(8)], axis=0)
     sel = jnp.concatenate([sel_0.astype(BF16), sel_1.astype(BF16)], axis=1)
     ups = jnp.concatenate([own_up[...], pair_up[...]], axis=0)
     picked = jnp.dot(order_bf[: 4 * cap], ups, preferred_element_type=F32)
     up_0[...] = picked[: 2 * cap].astype(BF16)
-    up_1[:, :width] = picked[2 * cap :].astype(BF16)
+    near[:, :width] = picked[2 * cap :].astype(BF16)
     for block, act in enumerate((own_act, pair_act)):
         for pick in range(picks):
             low = (2 * pick + block) * tokens
@@ -217,8 +226,9 @@
                 part = act[:, pick, side, :]
                 acts[low : low + tokens, side * units : (side + 1) * units] = part
     got = jnp.dot(sel, acts[...], preferred_element_type=F32)
-    for n, out in enumerate((saved_0, saved_1, saved_2, saved_3)):
-        out[:, :wide] = got[2 * cap * n : 2 * cap * (n + 1)].astype(BF16)
+    low = near.shape[1] - wide
+    for n, (out, lane) in enumerate(((saved_0, 0), (near, low), (saved_2, 0), (saved_3, 0))):
+        out[:, lane : lane + wide] = got[2 * cap * n : 2 * cap * (n + 1)].astype(BF16)
 
 
 def read_routes(routes):
@@ -243,44 +253,57 @@
 
 
 def through_expert(up, saved, gate, w_down, w_gate, w_up):
-    grad_hidden = lax.dot_general(up, w_down[...], LAST, preferred_element_type=F32)
-    grad_a, grad_b, scaled = hidden_grads(grad_hidden, saved, gate[:, :1].astype(F32))
+    units = w_down.shape[0]
+    gate = gate[:, :1].astype(F32)
+    by_a, by_b, both = factors(saved[:, :units], saved[:, units:])
+    grad_h = lax.dot_general(up, w_down[...], LAST, preferred_element_type=F32) * gate
+    grad_a = (grad_h * by_a).astype(BF16)
+    grad_b = (grad_h * by_b).astype(BF16)
     back = lax.dot_general(grad_a, w_gate[...], LAST, preferred_element_type=F32)
     back = back + lax.dot_general(grad_b, w_up[...], LAST, preferred_element_type=F32)
-    return back.astype(BF16), scaled
-
-
-def own_kernel(
-    up, saved, gate, w_down, w_gate, w_up,
-    back_out, scaled_out, down_here, gate_here, up_here, arrived,
-):
-    moves = ((w_down, down_here), (w_gate, gate_here), (w_up, up_here))
-    copies = [pltpu.make_async_copy(a, b, arrived.at[n]) for n, (a, b) in enumerate(moves)]
-    for copy in copies:
-        copy.start()
-    copies[0].wait()
-    grad_hidden = lax.dot_general(up[...], down_here[...], LAST, preferred_element_type=F32)
-    grad_a, grad_b, scaled = hidden_grads(grad_hidden, saved[...], gate[:, :1].astype(F32))
+    return back.astype(BF16), (gate * both).astype(BF16)
+
+
+def own_kernel(up, saved, gate, w_down, w_gate, w_up, back_out, scaled_out):
+    back, scaled = through_expert(up[...], saved[...], gate[...], w_down, w_gate, w_up)
+    back_out[...] = back
     scaled_out[...] = scaled
-    copies[1].wait()
-    back = lax.dot_general(grad_a, gate_here[...], LAST, preferred_element_type=F32)
-    copies[2].wait()
-    back = back + lax.dot_general(grad_b, up_here[...], LAST, preferred_element_type=F32)
+
+
+def both_kernel(near, up_2, saved_2, gate_2, w_down, w_gate, w_up, back_1, back_2, scaled_out):
+    each, width = up_2.shape
+    wide = 2 * w_down.shape[0]
+    up = jnp.concatenate([near[:, :width], up_2[...]], axis=0)
+    gate = jnp.concatenate([near[:, width : width + GATE_LANES], gate_2[...]], axis=0)
+    saved = jnp.concatenate([near[:, width + GATE_LANES :], saved_2[:, :wide]], axis=0)
+    back, scaled_out[...] = through_expert(up, saved, gate, w_down, w_gate, w_up)
+    back_1[...] = back[:each]
+    back_2[:, :width] = back[each:]
+    back_2[:, width:] = saved_2[:, wide:]
+
+
+def factors(gate_pre, up_pre):
+    gate_pre, up_pre = gate_pre.astype(F32), up_pre.astype(F32)
+    sig = 1.0 / (1.0 + jnp.exp(-gate_pre))
+    silu = gate_pre * sig
+    return up_pre * sig * (1.0 + gate_pre * (1.0 - sig)), silu, silu * up_pre
+
+
+def factors_kernel(saved, by_a, by_b, both):
+    units = by_a.shape[1]
+    by_a[...], by_b[...], both[...] = factors(saved[:, :units], saved[:, units:])
+
+
+def last_rows_kernel(up, by_a, by_b, both, w_down, w_gate, w_up, back_out, scaled_out):
+    width = back_out.shape[1]
+    gate = up[:, width : width + 1].astype(F32)
+    grad_h = lax.dot_general(up[:, :width], w_down[...], LAST, preferred_element_type=F32) * gate
+    grad_a = (grad_h * by_a[...]).astype(BF16)
+    grad_b = (grad_h * by_b[...]).astype(BF16)
+    scaled_out[...] = (gate * both[...]).astype(BF16)
+    back = lax.dot_general(grad_a, w_gate[...], LAST, preferred_element_type=F32)
+    back = back + lax.dot_general(grad_b, w_up[...], LAST, preferred_element_type=F32)
     back_out[...] = back.astype(BF16)
-
-
-def chunk_kernel(count, *refs):
-    ups, saveds, gates = refs[:count], refs[count : 2 * count], refs[2 * count : 3 * count]
-    w_down, w_gate, w_up = refs[3 * count : 3 * count + 3]
-    backs, scaled_out = refs[3 * count + 3 : -1], refs[-1]
-    width, units = w_gate.shape[0], w_gate.shape[1]
-    each = ups[0].shape[0]
-    up = jnp.concatenate([ref[:, :width] for ref in ups], axis=0)
-    saved = jnp.concatenate([ref[:, : 2 * units] for ref in saveds], axis=0)
-    gate = jnp.concatenate([ref[:, ref.shape[1] - GATE_LANES :] for ref in gates], axis=0)
-    back, scaled_out[...] = through_expert(up, saved, gate, w_down, w_gate, w_up)
-    for n, out in enumerate(backs):
-        out[...] = back[n * each : (n + 1) * each]
 
 
 def down_kernel(scaled_a, scaled_b, scaled_c, up_a, up_b, up_c, up_d, out):
@@ -289,25 +312,30 @@
     out[...] = lax.dot_general(scaled, ups, FIRST, preferred_element_type=F32).astype(BF16)
 
 
-def sum_kernel(routes, rows_0, rows_1, rows_2, own, other):
+def two_sum_kernel(rows_1, rows_2, part, order_0, order_67):
+    width = part.shape[1]
+    ids, gates = read_routes(rows_2[:, width:])
+    order = slot_order(ids, gates, (0, 2, 4, 6, 7), rows_2.shape[0] // 2)[0]
+    order_0[...] = jnp.concatenate(order[:2], axis=0).astype(BF16)
+    order_67[...] = jnp.concatenate([order[6], order[8]], axis=0).astype(BF16)
+    order = jnp.concatenate(order[2:6], axis=0).astype(BF16)
+    rows = jnp.concatenate([rows_1[...], rows_2[:, :width]], axis=0)
+    part[...] = lax.dot_general(order, rows, FIRST, preferred_element_type=F32)
+
+
+def sum_kernel(order, part, rows_0, own, other):
     tokens = own.shape[0]
-    ids, gates = read_routes(routes[...])
-    order = slot_order(ids, gates, (0, 2, 4), rows_0.shape[0] // 2)[0]
-    order = jnp.concatenate(order, axis=0).astype(BF16)
-    rows = jnp.concatenate([rows_0[...], rows_1[...], rows_2[...]], axis=0)
-    back = lax.dot_general(order, rows, FIRST, preferred_element_type=F32)
+    back = lax.dot_general(order[...], rows_0[...], FIRST, preferred_element_type=F32)
+    back = part[...] + back
     own[...] = back[:tokens]
     other[...] = back[tokens:].astype(BF16)
 
 
-def last_kernel(routes, own, other, rows_6, rows_7, out):
+def last_kernel(order, own, other, rows_6, rows_7, out):
     tokens, cap = own.shape[0], rows_6.shape[0] // 2
-    ids, gates = read_routes(routes[...])
-    order = slot_order(ids, gates, (6, 7), cap)[0]
-    order = jnp.concatenate([order[0], order[2]], axis=0).astype(BF16)
     rows = [rows_6[...].astype(F32)[:cap], rows_7[...].astype(F32)[cap:]]
     rows = jnp.concatenate(rows, axis=0).astype(BF16)
-    back = lax.dot_general(order, rows, FIRST, preferred_element_type=F32)
+    back = lax.dot_general(order[...], rows, FIRST, preferred_element_type=F32)
     out[...] = (own[...] + other[...].astype(F32) + back[:tokens]).astype(BF16)
 
 
@@ -321,23 +349,9 @@
         out_shape=outs,
         scratch_shapes=scratch,
         compiler_params=pltpu.CompilerParams(vmem_limit_bytes=limit * 1024 * 1024),
-        cost_estimate=pl.CostEstimate(flops=0, bytes_accessed=cost, transcendentals=0),
+        cost_estimate=pl.CostEstimate(flops=cost, bytes_accessed=0, transcendentals=0),
         **blocks,
     )(*args)
-
-
-def hidden_grads(grad_hidden, saved, gate):
-    units = grad_hidden.shape[1]
-    saved_f = saved.astype(F32)
-    gate_pre = saved_f[:, :units]
-    up_pre = saved_f[:, units:]
-    sig = 1.0 / (1.0 + jnp.exp(-gate_pre))
-    silu = gate_pre * sig
-    grad_h = grad_hidden * gate
-    grad_a = (grad_h * up_pre * sig * (1.0 + gate_pre * (1.0 - sig))).astype(BF16)
-    grad_b = (grad_h * silu).astype(BF16)
-    scaled = (gate * silu * up_pre).astype(BF16)
-    return grad_a, grad_b, scaled
 
 
 def after(value, *others):
@@ -367,35 +381,28 @@
     up, act = grad_out[0], pre_act[0]
     ids, gate = route_ids[0].T, route_gate[0].T
     far_up = swapped(up, 4)
-    routes, own_rows, near_rows, saved_0, saved_1, saved_2, saved_3, gate_0 = local_call(
+    (upto,) = local_call(earlier_kernel, [shape(2 * tokens, 2 * tokens)], (), cost=K0_COST)
+    own_rows, near_rows, saved_0, saved_2, saved_3, gate_0 = local_call(
         near_kernel,
-        [shape(2 * cap, 2 * tokens)]
-        + [shape(2 * cap, width), shape(2 * cap, width + GATE_LANES)]
-        + [shape(2 * cap, wide + (2 * tokens if n == 2 else 0)) for n in range(4)]
+        [shape(2 * cap, width), shape(2 * cap, width + GATE_LANES + wide)]
+        + [shape(2 * cap, wide), shape(2 * cap, wide + 2 * tokens), shape(2 * cap, wide)]
         + [shape(2 * cap, GATE_LANES)],
-        (ids, gate, up, act, swapped(ids, 1), swapped(gate, 1), swapped(up, 1), swapped(act, 1)),
+        (upto, ids, gate, up, act, swapped(ids, 1), swapped(gate, 1), swapped(up, 1), swapped(act, 1)),
         [pltpu.VMEM((4 * tokens, wide), BF16)],
     )
     near_rows = swapped(near_rows, 2)
     saved_2 = swapped(saved_2, 4)
-    saved_1 = swapped(saved_1, 2)
-    vmem, hbm = (pl.BlockSpec(memory_space=space) for space in (pltpu.VMEM, pltpu.HBM))
     weights = (w_down[0], w_gate[0], w_up[0])
-    back_0, scaled_0, *weights = local_call(
+    back_0, scaled_0 = local_call(
         own_kernel,
-        [shape(2 * cap, width), shape(2 * cap, units)] + [shape(*w.shape) for w in weights],
+        [shape(2 * cap, width), shape(2 * cap, units)],
         (own_rows, saved_0, gate_0, *weights),
-        [pltpu.SemaphoreType.DMA((3,))],
-        limit=OWN_LIMIT,
-        in_specs=[vmem] * 3 + [hbm] * 3,
-        out_specs=[vmem] * 5,
-    )
-    next_routes = before_section(routes, 0)
-    far_up = after(far_up, back_0, next_routes)
+    )
+    far_up = after(far_up, back_0)
     far_both = lax.all_gather(
         far_up, "expert", axis=0, tiled=True, axis_index_groups=[[i, i + 1] for i in range(0, 8, 2)]
     )
-    saved_3 = swapped(after(saved_3, far_up), 6)
+    saved_3 = swapped(saved_3, 6)
     two_rows, three_rows, gate_2 = local_call(
         far_kernel,
         [shape(2 * cap, width), shape(2 * cap, width + GATE_LANES), shape(2 * cap, GATE_LANES)],
@@ -403,17 +410,23 @@
     )
     three_rows = swapped(three_rows, 2)
     home_0 = before_section(back_0, 0)
-    saved_1 = after(saved_1, two_rows)
+    near_rows = after(near_rows, home_0)
     back_1, back_2, scaled_12 = local_call(
-        functools.partial(chunk_kernel, 2),
-        [shape(2 * cap, width)] * 2 + [shape(4 * cap, units)],
-        (near_rows, two_rows, saved_1, saved_2, near_rows, gate_2, *weights),
-    )
-    saved_3 = after(saved_3, back_2, home_0)
+        both_kernel,
+        [shape(2 * cap, width), shape(2 * cap, width + 2 * tokens), shape(4 * cap, units)],
+        (near_rows, two_rows, saved_2, gate_2, *weights),
+    )
+    saved_3 = after(saved_3, back_2)
+    by_saved = local_call(
+        factors_kernel,
+        [jax.ShapeDtypeStruct((2 * cap, units), F32)] * 3,
+        (saved_3,),
+        cost=FACTORS_COST,
+    )
     back_3, scaled_3 = local_call(
-        functools.partial(chunk_kernel, 1),
+        last_rows_kernel,
         [shape(2 * cap, width), shape(2 * cap, units)],
-        (three_rows, saved_3, three_rows, *weights),
+        (three_rows, *by_saved, *weights),
     )
     home_2 = before_section(back_2, 4)
     home_1 = before_section(back_1, 2)
@@ -437,18 +450,24 @@
         out_specs=[pl.BlockSpec((units, width // parts), lambda n: (0, n))],
     )
     home_2 = after(home_2, down)
+    part, order_0, order_67 = local_call(
+        two_sum_kernel,
+        [jax.ShapeDtypeStruct((2 * tokens, width), F32)]
+        + [shape(2 * cap, 2 * tokens)] * 2,
+        (home_1, home_2),
+        cost=SUM_COST,
+    )
+    home_3 = after(home_3, part)
     summed, other = local_call(
         sum_kernel,
         [jax.ShapeDtypeStruct((tokens, width), F32), shape(tokens, width)],
-        (next_routes, home_0, home_1, home_2),
-        cost=SUM_COST,
+        (order_0, part, home_0),
     )
     other = swapped(other, 1)
-    home_3 = after(home_3, summed)
     (total,) = local_call(
         last_kernel,
         [shape(tokens, width)],
-        (next_routes, summed, other, home_3, swapped(home_3, 1)),
+        (order_67, summed, other, home_3, swapped(home_3, 1)),
     )
     return total[None], down[None]
 

time: 58.5 us -> 55.9 us (0.956)
  the two profiles are of different devices: /device:TPU:3 before, /device:TPU:0 now
where the time goes in v4:
time: 55.9 us; the launch traced here: 55 us
  starting transfers between devices  21.6 us (39%)
  Pallas kernels  17.9 us (32%)
  waiting for transfers between devices  12.4 us (22%)
  blocking collectives  2.17 us (4%)
  between operations  0.79 us (1%)
    pallas_call x11, Pallas kernels, local_call(): pl.pallas_call(kernel, out_shape=outs, scratch_shapes=scratch, compiler_p...  17.9 us
    ppermute x11, starting transfers between devices, swapped(): return lax.ppermute(value, 'expert', [(i, i ^ mask) for i in range(count)])  11.2 us
    ppermute x4, starting transfers between devices, before_section(): return lax.ppermute(value, ('section', 'expert'), pairs)  10.5 us
    ppermute x11, waiting for transfers between devices, swapped(): return lax.ppermute(value, 'expert', [(i, i ^ mask) for i in range(count)])  8.67 us
    ppermute x4, waiting for transfers between devices, before_section(): return lax.ppermute(value, ('section', 'expert'), pairs)  3.75 us
    all_gather x1, blocking collectives, on_device_pairs(): lax.all_gather(far_up, 'expert', axis=0, tiled=True, axis_index_groups=[[...  2.17 us
  transfers between devices with their start and end apart: 15, of which 7 were waited for; matrix products, arithmetic and copies ran while one was open for 0% of the time, Pallas kernels for 31%

profile of v4, /device:TPU:0, one launch (start us, length us, event | category | flops | bytes accessed | tf_op | source)
XLA Modules:
  0.0 55.0 jit_solution(18415734561752294403)
XLA Ops:
  0.6 0.5 collective-permute-start.2
  1.1 3.7 %collective-permute-start.7 = (bf16[64,2048]{1,0:T(8,128)(2,1)}, bf16[64,2048]{1,0:T(8,128)(2,1)S(1)}, u32[]{:S(2)}, u32[]{:S(2)}) collective-permute-start(bf16[64,2048]{1,0:T(8,128)(2,1)} %bitcast.25), channel_id=1, source_target_pairs={{0,4},{1,5},{2,6},{3,7},{4,0},{5,1},{6,2},{7,3},{8,12},{9,13},{10,... | collective-permute-start | bytes 786440 | tf_op jit(solution)/shard_map/ppermute | solution.py:145
  4.8 0.2 collective-permute-start
  5.0 0.3 collective-permute-start.1
  5.3 0.2 collective-permute-start.3
  5.6 0.7 %collective-permute-done.1.pair_gate = bf16[2,64]{1,0:T(2,128)(2,1)S(1)} collective-permute-done((bf16[2,64]{1,0:T(2,128)(2,1)}, bf16[2,64]{1,0:T(2,128)(2,1)S(1)}, u32[]{:S(2)}, u32[]{:S(2)}) %collective-permute-start.1) | collective-permute-done | bytes 288 | tf_op jit(solution)/shard_map/ppermute | solution.py:145
  6.3 0.0 collective-permute-done.pair_ids
  6.3 0.0 collective-permute-done.2.pair_up
  6.3 1.1 %collective-permute-done.3.pair_act = bf16[64,2,2,768]{3,2,1,0:T(2,128)(2,1)S(1)} collective-permute-done((bf16[64,2,2,768]{3,2,1,0:T(2,128)(2,1)}, bf16[64,2,2,768]{3,2,1,0:T(2,128)(2,1)S(1)}, u32[]{:S(2)}, u32[]{:S(2)}) %collective-permute-start.3) | collective-permute-done | bytes 393248 | tf_op jit(solution)/shard_map/ppermute | solution.py:145
  7.3 0.0 copy-done.3
  7.3 0.0 copy-done.4
  7.3 0.0 copy-done.5
  7.3 0.0 copy-done.6
  7.4 2.3 %shard_map.87 = (bf16[48,2048]{1,0:T(8,128)(2,1)S(1)}, bf16[48,3712]{1,0:T(8,128)(2,1)S(1)}, bf16[48,1536]{1,0:T(8,128)(2,1)S(1)}, bf16[48,1664]{1,0:T(8,128)(2,...) custom-call(bf16[128,128]{1,0:T(8,128)(2,1)S(1)} %shard_map.86.upto, s32[2,64]{1,0:T(2,128)S(1)} %bitcast.28, ...), custom_call_target="tpu_custom_call" | custom-call | tf_op jit(solution)/shard_map/pallas_call | solution.py:347
  9.7 1.6 %collective-permute-start.4 = (bf16[48,3712]{1,0:T(8,128)(2,1)S(1)}, bf16[48,3712]{1,0:T(8,128)(2,1)S(1)}, u32[]{:S(2)}, u32[]{:S(2)}) collective-permute-start(bf16[48,3712]{1,0:T(8,128)(2,1)S(1)} %get-tuple-element.31), channel_id=1, source_target_pairs={{0,2},{1,3},{2,0},{3,1},{4,6},{5,7},{6,4},{7,5},{8,10},{9,11},{10,... | collective-permute-start | bytes 1069064 | tf_op jit(solution)/shard_map/ppermute | solution.py:145
  11.3 0.3 collective-permute-start.6
  11.7 0.0 copy-done
  11.7 0.0 copy-done.1
  11.7 0.0 copy-done.2
  11.7 3.3 %shard_map.88 = (bf16[48,2048]{1,0:T(8,128)(2,1)S(1)}, bf16[48,768]{1,0:T(8,128)(2,1)S(1)}) custom-call(bf16[48,2048]{1,0:T(8,128)(2,1)S(1)} %get-tuple-element.32.up.up_a, bf16[48,1536]{1,0:T(8,128)(2,1)S(1)} %get-tuple-element.33.saved, bf16[48,128]{1,0:T(8,128)(2,1)S(1)} %get-tuple-element.34.gate, bf16[768,2048]{1,0:T(8,128)(2,1)S(1)} %bitcast.13, ...), custom_call_target="tpu_custom_call" | custom-call | tf_op jit(solution)/shard_map/pallas_call | solution.py:347
  15.0 2.5 %collective-permute-start.5 = (bf16[48,2048]{1,0:T(8,128)(2,1)S(1)}, bf16[48,2048]{1,0:T(8,128)(2,1)S(1)}, u32[]{:S(2)}, u32[]{:S(2)}) collective-permute-start(bf16[48,2048]{1,0:T(8,128)(2,1)S(1)} %get-tuple-element.35), channel_id=1, source_target_pairs={{0,24},{1,25},{2,26},{3,27},{4,28},{5,29},{6,30},{7,31},{8,0},{9,1... | collective-permute-start | bytes 589832 | tf_op jit(solution)/shard_map/ppermute | solution.py:368
  17.5 0.4 collective-permute-done.7
  17.9 2.2 %all_gather.3.both_up = bf16[128,2048]{1,0:T(8,128)(2,1)S(1)} all-gather(bf16[64,2048]{1,0:T(8,128)(2,1)S(1)} %collective-permute-done.7), channel_id=1, replica_groups={{0,1},{2,3},{4,5},{6,7},{8,9},{10,11},{12,13},{14,15},{16,17},{18,19},{..., dimensions={0}, use_global_device_ids=true | all-gather | bytes 786432 | tf_op jit(solution)/shard_map/all_gather | solution.py:402
  20.1 4.5 %collective-permute-done.6.saved_2 = bf16[48,1664]{1,0:T(8,128)(2,1)S(1)} collective-permute-done((bf16[48,1664]{1,0:T(8,128)(2,1)S(1)}, bf16[48,1664]{1,0:T(8,128)(2,1)S(1)}, u32[]{:S(2)}, u32[]{:S(2)}) %collective-permute-start.6) | collective-permute-done | bytes 159776 | tf_op jit(solution)/shard_map/ppermute | solution.py:145
  24.5 0.5 shard_map.89
  25.0 0.7 %collective-permute-start.10 = (bf16[48,2176]{1,0:T(8,128)(2,1)S(1)}, bf16[48,2176]{1,0:T(8,128)(2,1)S(1)}, u32[]{:S(2)}, u32[]{:S(2)}) collective-permute-start(bf16[48,2176]{1,0:T(8,128)(2,1)S(1)} %get-tuple-element.45), channel_id=1, source_target_pairs={{0,2},{1,3},{2,0},{3,1},{4,6},{5,7},{6,4},{7,5},{8,10},{9,11},{10,... | collective-permute-start | bytes 626696 | tf_op jit(solution)/shard_map/ppermute | solution.py:145
  25.7 3.0 %collective-permute-start.11 = (bf16[48,1536]{1,0:T(8,128)(2,1)S(1)}, bf16[48,1536]{1,0:T(8,128)(2,1)S(1)}, u32[]{:S(2)}, u32[]{:S(2)}) collective-permute-start(bf16[48,1536]{1,0:T(8,128)(2,1)S(1)} %get-tuple-element.46), channel_id=1, source_target_pairs={{0,6},{1,7},{2,4},{3,5},{4,2},{5,3},{6,0},{7,1},{8,14},{9,15},{10,... | collective-permute-start | bytes 442376 | tf_op jit(solution)/shard_map/ppermute | solution.py:145
  28.7 0.0 collective-permute-done.5.rows_0
  28.7 0.0 collective-permute-done.4.near.up_b
  28.7 3.5 %shard_map.90 = (bf16[48,2048]{1,0:T(8,128)(2,1)S(1)}, bf16[48,2176]{1,0:T(8,128)(2,1)S(1)}, bf16[96,768]{1,0:T(8,128)(2,1)S(1)}) custom-call(bf16[48,3712]{1,0:T(8,128)(2,1)S(1)} %collective-permute-done.4.near.up_b, bf16[48,2048]{1,0:T(8,128)(2,1)S(1)} %get-tuple-element.39.up_2.up_c, bf16[48,1664]{1,0:T(8,128)(2,1)S(1)} %collective-permute-done.6.saved_2, ...), custom_call_target="tpu_custom_call" | custom-call | tf_op jit(solution)/shard_map/pallas_call | solution.py:347
  32.2 2.4 %collective-permute-start.9 = (bf16[48,2176]{1,0:T(8,128)(2,1)S(1)}, bf16[48,2176]{1,0:T(8,128)(2,1)S(1)}, u32[]{:S(2)}, u32[]{:S(2)}) collective-permute-start(bf16[48,2176]{1,0:T(8,128)(2,1)S(1)} %get-tuple-element.42), channel_id=1, source_target_pairs={{0,28},{1,29},{2,30},{3,31},{4,24},{5,25},{6,26},{7,27},{8,4},{9,5... | collective-permute-start | bytes 626696 | tf_op jit(solution)/shard_map/ppermute | solution.py:368
  34.6 1.8 %collective-permute-start.8 = (bf16[48,2048]{1,0:T(8,128)(2,1)S(1)}, bf16[48,2048]{1,0:T(8,128)(2,1)S(1)}, u32[]{:S(2)}, u32[]{:S(2)}) collective-permute-start(bf16[48,2048]{1,0:T(8,128)(2,1)S(1)} %get-tuple-element.41), channel_id=1, source_target_pairs={{0,26},{1,27},{2,24},{3,25},{4,30},{5,31},{6,28},{7,29},{8,2},{9,3... | collective-permute-start | bytes 589832 | tf_op jit(solution)/shard_map/ppermute | solution.py:368
  36.4 0.7 %collective-permute-done.11.saved = bf16[48,1536]{1,0:T(8,128)(2,1)S(1)} collective-permute-done((bf16[48,1536]{1,0:T(8,128)(2,1)S(1)}, bf16[48,1536]{1,0:T(8,128)(2,1)S(1)}, u32[]{:S(2)}, u32[]{:S(2)}) %collective-permute-start.11) | collective-permute-done | bytes 147488 | tf_op jit(solution)/shard_map/ppermute | solution.py:145
  37.1 0.1 shard_map.91
  37.2 0.0 collective-permute-done.10.up.up_d
  37.2 3.3 %shard_map.92 = (bf16[48,2048]{1,0:T(8,128)(2,1)S(1)}, bf16[48,768]{1,0:T(8,128)(2,1)S(1)}) custom-call(bf16[48,2176]{1,0:T(8,128)(2,1)S(1)} %collective-permute-done.10.up.up_d, f32[48,768]{1,0:T(8,128)S(1)} %get-tuple-element.48.by_a, f32[48,768]{1,0:T(8,128)S(1)} %get-tuple-element.49.by_b, f32[48,768]{1,0:T(8,128)S(1)} %get-tuple-element.50.both, ...), custom_call_target="tpu_custom_call" | custom-call | tf_op jit(solution)/shard_map/pallas_call | solution.py:347
  40.5 3.8 %collective-permute-start.13 = (bf16[48,2048]{1,0:T(8,128)(2,1)S(1)}, bf16[48,2048]{1,0:T(8,128)(2,1)S(1)}, u32[]{:S(2)}, u32[]{:S(2)}) collective-permute-start(bf16[48,2048]{1,0:T(8,128)(2,1)S(1)} %get-tuple-element.58), channel_id=1, source_target_pairs={{0,30},{1,31},{2,28},{3,29},{4,26},{5,27},{6,24},{7,25},{8,6},{9,7... | collective-permute-start | bytes 589832 | tf_op jit(solution)/shard_map/ppermute | solution.py:368
  44.3 3.2 %shard_map.93 = bf16[768,2048]{1,0:T(8,128)(2,1)} custom-call(bf16[48,768]{1,0:T(8,128)(2,1)S(1)} %get-tuple-element.43.scaled_a, bf16[96,768]{1,0:T(8,128)(2,1)S(1)} %get-tuple-element.44.scaled_b, bf16[48,768]{1,0:T(8,128)(2,1)S(1)} %get-tuple-element.51.scaled_c, bf16[48,2048]{1,0:T(8,128)(2,1)S(1)} %get-tuple-element.32.up.up_a, ...), custom_call_target="tpu_custom_call" | custom-call | tf_op jit(solution)/shard_map/pallas_call | solution.py:347
  47.5 3.7 %collective-permute-done.9.rows_2 = bf16[48,2176]{1,0:T(8,128)(2,1)S(1)} collective-permute-done((bf16[48,2176]{1,0:T(8,128)(2,1)S(1)}, bf16[48,2176]{1,0:T(8,128)(2,1)S(1)}, u32[]{:S(2)}, u32[]{:S(2)}) %collective-permute-start.9) | collective-permute-done | bytes 208928 | tf_op jit(solution)/shard_map/ppermute | solution.py:368
  51.3 0.0 collective-permute-done.8.rows_1
  51.3 0.5 shard_map.94
  51.7 0.3 shard_map.95
  52.1 0.1 collective-permute-start.12
  52.1 0.0 collective-permute-done.13.rows_6
  52.2 0.5 collective-permute-start.14
  52.6 1.3 %collective-permute-done.14.rows_7 = bf16[48,2048]{1,0:T(8,128)(2,1)S(1)} collective-permute-done((bf16[48,2048]{1,0:T(8,128)(2,1)S(1)}, bf16[48,2048]{1,0:T(8,128)(2,1)S(1)}, u32[]{:S(2)}, u32[]{:S(2)}) %collective-permute-start.14) | collective-permute-done | bytes 196640 | tf_op jit(solution)/shard_map/ppermute | solution.py:145
  53.9 0.0 collective-permute-done.12.other
  54.0 1.0 %shard_map.96 = bf16[64,2048]{1,0:T(8,128)(2,1)} custom-call(bf16[48,128]{1,0:T(8,128)(2,1)S(1)} %get-tuple-element.53.order, f32[64,2048]{1,0:T(8,128)S(1)} %get-tuple-element.56.own, bf16[64,2048]{1,0:T(8,128)(2,1)S(1)} %collective-permute-done.12.other, bf16[48,2048]{1,0:T(8,128)(2,1)S(1)} %collective-permute-done.13.rows_6, ...), custom_call_target="tpu_custom_call" | custom-call | tf_op jit(solution)/shard_map/pallas_call | solution.py:347
  (8 shorter events, 0.0 us)
Async XLA Ops:
  0.6 5.7 %collective-permute-start.2 = (bf16[64,2048]{1,0:T(8,128)(2,1)}, bf16[64,2048]{1,0:T(8,128)(2,1)S(1)}, u32[]{:S(2)}, u32[]{:S(2)}) collective-permute-start(bf16[64,2048]{1,0:T(8,128)(2,1)} %bitcast.24), channel_id=1, source_target_pairs={{0,1},{1,0},{2,3},{3,2},{4,5},{5,4},{6,7},{7,6},{8,9},{9,8},{10,11... | collective-permute-start | bytes 786440 | tf_op jit(solution)/shard_map/ppermute | solution.py:145
  1.1 16.7 %collective-permute-start.7 = (bf16[64,2048]{1,0:T(8,128)(2,1)}, bf16[64,2048]{1,0:T(8,128)(2,1)S(1)}, u32[]{:S(2)}, u32[]{:S(2)}) collective-permute-start(bf16[64,2048]{1,0:T(8,128)(2,1)} %bitcast.25), channel_id=1, source_target_pairs={{0,4},{1,5},{2,6},{3,7},{4,0},{5,1},{6,2},{7,3},{8,12},{9,13},{10,... | collective-permute-start | bytes 786440 | tf_op jit(solution)/shard_map/ppermute | solution.py:145
  4.8 1.5 %collective-permute-start = (s32[2,64]{1,0:T(2,128)}, s32[2,64]{1,0:T(2,128)S(1)}, u32[]{:S(2)}, u32[]{:S(2)}) collective-permute-start(s32[2,64]{1,0:T(2,128)} %bitcast.27), channel_id=1, source_target_pairs={{0,1},{1,0},{2,3},{3,2},{4,5},{5,4},{6,7},{7,6},{8,9},{9,8},{10,11... | collective-permute-start | bytes 1544 | tf_op jit(solution)/shard_map/ppermute | solution.py:145
  5.0 1.3 %collective-permute-start.1 = (bf16[2,64]{1,0:T(2,128)(2,1)}, bf16[2,64]{1,0:T(2,128)(2,1)S(1)}, u32[]{:S(2)}, u32[]{:S(2)}) collective-permute-start(bf16[2,64]{1,0:T(2,128)(2,1)} %bitcast.29), channel_id=1, source_target_pairs={{0,1},{1,0},{2,3},{3,2},{4,5},{5,4},{6,7},{7,6},{8,9},{9,8},{10,11... | collective-permute-start | bytes 776 | tf_op jit(solution)/shard_map/ppermute | solution.py:145
  5.3 2.0 %copy-start.3 = (bf16[1,64,2,2,768]{4,3,2,1,0:T(2,128)(2,1)S(1)}, bf16[1,64,2,2,768]{4,3,2,1,0:T(2,128)(2,1)}, u32[]{:S(2)}) copy-start(bf16[1,64,2,2,768]{4,3,2,1,0:T(2,128)(2,1)} %param.8) | copy-start | bytes 1179652
  5.3 2.0 %copy-start.4 = (bf16[1,64,2048]{2,1,0:T(8,128)(2,1)S(1)}, bf16[1,64,2048]{2,1,0:T(8,128)(2,1)}, u32[]{:S(2)}) copy-start(bf16[1,64,2048]{2,1,0:T(8,128)(2,1)} %param.7) | copy-start | bytes 786436
  5.3 2.0 %copy-start.5 = (s32[1,64,2]{1,2,0:T(2,128)S(1)}, s32[1,64,2]{1,2,0:T(2,128)}, u32[]{:S(2)}) copy-start(s32[1,64,2]{1,2,0:T(2,128)} %param.9) | copy-start | bytes 1540
  5.3 2.0 %copy-start.6 = (bf16[1,64,2]{1,2,0:T(2,128)(2,1)S(1)}, bf16[1,64,2]{1,2,0:T(2,128)(2,1)}, u32[]{:S(2)}) copy-start(bf16[1,64,2]{1,2,0:T(2,128)(2,1)} %param.10) | copy-start | bytes 772
  5.3 2.0 %collective-permute-start.3 = (bf16[64,2,2,768]{3,2,1,0:T(2,128)(2,1)}, bf16[64,2,2,768]{3,2,1,0:T(2,128)(2,1)S(1)}, u32[]{:S(2)}, u32[]{:S(2)}) collective-permute-start(bf16[64,2,2,768]{3,2,1,0:T(2,128)(2,1)} %bitcast.22), channel_id=1, source_target_pairs={{0,1},{1,0},{2,3},{3,2},{4,5},{5,4},{6,7},{7,6},{8,9},{9,8},{10,11... | collective-permute-start | bytes 1179656 | tf_op jit(solution)/shard_map/ppermute | solution.py:145
  5.6 6.1 %copy-start = (bf16[1,768,2048]{2,1,0:T(8,128)(2,1)S(1)}, bf16[1,768,2048]{2,1,0:T(8,128)(2,1)}, u32[]{:S(2)}) copy-start(bf16[1,768,2048]{2,1,0:T(8,128)(2,1)} %param.13) | copy-start | bytes 9437188
  5.6 6.1 %copy-start.1 = (bf16[1,2048,768]{2,1,0:T(8,128)(2,1)S(1)}, bf16[1,2048,768]{2,1,0:T(8,128)(2,1)}, u32[]{:S(2)}) copy-start(bf16[1,2048,768]{2,1,0:T(8,128)(2,1)} %param.11) | copy-start | bytes 9437188
  5.6 6.1 %copy-start.2 = (bf16[1,2048,768]{2,1,0:T(8,128)(2,1)S(1)}, bf16[1,2048,768]{2,1,0:T(8,128)(2,1)}, u32[]{:S(2)}) copy-start(bf16[1,2048,768]{2,1,0:T(8,128)(2,1)} %param.12) | copy-start | bytes 9437188
  9.7 19.0 %collective-permute-start.4 = (bf16[48,3712]{1,0:T(8,128)(2,1)S(1)}, bf16[48,3712]{1,0:T(8,128)(2,1)S(1)}, u32[]{:S(2)}, u32[]{:S(2)}) collective-permute-start(bf16[48,3712]{1,0:T(8,128)(2,1)S(1)} %get-tuple-element.31), channel_id=1, source_target_pairs={{0,2},{1,3},{2,0},{3,1},{4,6},{5,7},{6,4},{7,5},{8,10},{9,11},{10,... | collective-permute-start | bytes 1069064 | tf_op jit(solution)/shard_map/ppermute | solution.py:145
  11.3 13.2 %collective-permute-start.6 = (bf16[48,1664]{1,0:T(8,128)(2,1)S(1)}, bf16[48,1664]{1,0:T(8,128)(2,1)S(1)}, u32[]{:S(2)}, u32[]{:S(2)}) collective-permute-start(bf16[48,1664]{1,0:T(8,128)(2,1)S(1)} %get-tuple-element.37), channel_id=1, source_target_pairs={{0,4},{1,5},{2,6},{3,7},{4,0},{5,1},{6,2},{7,3},{8,12},{9,13},{10,... | collective-permute-start | bytes 479240 | tf_op jit(solution)/shard_map/ppermute | solution.py:145
  15.0 13.7 %collective-permute-start.5 = (bf16[48,2048]{1,0:T(8,128)(2,1)S(1)}, bf16[48,2048]{1,0:T(8,128)(2,1)S(1)}, u32[]{:S(2)}, u32[]{:S(2)}) collective-permute-start(bf16[48,2048]{1,0:T(8,128)(2,1)S(1)} %get-tuple-element.35), channel_id=1, source_target_pairs={{0,24},{1,25},{2,26},{3,27},{4,28},{5,29},{6,30},{7,31},{8,0},{9,1... | collective-permute-start | bytes 589832 | tf_op jit(solution)/shard_map/ppermute | solution.py:368
  25.0 12.2 %collective-permute-start.10 = (bf16[48,2176]{1,0:T(8,128)(2,1)S(1)}, bf16[48,2176]{1,0:T(8,128)(2,1)S(1)}, u32[]{:S(2)}, u32[]{:S(2)}) collective-permute-start(bf16[48,2176]{1,0:T(8,128)(2,1)S(1)} %get-tuple-element.45), channel_id=1, source_target_pairs={{0,2},{1,3},{2,0},{3,1},{4,6},{5,7},{6,4},{7,5},{8,10},{9,11},{10,... | collective-permute-start | bytes 626696 | tf_op jit(solution)/shard_map/ppermute | solution.py:145
  25.7 11.4 %collective-permute-start.11 = (bf16[48,1536]{1,0:T(8,128)(2,1)S(1)}, bf16[48,1536]{1,0:T(8,128)(2,1)S(1)}, u32[]{:S(2)}, u32[]{:S(2)}) collective-permute-start(bf16[48,1536]{1,0:T(8,128)(2,1)S(1)} %get-tuple-element.46), channel_id=1, source_target_pairs={{0,6},{1,7},{2,4},{3,5},{4,2},{5,3},{6,0},{7,1},{8,14},{9,15},{10,... | collective-permute-start | bytes 442376 | tf_op jit(solution)/shard_map/ppermute | solution.py:145
  32.2 19.1 %collective-permute-start.9 = (bf16[48,2176]{1,0:T(8,128)(2,1)S(1)}, bf16[48,2176]{1,0:T(8,128)(2,1)S(1)}, u32[]{:S(2)}, u32[]{:S(2)}) collective-permute-start(bf16[48,2176]{1,0:T(8,128)(2,1)S(1)} %get-tuple-element.42), channel_id=1, source_target_pairs={{0,28},{1,29},{2,30},{3,31},{4,24},{5,25},{6,26},{7,27},{8,4},{9,5... | collective-permute-start | bytes 626696 | tf_op jit(solution)/shard_map/ppermute | solution.py:368
  34.6 16.7 %collective-permute-start.8 = (bf16[48,2048]{1,0:T(8,128)(2,1)S(1)}, bf16[48,2048]{1,0:T(8,128)(2,1)S(1)}, u32[]{:S(2)}, u32[]{:S(2)}) collective-permute-start(bf16[48,2048]{1,0:T(8,128)(2,1)S(1)} %get-tuple-element.41), channel_id=1, source_target_pairs={{0,26},{1,27},{2,24},{3,25},{4,30},{5,31},{6,28},{7,29},{8,2},{9,3... | collective-permute-start | bytes 589832 | tf_op jit(solution)/shard_map/ppermute | solution.py:368
  40.5 11.6 %collective-permute-start.13 = (bf16[48,2048]{1,0:T(8,128)(2,1)S(1)}, bf16[48,2048]{1,0:T(8,128)(2,1)S(1)}, u32[]{:S(2)}, u32[]{:S(2)}) collective-permute-start(bf16[48,2048]{1,0:T(8,128)(2,1)S(1)} %get-tuple-element.58), channel_id=1, source_target_pairs={{0,30},{1,31},{2,28},{3,29},{4,26},{5,27},{6,24},{7,25},{8,6},{9,7... | collective-permute-start | bytes 589832 | tf_op jit(solution)/shard_map/ppermute | solution.py:368
  52.1 1.9 %collective-permute-start.12 = (bf16[64,2048]{1,0:T(8,128)(2,1)S(1)}, bf16[64,2048]{1,0:T(8,128)(2,1)S(1)}, u32[]{:S(2)}, u32[]{:S(2)}) collective-permute-start(bf16[64,2048]{1,0:T(8,128)(2,1)S(1)} %get-tuple-element.57), channel_id=1, source_target_pairs={{0,1},{1,0},{2,3},{3,2},{4,5},{5,4},{6,7},{7,6},{8,9},{9,8},{10,11... | collective-permute-start | bytes 786440 | tf_op jit(solution)/shard_map/ppermute | solution.py:145
  52.2 1.8 %collective-permute-start.14 = (bf16[48,2048]{1,0:T(8,128)(2,1)S(1)}, bf16[48,2048]{1,0:T(8,128)(2,1)S(1)}, u32[]{:S(2)}, u32[]{:S(2)}) collective-permute-start(bf16[48,2048]{1,0:T(8,128)(2,1)S(1)} %collective-permute-done.13.rows_6), channel_id=1, source_target_pairs={{0,1},{1,0},{2,3},{3,2},{4,5},{5,4},{6,7},{7,6},{8,9},{9,8},{10,11... | collective-permute-start | bytes 589832 | tf_op jit(solution)/shard_map/ppermute | solution.py:145

commit v5 on v4

--- a/solution.py
+++ b/solution.py
@@ -134,9 +134,8 @@
 F32 = jnp.float32
 BF16 = jnp.bfloat16
 GATE_LANES = 128
-SUM_COST = 0
-FACTORS_COST = 0
-OWN_LIMIT = 44
+FACTORS_COST = 8*10**8
+THREE_COST = 2*10**9
 K0_COST = 10 ** 10
 
 
@@ -264,22 +263,19 @@
     return back.astype(BF16), (gate * both).astype(BF16)
 
 
-def own_kernel(up, saved, gate, w_down, w_gate, w_up, back_out, scaled_out):
+def own_kernel(up, saved, gate, beside, w_down, w_gate, w_up, back_out, scaled_out):
+    width, wide = up.shape[1], saved.shape[1]
     back, scaled = through_expert(up[...], saved[...], gate[...], w_down, w_gate, w_up)
+    back_out[:, :width] = back
+    back_out[:, width:] = beside[:, wide:]
+    scaled_out[...] = scaled
+
+
+def two_kernel(up, saved, gate, w_down, w_gate, w_up, back_out, scaled_out):
+    wide = 2 * w_down.shape[0]
+    back, scaled = through_expert(up[...], saved[:, :wide], gate[...], w_down, w_gate, w_up)
     back_out[...] = back
     scaled_out[...] = scaled
-
-
-def both_kernel(near, up_2, saved_2, gate_2, w_down, w_gate, w_up, back_1, back_2, scaled_out):
-    each, width = up_2.shape
-    wide = 2 * w_down.shape[0]
-    up = jnp.concatenate([near[:, :width], up_2[...]], axis=0)
-    gate = jnp.concatenate([near[:, width : width + GATE_LANES], gate_2[...]], axis=0)
-    saved = jnp.concatenate([near[:, width + GATE_LANES :], saved_2[:, :wide]], axis=0)
-    back, scaled_out[...] = through_expert(up, saved, gate, w_down, w_gate, w_up)
-    back_1[...] = back[:each]
-    back_2[:, :width] = back[each:]
-    back_2[:, width:] = saved_2[:, wide:]
 
 
 def factors(gate_pre, up_pre):
@@ -289,21 +285,31 @@
     return up_pre * sig * (1.0 + gate_pre * (1.0 - sig)), silu, silu * up_pre
 
 
-def factors_kernel(saved, by_a, by_b, both):
+def factors_kernel(near, saved, by_a, by_b, both):
     units = by_a.shape[1]
-    by_a[...], by_b[...], both[...] = factors(saved[:, :units], saved[:, units:])
-
-
-def last_rows_kernel(up, by_a, by_b, both, w_down, w_gate, w_up, back_out, scaled_out):
-    width = back_out.shape[1]
-    gate = up[:, width : width + 1].astype(F32)
-    grad_h = lax.dot_general(up[:, :width], w_down[...], LAST, preferred_element_type=F32) * gate
+    low = near.shape[1] - 2 * units
+    gate_pre = jnp.concatenate([near[:, low : low + units], saved[:, :units]], axis=0)
+    up_pre = jnp.concatenate([near[:, low + units :], saved[:, units:]], axis=0)
+    by_a[...], by_b[...], both[...] = factors(gate_pre, up_pre)
+
+
+def odd_kernel(
+    near, up_3, by_a, by_b, both, w_down, w_gate, w_up, back_1, back_6, back_7, scaled_out
+):
+    each, width = back_1.shape
+    gate = [near[:, width : width + 1].astype(F32), up_3[:, width : width + 1].astype(F32)]
+    gate = jnp.concatenate(gate, axis=0)
+    up = jnp.concatenate([near[:, :width], up_3[:, :width]], axis=0)
+    grad_h = lax.dot_general(up, w_down[...], LAST, preferred_element_type=F32) * gate
     grad_a = (grad_h * by_a[...]).astype(BF16)
     grad_b = (grad_h * by_b[...]).astype(BF16)
     scaled_out[...] = (gate * both[...]).astype(BF16)
     back = lax.dot_general(grad_a, w_gate[...], LAST, preferred_element_type=F32)
     back = back + lax.dot_general(grad_b, w_up[...], LAST, preferred_element_type=F32)
-    back_out[...] = back.astype(BF16)
+    back_1[...] = back[:each].astype(BF16)
+    half = each // 2
+    back_6[...] = back[each : each + half].astype(BF16)
+    back_7[...] = back[each + half :].astype(BF16)
 
 
 def down_kernel(scaled_a, scaled_b, scaled_c, up_a, up_b, up_c, up_d, out):
@@ -312,31 +318,34 @@
     out[...] = lax.dot_general(scaled, ups, FIRST, preferred_element_type=F32).astype(BF16)
 
 
-def two_sum_kernel(rows_1, rows_2, part, order_0, order_67):
+def two_sum_kernel(rows_0, rows_2, part, order_1, order_67):
     width = part.shape[1]
-    ids, gates = read_routes(rows_2[:, width:])
-    order = slot_order(ids, gates, (0, 2, 4, 6, 7), rows_2.shape[0] // 2)[0]
-    order_0[...] = jnp.concatenate(order[:2], axis=0).astype(BF16)
+    ids, gates = read_routes(rows_0[:, width:])
+    order = slot_order(ids, gates, (0, 4, 2, 6, 7), rows_2.shape[0] // 2)[0]
+    order_1[...] = jnp.concatenate(order[4:6], axis=0).astype(BF16)
     order_67[...] = jnp.concatenate([order[6], order[8]], axis=0).astype(BF16)
-    order = jnp.concatenate(order[2:6], axis=0).astype(BF16)
-    rows = jnp.concatenate([rows_1[...], rows_2[:, :width]], axis=0)
+    order = jnp.concatenate(order[:4], axis=0).astype(BF16)
+    rows = jnp.concatenate([rows_0[:, :width], rows_2[...]], axis=0)
     part[...] = lax.dot_general(order, rows, FIRST, preferred_element_type=F32)
 
 
-def sum_kernel(order, part, rows_0, own, other):
+def sum_kernel(order, part, rows_1, own, other):
     tokens = own.shape[0]
-    back = lax.dot_general(order[...], rows_0[...], FIRST, preferred_element_type=F32)
+    back = lax.dot_general(order[...], rows_1[...], FIRST, preferred_element_type=F32)
     back = part[...] + back
     own[...] = back[:tokens]
     other[...] = back[tokens:].astype(BF16)
 
 
-def last_kernel(order, own, other, rows_6, rows_7, out):
-    tokens, cap = own.shape[0], rows_6.shape[0] // 2
-    rows = [rows_6[...].astype(F32)[:cap], rows_7[...].astype(F32)[cap:]]
-    rows = jnp.concatenate(rows, axis=0).astype(BF16)
-    back = lax.dot_general(order[...], rows, FIRST, preferred_element_type=F32)
-    out[...] = (own[...] + other[...].astype(F32) + back[:tokens]).astype(BF16)
+def three_sum_kernel(order, rows_6, rows_7, part):
+    tokens = part.shape[0]
+    rows = jnp.concatenate([rows_6[...].astype(F32), rows_7[...].astype(F32)], axis=0)
+    back = lax.dot_general(order[...], rows.astype(BF16), FIRST, preferred_element_type=F32)
+    part[...] = back[:tokens]
+
+
+def last_kernel(own, other, part, out):
+    out[...] = (own[...] + other[...].astype(F32) + part[...]).astype(BF16)
 
 
 def local_call(kernel, outs, args, scratch=(), cost=0, limit=28, **blocks):
@@ -391,18 +400,18 @@
         [pltpu.VMEM((4 * tokens, wide), BF16)],
     )
     near_rows = swapped(near_rows, 2)
-    saved_2 = swapped(saved_2, 4)
+    beside, saved_2 = saved_2, swapped(saved_2, 4)
     weights = (w_down[0], w_gate[0], w_up[0])
     back_0, scaled_0 = local_call(
         own_kernel,
-        [shape(2 * cap, width), shape(2 * cap, units)],
-        (own_rows, saved_0, gate_0, *weights),
+        [shape(2 * cap, width + 2 * tokens), shape(2 * cap, units)],
+        (own_rows, saved_0, gate_0, beside, *weights),
     )
     far_up = after(far_up, back_0)
     far_both = lax.all_gather(
         far_up, "expert", axis=0, tiled=True, axis_index_groups=[[i, i + 1] for i in range(0, 8, 2)]
     )
-    saved_3 = swapped(saved_3, 6)
+    saved_3 = swapped(after(saved_3, far_both), 6)
     two_rows, three_rows, gate_2 = local_call(
         far_kernel,
         [shape(2 * cap, width), shape(2 * cap, width + GATE_LANES), shape(2 * cap, GATE_LANES)],
@@ -410,27 +419,28 @@
     )
     three_rows = swapped(three_rows, 2)
     home_0 = before_section(back_0, 0)
-    near_rows = after(near_rows, home_0)
-    back_1, back_2, scaled_12 = local_call(
-        both_kernel,
-        [shape(2 * cap, width), shape(2 * cap, width + 2 * tokens), shape(4 * cap, units)],
-        (near_rows, two_rows, saved_2, gate_2, *weights),
+    two_rows = after(two_rows, home_0)
+    back_2, scaled_2 = local_call(
+        two_kernel,
+        [shape(2 * cap, width), shape(2 * cap, units)],
+        (two_rows, saved_2, gate_2, *weights),
     )
     saved_3 = after(saved_3, back_2)
     by_saved = local_call(
         factors_kernel,
-        [jax.ShapeDtypeStruct((2 * cap, units), F32)] * 3,
-        (saved_3,),
+        [jax.ShapeDtypeStruct((4 * cap, units), F32)] * 3,
+        (near_rows, saved_3),
         cost=FACTORS_COST,
     )
-    back_3, scaled_3 = local_call(
-        last_rows_kernel,
-        [shape(2 * cap, width), shape(2 * cap, units)],
-        (three_rows, *by_saved, *weights),
+    back_1, back_6, back_7, scaled_13 = local_call(
+        odd_kernel,
+        [shape(2 * cap, width)] + [shape(cap, width)] * 2 + [shape(4 * cap, units)],
+        (near_rows, three_rows, *by_saved, *weights),
     )
     home_2 = before_section(back_2, 4)
     home_1 = before_section(back_1, 2)
-    home_3 = before_section(back_3, 6)
+    rows_6 = before_section(back_6, 6)
+    rows_7 = before_section(back_7, 7)
     parts = 4
 
     def columns(array):
@@ -439,8 +449,8 @@
     def every(array):
         return pl.BlockSpec(array.shape, lambda n: (0, 0))
 
-    scaled = (scaled_0, scaled_12, scaled_3)
-    ups = (own_rows, near_rows, two_rows, three_rows)
+    scaled = (scaled_0, scaled_2, scaled_13)
+    ups = (own_rows, two_rows, near_rows, three_rows)
     (down,) = local_call(
         down_kernel,
         [shape(units, width)],
@@ -450,25 +460,26 @@
         out_specs=[pl.BlockSpec((units, width // parts), lambda n: (0, n))],
     )
     home_2 = after(home_2, down)
-    part, order_0, order_67 = local_call(
+    part, order_1, order_67 = local_call(
         two_sum_kernel,
         [jax.ShapeDtypeStruct((2 * tokens, width), F32)]
         + [shape(2 * cap, 2 * tokens)] * 2,
-        (home_1, home_2),
-        cost=SUM_COST,
-    )
-    home_3 = after(home_3, part)
+        (home_0, home_2),
+    )
+    rows_6 = after(rows_6, part)
     summed, other = local_call(
         sum_kernel,
         [jax.ShapeDtypeStruct((tokens, width), F32), shape(tokens, width)],
-        (order_0, part, home_0),
+        (order_1, part, home_1),
     )
     other = swapped(other, 1)
-    (total,) = local_call(
-        last_kernel,
-        [shape(tokens, width)],
-        (order_67, summed, other, home_3, swapped(home_3, 1)),
-    )
+    (three,) = local_call(
+        three_sum_kernel,
+        [jax.ShapeDtypeStruct((tokens, width), F32)],
+        (order_67, rows_6, rows_7),
+        cost=THREE_COST,
+    )
+    (total,) = local_call(last_kernel, [shape(tokens, width)], (summed, other, three))
     return total[None], down[None]
 
 

time: 55.9 us -> 54.4 us (0.973)
  waiting for transfers between devices: 12.4 us -> 6.41 us
  starting transfers between devices: 21.6 us -> 26.1 us
    ppermute x11 -> x10, waiting for transfers between devices: 8.67 us -> 4.51 us  [swapped(): return lax.ppermute(value, 'expert', [(i, i ^ mask) for i in range(count)])]
    ppermute x4 -> x5, starting transfers between devices: 10.5 us -> 13.6 us  [before_section(): return lax.ppermute(value, ('section', 'expert'), pairs)]
    ppermute x4 -> x5, waiting for transfers between devices: 3.75 us -> 1.9 us  [before_section(): return lax.ppermute(value, ('section', 'expert'), pairs)]
    ppermute x11 -> x10, starting transfers between devices: 11.2 us -> 12.5 us  [swapped(): return lax.ppermute(value, 'expert', [(i, i ^ mask) for i in range(count)])]
    pallas_call x11 -> x12, Pallas kernels: 17.9 us -> 18.1 us  [local_call(): pl.pallas_call(kernel, out_shape=outs, scratch_shapes=scratch, compiler_p...]
  transfers between devices with their start and end apart: 15 -> 15, of which waited for: 7 -> 6; matrix products, arithmetic and copies ran while one was open for 0% -> 0% of each run, Pallas kernels for 31% -> 32%
where the time goes in v5:
time: 54.4 us; the launch traced here: 53.6 us
  starting transfers between devices  26.1 us (48%)
  Pallas kernels  18.1 us (33%)
  waiting for transfers between devices  6.41 us (12%)
  blocking collectives  2.17 us (4%)
  between operations  0.78 us (1%)
    pallas_call x12, Pallas kernels, local_call(): pl.pallas_call(kernel, out_shape=outs, scratch_shapes=scratch, compiler_p...  18.1 us
    ppermute x5, starting transfers between devices, before_section(): return lax.ppermute(value, ('section', 'expert'), pairs)  13.6 us
    ppermute x10, starting transfers between devices, swapped(): return lax.ppermute(value, 'expert', [(i, i ^ mask) for i in range(count)])  12.5 us
    ppermute x10, waiting for transfers between devices, swapped(): return lax.ppermute(value, 'expert', [(i, i ^ mask) for i in range(count)])  4.51 us
    all_gather x1, blocking collectives, on_device_pairs(): lax.all_gather(far_up, 'expert', axis=0, tiled=True, axis_index_groups=[[...  2.17 us
    ppermute x5, waiting for transfers between devices, before_section(): return lax.ppermute(value, ('section', 'expert'), pairs)  1.9 us
  transfers between devices with their start and end apart: 15, of which 6 were waited for; matrix products, arithmetic and copies ran while one was open for 0% of the time, Pallas kernels for 32%

profile of v5, /device:TPU:0, one launch (start us, length us, event | category | flops | bytes accessed | tf_op | source)
XLA Modules:
  0.0 53.6 jit_solution(8104606307964584849)
XLA Ops:
  0.6 0.5 collective-permute-start.2
  1.1 3.7 %collective-permute-start.6 = (bf16[64,2048]{1,0:T(8,128)(2,1)}, bf16[64,2048]{1,0:T(8,128)(2,1)S(1)}, u32[]{:S(2)}, u32[]{:S(2)}) collective-permute-start(bf16[64,2048]{1,0:T(8,128)(2,1)} %bitcast.25), channel_id=1, source_target_pairs={{0,4},{1,5},{2,6},{3,7},{4,0},{5,1},{6,2},{7,3},{8,12},{9,13},{10,... | collective-permute-start | bytes 786440 | tf_op jit(solution)/shard_map/ppermute | solution.py:144
  4.8 0.2 collective-permute-start
  5.0 0.3 collective-permute-start.1
  5.3 0.2 collective-permute-start.3
  5.6 0.7 %collective-permute-done.1.pair_gate = bf16[2,64]{1,0:T(2,128)(2,1)S(1)} collective-permute-done((bf16[2,64]{1,0:T(2,128)(2,1)}, bf16[2,64]{1,0:T(2,128)(2,1)S(1)}, u32[]{:S(2)}, u32[]{:S(2)}) %collective-permute-start.1) | collective-permute-done | bytes 288 | tf_op jit(solution)/shard_map/ppermute | solution.py:144
  6.3 0.0 collective-permute-done.pair_ids
  6.3 0.0 collective-permute-done.2.pair_up
  6.3 1.1 %collective-permute-done.3.pair_act = bf16[64,2,2,768]{3,2,1,0:T(2,128)(2,1)S(1)} collective-permute-done((bf16[64,2,2,768]{3,2,1,0:T(2,128)(2,1)}, bf16[64,2,2,768]{3,2,1,0:T(2,128)(2,1)S(1)}, u32[]{:S(2)}, u32[]{:S(2)}) %collective-permute-start.3) | collective-permute-done | bytes 393248 | tf_op jit(solution)/shard_map/ppermute | solution.py:144
  7.3 0.0 copy-done.3
  7.3 0.0 copy-done.4
  7.3 0.0 copy-done.5
  7.3 0.0 copy-done.6
  7.4 2.3 %shard_map.87 = (bf16[48,2048]{1,0:T(8,128)(2,1)S(1)}, bf16[48,3712]{1,0:T(8,128)(2,1)S(1)}, bf16[48,1536]{1,0:T(8,128)(2,1)S(1)}, bf16[48,1664]{1,0:T(8,128)(2,...) custom-call(bf16[128,128]{1,0:T(8,128)(2,1)S(1)} %shard_map.86.upto, s32[2,64]{1,0:T(2,128)S(1)} %bitcast.28, ...), custom_call_target="tpu_custom_call" | custom-call | tf_op jit(solution)/shard_map/pallas_call | solution.py:356
  9.7 1.6 %collective-permute-start.8 = (bf16[48,3712]{1,0:T(8,128)(2,1)S(1)}, bf16[48,3712]{1,0:T(8,128)(2,1)S(1)}, u32[]{:S(2)}, u32[]{:S(2)}) collective-permute-start(bf16[48,3712]{1,0:T(8,128)(2,1)S(1)} %get-tuple-element.45), channel_id=1, source_target_pairs={{0,2},{1,3},{2,0},{3,1},{4,6},{5,7},{6,4},{7,5},{8,10},{9,11},{10,... | collective-permute-start | bytes 1069064 | tf_op jit(solution)/shard_map/ppermute | solution.py:144
  11.4 0.3 collective-permute-start.5
  11.7 0.0 copy-done
  11.7 0.0 copy-done.1
  11.7 3.3 %shard_map.88 = (bf16[48,2176]{1,0:T(8,128)(2,1)S(1)}, bf16[48,768]{1,0:T(8,128)(2,1)S(1)}) custom-call(bf16[48,2048]{1,0:T(8,128)(2,1)S(1)} %get-tuple-element.33.up.up_a, bf16[48,1536]{1,0:T(8,128)(2,1)S(1)} %get-tuple-element.34.saved, bf16[48,128]{1,0:T(8,128)(2,1)S(1)} %get-tuple-element.35.gate, bf16[48,1664]{1,0:T(8,128)(2,1)S(1)} %get-tuple-element.36.beside, ...), custom_call_target="tpu_custom_call" | custom-call | tf_op jit(solution)/shard_map/pallas_call | solution.py:356
  15.0 2.5 %collective-permute-start.4 = (bf16[48,2176]{1,0:T(8,128)(2,1)S(1)}, bf16[48,2176]{1,0:T(8,128)(2,1)S(1)}, u32[]{:S(2)}, u32[]{:S(2)}) collective-permute-start(bf16[48,2176]{1,0:T(8,128)(2,1)S(1)} %get-tuple-element.37), channel_id=1, source_target_pairs={{0,24},{1,25},{2,26},{3,27},{4,28},{5,29},{6,30},{7,31},{8,0},{9,1... | collective-permute-start | bytes 626696 | tf_op jit(solution)/shard_map/ppermute | solution.py:377
  17.5 0.4 collective-permute-done.6
  17.9 2.2 %all_gather.3.both_up = bf16[128,2048]{1,0:T(8,128)(2,1)S(1)} all-gather(bf16[64,2048]{1,0:T(8,128)(2,1)S(1)} %collective-permute-done.6), channel_id=1, replica_groups={{0,1},{2,3},{4,5},{6,7},{8,9},{10,11},{12,13},{14,15},{16,17},{18,19},{..., dimensions={0}, use_global_device_ids=true | all-gather | bytes 786432 | tf_op jit(solution)/shard_map/all_gather | solution.py:411
  20.1 3.3 %collective-permute-start.10 = (bf16[48,1536]{1,0:T(8,128)(2,1)S(1)}, bf16[48,1536]{1,0:T(8,128)(2,1)S(1)}, u32[]{:S(2)}, u32[]{:S(2)}) collective-permute-start(bf16[48,1536]{1,0:T(8,128)(2,1)S(1)} %get-tuple-element.48), channel_id=1, source_target_pairs={{0,6},{1,7},{2,4},{3,5},{4,2},{5,3},{6,0},{7,1},{8,14},{9,15},{10,... | collective-permute-start | bytes 442376 | tf_op jit(solution)/shard_map/ppermute | solution.py:144
  23.4 1.2 %collective-permute-done.5.saved_2.saved = bf16[48,1664]{1,0:T(8,128)(2,1)S(1)} collective-permute-done((bf16[48,1664]{1,0:T(8,128)(2,1)S(1)}, bf16[48,1664]{1,0:T(8,128)(2,1)S(1)}, u32[]{:S(2)}, u32[]{:S(2)}) %collective-permute-start.5) | collective-permute-done | bytes 159776 | tf_op jit(solution)/shard_map/ppermute | solution.py:144
  24.6 0.5 shard_map.89
  25.1 0.8 %collective-permute-start.9 = (bf16[48,2176]{1,0:T(8,128)(2,1)S(1)}, bf16[48,2176]{1,0:T(8,128)(2,1)S(1)}, u32[]{:S(2)}, u32[]{:S(2)}) collective-permute-start(bf16[48,2176]{1,0:T(8,128)(2,1)S(1)} %get-tuple-element.46), channel_id=1, source_target_pairs={{0,2},{1,3},{2,0},{3,1},{4,6},{5,7},{6,4},{7,5},{8,10},{9,11},{10,... | collective-permute-start | bytes 626696 | tf_op jit(solution)/shard_map/ppermute | solution.py:144
  25.9 0.0 collective-permute-done.4.rows_0
  25.9 3.3 %shard_map.90 = (bf16[48,2048]{1,0:T(8,128)(2,1)S(1)}, bf16[48,768]{1,0:T(8,128)(2,1)S(1)}) custom-call(bf16[48,2048]{1,0:T(8,128)(2,1)S(1)} %get-tuple-element.40.up.up_b, bf16[48,1664]{1,0:T(8,128)(2,1)S(1)} %collective-permute-done.5.saved_2.saved, bf16[48,128]{1,0:T(8,128)(2,1)S(1)} %get-tuple-element.41.gate, bf16[768,2048]{1,0:T(8,128)(2,1)S(1)} %bitcast.14, ...), custom_call_target="tpu_custom_call" | custom-call | tf_op jit(solution)/shard_map/pallas_call | solution.py:356
  29.2 5.3 %collective-permute-start.7 = (bf16[48,2048]{1,0:T(8,128)(2,1)S(1)}, bf16[48,2048]{1,0:T(8,128)(2,1)S(1)}, u32[]{:S(2)}, u32[]{:S(2)}) collective-permute-start(bf16[48,2048]{1,0:T(8,128)(2,1)S(1)} %get-tuple-element.42), channel_id=1, source_target_pairs={{0,28},{1,29},{2,30},{3,31},{4,24},{5,25},{6,26},{7,27},{8,4},{9,5... | collective-permute-start | bytes 589832 | tf_op jit(solution)/shard_map/ppermute | solution.py:377
  34.4 0.0 collective-permute-done.10.saved
  34.4 0.0 collective-permute-done.8.near.up_c
  34.4 0.2 shard_map.91
  34.6 1.2 %collective-permute-done.9.up_3.up_d = bf16[48,2176]{1,0:T(8,128)(2,1)S(1)} collective-permute-done((bf16[48,2176]{1,0:T(8,128)(2,1)S(1)}, bf16[48,2176]{1,0:T(8,128)(2,1)S(1)}, u32[]{:S(2)}, u32[]{:S(2)}) %collective-permute-start.9) | collective-permute-done | bytes 208928 | tf_op jit(solution)/shard_map/ppermute | solution.py:144
  35.8 3.5 %shard_map.92 = (bf16[48,2048]{1,0:T(8,128)(2,1)S(1)}, bf16[24,2048]{1,0:T(8,128)(2,1)S(1)}, bf16[24,2048]{1,0:T(8,128)(2,1)S(1)}, bf16[96,768]{1,0:T(8,128)(2,1)S(1)}) custom-call(bf16[48,3712]{1,0:T(8,128)(2,1)S(1)} %collective-permute-done.8.near.up_c, bf16[48,2176]{1,0:T(8,128)(2,1)S(1)} %collective-permute-done.9.up_3.up_d, ...), custom_call_target="tpu_custom_call" | custom-call | tf_op jit(solution)/shard_map/pallas_call | solution.py:356
  39.2 2.4 %collective-permute-start.11 = (bf16[48,2048]{1,0:T(8,128)(2,1)S(1)}, bf16[48,2048]{1,0:T(8,128)(2,1)S(1)}, u32[]{:S(2)}, u32[]{:S(2)}) collective-permute-start(bf16[48,2048]{1,0:T(8,128)(2,1)S(1)} %get-tuple-element.57), channel_id=1, source_target_pairs={{0,26},{1,27},{2,24},{3,25},{4,30},{5,31},{6,28},{7,29},{8,2},{9,3... | collective-permute-start | bytes 589832 | tf_op jit(solution)/shard_map/ppermute | solution.py:377
  41.6 3.2 %collective-permute-start.13 = (bf16[24,2048]{1,0:T(8,128)(2,1)S(1)}, bf16[24,2048]{1,0:T(8,128)(2,1)S(1)}, u32[]{:S(2)}, u32[]{:S(2)}) collective-permute-start(bf16[24,2048]{1,0:T(8,128)(2,1)S(1)} %get-tuple-element.61), channel_id=1, source_target_pairs={{0,30},{1,31},{2,28},{3,29},{4,26},{5,27},{6,24},{7,25},{8,6},{9,7... | collective-permute-start | bytes 294920 | tf_op jit(solution)/shard_map/ppermute | solution.py:377
  44.8 0.2 collective-permute-start.14
  45.0 3.3 %shard_map.93 = bf16[768,2048]{1,0:T(8,128)(2,1)} custom-call(bf16[48,768]{1,0:T(8,128)(2,1)S(1)} %get-tuple-element.43.scaled_a, bf16[48,768]{1,0:T(8,128)(2,1)S(1)} %get-tuple-element.44.scaled_b, bf16[96,768]{1,0:T(8,128)(2,1)S(1)} %get-tuple-element.53.scaled_c, bf16[48,2048]{1,0:T(8,128)(2,1)S(1)} %get-tuple-element.33.up.up_a, ...), custom_call_target="tpu_custom_call" | custom-call | tf_op jit(solution)/shard_map/pallas_call | solution.py:356
  48.3 0.0 collective-permute-done.7.rows_2
  48.3 0.5 shard_map.94
  48.8 0.0 collective-permute-done.11.rows_1
  48.8 0.3 shard_map.95
  49.1 1.5 %collective-permute-start.12 = (bf16[64,2048]{1,0:T(8,128)(2,1)S(1)}, bf16[64,2048]{1,0:T(8,128)(2,1)S(1)}, u32[]{:S(2)}, u32[]{:S(2)}) collective-permute-start(bf16[64,2048]{1,0:T(8,128)(2,1)S(1)} %get-tuple-element.59), channel_id=1, source_target_pairs={{0,1},{1,0},{2,3},{3,2},{4,5},{5,4},{6,7},{7,6},{8,9},{9,8},{10,11... | collective-permute-start | bytes 786440 | tf_op jit(solution)/shard_map/ppermute | solution.py:144
  50.6 0.0 collective-permute-done.13.rows_6
  50.6 1.9 %collective-permute-done.14.rows_7 = bf16[24,2048]{1,0:T(8,128)(2,1)S(1)} collective-permute-done((bf16[24,2048]{1,0:T(8,128)(2,1)S(1)}, bf16[24,2048]{1,0:T(8,128)(2,1)S(1)}, u32[]{:S(2)}, u32[]{:S(2)}) %collective-permute-start.14) | collective-permute-done | bytes 98336 | tf_op jit(solution)/shard_map/ppermute | solution.py:377
  52.5 0.3 shard_map.96.part
  52.8 0.0 collective-permute-done.12.other
  52.8 0.8 %shard_map.97 = bf16[64,2048]{1,0:T(8,128)(2,1)} custom-call(f32[64,2048]{1,0:T(8,128)S(1)} %get-tuple-element.58.own, bf16[64,2048]{1,0:T(8,128)(2,1)S(1)} %collective-permute-done.12.other, f32[64,2048]{1,0:T(8,128)S(1)} %shard_map.96.part), custom_call_target="tpu_custom_call" | custom-call | tf_op jit(solution)/shard_map/pallas_call | solution.py:356
  (9 shorter events, 0.0 us)
Async XLA Ops:
  0.6 5.7 %collective-permute-start.2 = (bf16[64,2048]{1,0:T(8,128)(2,1)}, bf16[64,2048]{1,0:T(8,128)(2,1)S(1)}, u32[]{:S(2)}, u32[]{:S(2)}) collective-permute-start(bf16[64,2048]{1,0:T(8,128)(2,1)} %bitcast.24), channel_id=1, source_target_pairs={{0,1},{1,0},{2,3},{3,2},{4,5},{5,4},{6,7},{7,6},{8,9},{9,8},{10,11... | collective-permute-start | bytes 786440 | tf_op jit(solution)/shard_map/ppermute | solution.py:144
  1.1 16.8 %collective-permute-start.6 = (bf16[64,2048]{1,0:T(8,128)(2,1)}, bf16[64,2048]{1,0:T(8,128)(2,1)S(1)}, u32[]{:S(2)}, u32[]{:S(2)}) collective-permute-start(bf16[64,2048]{1,0:T(8,128)(2,1)} %bitcast.25), channel_id=1, source_target_pairs={{0,4},{1,5},{2,6},{3,7},{4,0},{5,1},{6,2},{7,3},{8,12},{9,13},{10,... | collective-permute-start | bytes 786440 | tf_op jit(solution)/shard_map/ppermute | solution.py:144
  4.8 1.5 %collective-permute-start = (s32[2,64]{1,0:T(2,128)}, s32[2,64]{1,0:T(2,128)S(1)}, u32[]{:S(2)}, u32[]{:S(2)}) collective-permute-start(s32[2,64]{1,0:T(2,128)} %bitcast.27), channel_id=1, source_target_pairs={{0,1},{1,0},{2,3},{3,2},{4,5},{5,4},{6,7},{7,6},{8,9},{9,8},{10,11... | collective-permute-start | bytes 1544 | tf_op jit(solution)/shard_map/ppermute | solution.py:144
  5.0 1.3 %collective-permute-start.1 = (bf16[2,64]{1,0:T(2,128)(2,1)}, bf16[2,64]{1,0:T(2,128)(2,1)S(1)}, u32[]{:S(2)}, u32[]{:S(2)}) collective-permute-start(bf16[2,64]{1,0:T(2,128)(2,1)} %bitcast.29), channel_id=1, source_target_pairs={{0,1},{1,0},{2,3},{3,2},{4,5},{5,4},{6,7},{7,6},{8,9},{9,8},{10,11... | collective-permute-start | bytes 776 | tf_op jit(solution)/shard_map/ppermute | solution.py:144
  5.3 2.0 %copy-start.3 = (bf16[1,64,2,2,768]{4,3,2,1,0:T(2,128)(2,1)S(1)}, bf16[1,64,2,2,768]{4,3,2,1,0:T(2,128)(2,1)}, u32[]{:S(2)}) copy-start(bf16[1,64,2,2,768]{4,3,2,1,0:T(2,128)(2,1)} %param.8) | copy-start | bytes 1179652
  5.3 2.0 %copy-start.4 = (bf16[1,64,2048]{2,1,0:T(8,128)(2,1)S(1)}, bf16[1,64,2048]{2,1,0:T(8,128)(2,1)}, u32[]{:S(2)}) copy-start(bf16[1,64,2048]{2,1,0:T(8,128)(2,1)} %param.7) | copy-start | bytes 786436
  5.3 2.0 %copy-start.5 = (s32[1,64,2]{1,2,0:T(2,128)S(1)}, s32[1,64,2]{1,2,0:T(2,128)}, u32[]{:S(2)}) copy-start(s32[1,64,2]{1,2,0:T(2,128)} %param.9) | copy-start | bytes 1540
  5.3 2.0 %copy-start.6 = (bf16[1,64,2]{1,2,0:T(2,128)(2,1)S(1)}, bf16[1,64,2]{1,2,0:T(2,128)(2,1)}, u32[]{:S(2)}) copy-start(bf16[1,64,2]{1,2,0:T(2,128)(2,1)} %param.10) | copy-start | bytes 772
  5.3 2.0 %collective-permute-start.3 = (bf16[64,2,2,768]{3,2,1,0:T(2,128)(2,1)}, bf16[64,2,2,768]{3,2,1,0:T(2,128)(2,1)S(1)}, u32[]{:S(2)}, u32[]{:S(2)}) collective-permute-start(bf16[64,2,2,768]{3,2,1,0:T(2,128)(2,1)} %bitcast.22), channel_id=1, source_target_pairs={{0,1},{1,0},{2,3},{3,2},{4,5},{5,4},{6,7},{7,6},{8,9},{9,8},{10,11... | collective-permute-start | bytes 1179656 | tf_op jit(solution)/shard_map/ppermute | solution.py:144
  5.6 6.1 %copy-start = (bf16[1,768,2048]{2,1,0:T(8,128)(2,1)S(1)}, bf16[1,768,2048]{2,1,0:T(8,128)(2,1)}, u32[]{:S(2)}) copy-start(bf16[1,768,2048]{2,1,0:T(8,128)(2,1)} %param.13) | copy-start | bytes 9437188
  5.6 6.1 %copy-start.1 = (bf16[1,2048,768]{2,1,0:T(8,128)(2,1)S(1)}, bf16[1,2048,768]{2,1,0:T(8,128)(2,1)}, u32[]{:S(2)}) copy-start(bf16[1,2048,768]{2,1,0:T(8,128)(2,1)} %param.11) | copy-start | bytes 9437188
  5.6 6.1 %copy-start.2 = (bf16[1,2048,768]{2,1,0:T(8,128)(2,1)S(1)}, bf16[1,2048,768]{2,1,0:T(8,128)(2,1)}, u32[]{:S(2)}) copy-start(bf16[1,2048,768]{2,1,0:T(8,128)(2,1)} %param.12) | copy-start | bytes 9437188
  9.7 24.7 %collective-permute-start.8 = (bf16[48,3712]{1,0:T(8,128)(2,1)S(1)}, bf16[48,3712]{1,0:T(8,128)(2,1)S(1)}, u32[]{:S(2)}, u32[]{:S(2)}) collective-permute-start(bf16[48,3712]{1,0:T(8,128)(2,1)S(1)} %get-tuple-element.45), channel_id=1, source_target_pairs={{0,2},{1,3},{2,0},{3,1},{4,6},{5,7},{6,4},{7,5},{8,10},{9,11},{10,... | collective-permute-start | bytes 1069064 | tf_op jit(solution)/shard_map/ppermute | solution.py:144
  11.4 13.2 %collective-permute-start.5 = (bf16[48,1664]{1,0:T(8,128)(2,1)S(1)}, bf16[48,1664]{1,0:T(8,128)(2,1)S(1)}, u32[]{:S(2)}, u32[]{:S(2)}) collective-permute-start(bf16[48,1664]{1,0:T(8,128)(2,1)S(1)} %get-tuple-element.36.beside), channel_id=1, source_target_pairs={{0,4},{1,5},{2,6},{3,7},{4,0},{5,1},{6,2},{7,3},{8,12},{9,13},{10,... | collective-permute-start | bytes 479240 | tf_op jit(solution)/shard_map/ppermute | solution.py:144
  15.0 10.9 %collective-permute-start.4 = (bf16[48,2176]{1,0:T(8,128)(2,1)S(1)}, bf16[48,2176]{1,0:T(8,128)(2,1)S(1)}, u32[]{:S(2)}, u32[]{:S(2)}) collective-permute-start(bf16[48,2176]{1,0:T(8,128)(2,1)S(1)} %get-tuple-element.37), channel_id=1, source_target_pairs={{0,24},{1,25},{2,26},{3,27},{4,28},{5,29},{6,30},{7,31},{8,0},{9,1... | collective-permute-start | bytes 626696 | tf_op jit(solution)/shard_map/ppermute | solution.py:377
  20.1 14.4 %collective-permute-start.10 = (bf16[48,1536]{1,0:T(8,128)(2,1)S(1)}, bf16[48,1536]{1,0:T(8,128)(2,1)S(1)}, u32[]{:S(2)}, u32[]{:S(2)}) collective-permute-start(bf16[48,1536]{1,0:T(8,128)(2,1)S(1)} %get-tuple-element.48), channel_id=1, source_target_pairs={{0,6},{1,7},{2,4},{3,5},{4,2},{5,3},{6,0},{7,1},{8,14},{9,15},{10,... | collective-permute-start | bytes 442376 | tf_op jit(solution)/shard_map/ppermute | solution.py:144
  25.1 10.7 %collective-permute-start.9 = (bf16[48,2176]{1,0:T(8,128)(2,1)S(1)}, bf16[48,2176]{1,0:T(8,128)(2,1)S(1)}, u32[]{:S(2)}, u32[]{:S(2)}) collective-permute-start(bf16[48,2176]{1,0:T(8,128)(2,1)S(1)} %get-tuple-element.46), channel_id=1, source_target_pairs={{0,2},{1,3},{2,0},{3,1},{4,6},{5,7},{6,4},{7,5},{8,10},{9,11},{10,... | collective-permute-start | bytes 626696 | tf_op jit(solution)/shard_map/ppermute | solution.py:144
  29.2 19.1 %collective-permute-start.7 = (bf16[48,2048]{1,0:T(8,128)(2,1)S(1)}, bf16[48,2048]{1,0:T(8,128)(2,1)S(1)}, u32[]{:S(2)}, u32[]{:S(2)}) collective-permute-start(bf16[48,2048]{1,0:T(8,128)(2,1)S(1)} %get-tuple-element.42), channel_id=1, source_target_pairs={{0,28},{1,29},{2,30},{3,31},{4,24},{5,25},{6,26},{7,27},{8,4},{9,5... | collective-permute-start | bytes 589832 | tf_op jit(solution)/shard_map/ppermute | solution.py:377
  39.2 9.6 %collective-permute-start.11 = (bf16[48,2048]{1,0:T(8,128)(2,1)S(1)}, bf16[48,2048]{1,0:T(8,128)(2,1)S(1)}, u32[]{:S(2)}, u32[]{:S(2)}) collective-permute-start(bf16[48,2048]{1,0:T(8,128)(2,1)S(1)} %get-tuple-element.57), channel_id=1, source_target_pairs={{0,26},{1,27},{2,24},{3,25},{4,30},{5,31},{6,28},{7,29},{8,2},{9,3... | collective-permute-start | bytes 589832 | tf_op jit(solution)/shard_map/ppermute | solution.py:377
  41.6 9.0 %collective-permute-start.13 = (bf16[24,2048]{1,0:T(8,128)(2,1)S(1)}, bf16[24,2048]{1,0:T(8,128)(2,1)S(1)}, u32[]{:S(2)}, u32[]{:S(2)}) collective-permute-start(bf16[24,2048]{1,0:T(8,128)(2,1)S(1)} %get-tuple-element.61), channel_id=1, source_target_pairs={{0,30},{1,31},{2,28},{3,29},{4,26},{5,27},{6,24},{7,25},{8,6},{9,7... | collective-permute-start | bytes 294920 | tf_op jit(solution)/shard_map/ppermute | solution.py:377
  44.8 7.7 %collective-permute-start.14 = (bf16[24,2048]{1,0:T(8,128)(2,1)S(1)}, bf16[24,2048]{1,0:T(8,128)(2,1)S(1)}, u32[]{:S(2)}, u32[]{:S(2)}) collective-permute-start(bf16[24,2048]{1,0:T(8,128)(2,1)S(1)} %get-tuple-element.63), channel_id=1, source_target_pairs={{0,31},{1,30},{2,29},{3,28},{4,27},{5,26},{6,25},{7,24},{8,7},{9,6... | collective-permute-start | bytes 294920 | tf_op jit(solution)/shard_map/ppermute | solution.py:377
  49.1 3.7 %collective-permute-start.12 = (bf16[64,2048]{1,0:T(8,128)(2,1)S(1)}, bf16[64,2048]{1,0:T(8,128)(2,1)S(1)}, u32[]{:S(2)}, u32[]{:S(2)}) collective-permute-start(bf16[64,2048]{1,0:T(8,128)(2,1)S(1)} %get-tuple-element.59), channel_id=1, source_target_pairs={{0,1},{1,0},{2,3},{3,2},{4,5},{5,4},{6,7},{7,6},{8,9},{9,8},{10,11... | collective-permute-start | bytes 786440 | tf_op jit(solution)/shard_map/ppermute | solution.py:144

commit v6 on v5

--- a/solution.py
+++ b/solution.py
@@ -344,8 +344,18 @@
     part[...] = back[:tokens]
 
 
-def last_kernel(own, other, part, out):
-    out[...] = (own[...] + other[...].astype(F32) + part[...]).astype(BF16)
+def last_kernel(own, other, part, out, done, sent):
+    pieces = 4
+    each = own.shape[1] // pieces
+    copies = []
+    for n in range(pieces):
+        lanes = pl.ds(n * each, each)
+        total = own[:, lanes] + other[:, lanes].astype(F32) + part[:, lanes]
+        done[:, lanes] = total.astype(BF16)
+        copies.append(pltpu.make_async_copy(done.at[:, lanes], out.at[:, lanes], sent.at[n]))
+        copies[-1].start()
+    for copy in copies:
+        copy.wait()
 
 
 def local_call(kernel, outs, args, scratch=(), cost=0, limit=28, **blocks):
@@ -479,7 +489,15 @@
         (order_67, rows_6, rows_7),
         cost=THREE_COST,
     )
-    (total,) = local_call(last_kernel, [shape(tokens, width)], (summed, other, three))
+    vmem = pl.BlockSpec(memory_space=pltpu.VMEM)
+    (total,) = local_call(
+        last_kernel,
+        [shape(tokens, width)],
+        (summed, other, three),
+        [pltpu.VMEM((tokens, width), BF16), pltpu.SemaphoreType.DMA((4,))],
+        in_specs=[vmem] * 3,
+        out_specs=[pl.BlockSpec(memory_space=pltpu.HBM)],
+    )
     return total[None], down[None]
 
 

time: 54.4 us -> 54.4 us (level)
  no operation moved by 1% of the time
where the time goes in v6:
time: 54.4 us; the launch traced here: 53.6 us
  starting transfers between devices  26.1 us (48%)
  Pallas kernels  18.1 us (33%)
  waiting for transfers between devices  6.41 us (12%)
  blocking collectives  2.17 us (4%)
  between operations  0.78 us (1%)
    pallas_call x12, Pallas kernels, local_call(): pl.pallas_call(kernel, out_shape=outs, scratch_shapes=scratch, compiler_p...  18.1 us
    ppermute x5, starting transfers between devices, before_section(): return lax.ppermute(value, ('section', 'expert'), pairs)  13.6 us
    ppermute x10, starting transfers between devices, swapped(): return lax.ppermute(value, 'expert', [(i, i ^ mask) for i in range(count)])  12.5 us
    ppermute x10, waiting for transfers between devices, swapped(): return lax.ppermute(value, 'expert', [(i, i ^ mask) for i in range(count)])  4.51 us
    all_gather x1, blocking collectives, on_device_pairs(): lax.all_gather(far_up, 'expert', axis=0, tiled=True, axis_index_groups=[[...  2.17 us
    ppermute x5, waiting for transfers between devices, before_section(): return lax.ppermute(value, ('section', 'expert'), pairs)  1.9 us
  transfers between devices with their start and end apart: 15, of which 6 were waited for; matrix products, arithmetic and copies ran while one was open for 0% of the time, Pallas kernels for 32%

profile of v6, /device:TPU:0, one launch (start us, length us, event | category | flops | bytes accessed | tf_op | source)
XLA Modules:
  0.0 53.6 jit_solution(14003812760788220143)
XLA Ops:
  0.6 0.5 collective-permute-start.2
  1.1 3.7 %collective-permute-start.6 = (bf16[64,2048]{1,0:T(8,128)(2,1)}, bf16[64,2048]{1,0:T(8,128)(2,1)S(1)}, u32[]{:S(2)}, u32[]{:S(2)}) collective-permute-start(bf16[64,2048]{1,0:T(8,128)(2,1)} %bitcast.25), channel_id=1, source_target_pairs={{0,4},{1,5},{2,6},{3,7},{4,0},{5,1},{6,2},{7,3},{8,12},{9,13},{10,... | collective-permute-start | bytes 786440 | tf_op jit(solution)/shard_map/ppermute | solution.py:144
  4.8 0.2 collective-permute-start
  5.0 0.3 collective-permute-start.1
  5.3 0.2 collective-permute-start.3
  5.6 0.7 %collective-permute-done.1.pair_gate = bf16[2,64]{1,0:T(2,128)(2,1)S(1)} collective-permute-done((bf16[2,64]{1,0:T(2,128)(2,1)}, bf16[2,64]{1,0:T(2,128)(2,1)S(1)}, u32[]{:S(2)}, u32[]{:S(2)}) %collective-permute-start.1) | collective-permute-done | bytes 288 | tf_op jit(solution)/shard_map/ppermute | solution.py:144
  6.3 0.0 collective-permute-done.pair_ids
  6.3 0.0 collective-permute-done.2.pair_up
  6.3 1.1 %collective-permute-done.3.pair_act = bf16[64,2,2,768]{3,2,1,0:T(2,128)(2,1)S(1)} collective-permute-done((bf16[64,2,2,768]{3,2,1,0:T(2,128)(2,1)}, bf16[64,2,2,768]{3,2,1,0:T(2,128)(2,1)S(1)}, u32[]{:S(2)}, u32[]{:S(2)}) %collective-permute-start.3) | collective-permute-done | bytes 393248 | tf_op jit(solution)/shard_map/ppermute | solution.py:144
  7.3 0.0 copy-done.3
  7.3 0.0 copy-done.4
  7.3 0.0 copy-done.5
  7.3 0.0 copy-done.6
  7.4 2.3 %shard_map.87 = (bf16[48,2048]{1,0:T(8,128)(2,1)S(1)}, bf16[48,3712]{1,0:T(8,128)(2,1)S(1)}, bf16[48,1536]{1,0:T(8,128)(2,1)S(1)}, bf16[48,1664]{1,0:T(8,128)(2,...) custom-call(bf16[128,128]{1,0:T(8,128)(2,1)S(1)} %shard_map.86.upto, s32[2,64]{1,0:T(2,128)S(1)} %bitcast.28, ...), custom_call_target="tpu_custom_call" | custom-call | tf_op jit(solution)/shard_map/pallas_call | solution.py:366
  9.7 1.6 %collective-permute-start.8 = (bf16[48,3712]{1,0:T(8,128)(2,1)S(1)}, bf16[48,3712]{1,0:T(8,128)(2,1)S(1)}, u32[]{:S(2)}, u32[]{:S(2)}) collective-permute-start(bf16[48,3712]{1,0:T(8,128)(2,1)S(1)} %get-tuple-element.45), channel_id=1, source_target_pairs={{0,2},{1,3},{2,0},{3,1},{4,6},{5,7},{6,4},{7,5},{8,10},{9,11},{10,... | collective-permute-start | bytes 1069064 | tf_op jit(solution)/shard_map/ppermute | solution.py:144
  11.4 0.3 collective-permute-start.5
  11.7 0.0 copy-done
  11.7 0.0 copy-done.1
  11.7 3.3 %shard_map.88 = (bf16[48,2176]{1,0:T(8,128)(2,1)S(1)}, bf16[48,768]{1,0:T(8,128)(2,1)S(1)}) custom-call(bf16[48,2048]{1,0:T(8,128)(2,1)S(1)} %get-tuple-element.33.up.up_a, bf16[48,1536]{1,0:T(8,128)(2,1)S(1)} %get-tuple-element.34.saved, bf16[48,128]{1,0:T(8,128)(2,1)S(1)} %get-tuple-element.35.gate, bf16[48,1664]{1,0:T(8,128)(2,1)S(1)} %get-tuple-element.36.beside, ...), custom_call_target="tpu_custom_call" | custom-call | tf_op jit(solution)/shard_map/pallas_call | solution.py:366
  15.0 2.5 %collective-permute-start.4 = (bf16[48,2176]{1,0:T(8,128)(2,1)S(1)}, bf16[48,2176]{1,0:T(8,128)(2,1)S(1)}, u32[]{:S(2)}, u32[]{:S(2)}) collective-permute-start(bf16[48,2176]{1,0:T(8,128)(2,1)S(1)} %get-tuple-element.37), channel_id=1, source_target_pairs={{0,24},{1,25},{2,26},{3,27},{4,28},{5,29},{6,30},{7,31},{8,0},{9,1... | collective-permute-start | bytes 626696 | tf_op jit(solution)/shard_map/ppermute | solution.py:387
  17.5 0.4 collective-permute-done.6
  17.9 2.2 %all_gather.3.both_up = bf16[128,2048]{1,0:T(8,128)(2,1)S(1)} all-gather(bf16[64,2048]{1,0:T(8,128)(2,1)S(1)} %collective-permute-done.6), channel_id=1, replica_groups={{0,1},{2,3},{4,5},{6,7},{8,9},{10,11},{12,13},{14,15},{16,17},{18,19},{..., dimensions={0}, use_global_device_ids=true | all-gather | bytes 786432 | tf_op jit(solution)/shard_map/all_gather | solution.py:421
  20.1 3.3 %collective-permute-start.10 = (bf16[48,1536]{1,0:T(8,128)(2,1)S(1)}, bf16[48,1536]{1,0:T(8,128)(2,1)S(1)}, u32[]{:S(2)}, u32[]{:S(2)}) collective-permute-start(bf16[48,1536]{1,0:T(8,128)(2,1)S(1)} %get-tuple-element.48), channel_id=1, source_target_pairs={{0,6},{1,7},{2,4},{3,5},{4,2},{5,3},{6,0},{7,1},{8,14},{9,15},{10,... | collective-permute-start | bytes 442376 | tf_op jit(solution)/shard_map/ppermute | solution.py:144
  23.4 1.2 %collective-permute-done.5.saved_2.saved = bf16[48,1664]{1,0:T(8,128)(2,1)S(1)} collective-permute-done((bf16[48,1664]{1,0:T(8,128)(2,1)S(1)}, bf16[48,1664]{1,0:T(8,128)(2,1)S(1)}, u32[]{:S(2)}, u32[]{:S(2)}) %collective-permute-start.5) | collective-permute-done | bytes 159776 | tf_op jit(solution)/shard_map/ppermute | solution.py:144
  24.6 0.5 shard_map.89
  25.1 0.8 %collective-permute-start.9 = (bf16[48,2176]{1,0:T(8,128)(2,1)S(1)}, bf16[48,2176]{1,0:T(8,128)(2,1)S(1)}, u32[]{:S(2)}, u32[]{:S(2)}) collective-permute-start(bf16[48,2176]{1,0:T(8,128)(2,1)S(1)} %get-tuple-element.46), channel_id=1, source_target_pairs={{0,2},{1,3},{2,0},{3,1},{4,6},{5,7},{6,4},{7,5},{8,10},{9,11},{10,... | collective-permute-start | bytes 626696 | tf_op jit(solution)/shard_map/ppermute | solution.py:144
  25.9 0.0 collective-permute-done.4.rows_0
  25.9 3.3 %shard_map.90 = (bf16[48,2048]{1,0:T(8,128)(2,1)S(1)}, bf16[48,768]{1,0:T(8,128)(2,1)S(1)}) custom-call(bf16[48,2048]{1,0:T(8,128)(2,1)S(1)} %get-tuple-element.40.up.up_b, bf16[48,1664]{1,0:T(8,128)(2,1)S(1)} %collective-permute-done.5.saved_2.saved, bf16[48,128]{1,0:T(8,128)(2,1)S(1)} %get-tuple-element.41.gate, bf16[768,2048]{1,0:T(8,128)(2,1)S(1)} %bitcast.14, ...), custom_call_target="tpu_custom_call" | custom-call | tf_op jit(solution)/shard_map/pallas_call | solution.py:366
  29.2 5.3 %collective-permute-start.7 = (bf16[48,2048]{1,0:T(8,128)(2,1)S(1)}, bf16[48,2048]{1,0:T(8,128)(2,1)S(1)}, u32[]{:S(2)}, u32[]{:S(2)}) collective-permute-start(bf16[48,2048]{1,0:T(8,128)(2,1)S(1)} %get-tuple-element.42), channel_id=1, source_target_pairs={{0,28},{1,29},{2,30},{3,31},{4,24},{5,25},{6,26},{7,27},{8,4},{9,5... | collective-permute-start | bytes 589832 | tf_op jit(solution)/shard_map/ppermute | solution.py:387
  34.4 0.0 collective-permute-done.10.saved
  34.4 0.0 collective-permute-done.8.near.up_c
  34.4 0.2 shard_map.91
  34.6 1.2 %collective-permute-done.9.up_3.up_d = bf16[48,2176]{1,0:T(8,128)(2,1)S(1)} collective-permute-done((bf16[48,2176]{1,0:T(8,128)(2,1)S(1)}, bf16[48,2176]{1,0:T(8,128)(2,1)S(1)}, u32[]{:S(2)}, u32[]{:S(2)}) %collective-permute-start.9) | collective-permute-done | bytes 208928 | tf_op jit(solution)/shard_map/ppermute | solution.py:144
  35.8 3.5 %shard_map.92 = (bf16[48,2048]{1,0:T(8,128)(2,1)S(1)}, bf16[24,2048]{1,0:T(8,128)(2,1)S(1)}, bf16[24,2048]{1,0:T(8,128)(2,1)S(1)}, bf16[96,768]{1,0:T(8,128)(2,1)S(1)}) custom-call(bf16[48,3712]{1,0:T(8,128)(2,1)S(1)} %collective-permute-done.8.near.up_c, bf16[48,2176]{1,0:T(8,128)(2,1)S(1)} %collective-permute-done.9.up_3.up_d, ...), custom_call_target="tpu_custom_call" | custom-call | tf_op jit(solution)/shard_map/pallas_call | solution.py:366
  39.2 2.4 %collective-permute-start.11 = (bf16[48,2048]{1,0:T(8,128)(2,1)S(1)}, bf16[48,2048]{1,0:T(8,128)(2,1)S(1)}, u32[]{:S(2)}, u32[]{:S(2)}) collective-permute-start(bf16[48,2048]{1,0:T(8,128)(2,1)S(1)} %get-tuple-element.57), channel_id=1, source_target_pairs={{0,26},{1,27},{2,24},{3,25},{4,30},{5,31},{6,28},{7,29},{8,2},{9,3... | collective-permute-start | bytes 589832 | tf_op jit(solution)/shard_map/ppermute | solution.py:387
  41.6 3.2 %collective-permute-start.13 = (bf16[24,2048]{1,0:T(8,128)(2,1)S(1)}, bf16[24,2048]{1,0:T(8,128)(2,1)S(1)}, u32[]{:S(2)}, u32[]{:S(2)}) collective-permute-start(bf16[24,2048]{1,0:T(8,128)(2,1)S(1)} %get-tuple-element.61), channel_id=1, source_target_pairs={{0,30},{1,31},{2,28},{3,29},{4,26},{5,27},{6,24},{7,25},{8,6},{9,7... | collective-permute-start | bytes 294920 | tf_op jit(solution)/shard_map/ppermute | solution.py:387
  44.8 0.2 collective-permute-start.14
  45.0 3.3 %shard_map.93 = bf16[768,2048]{1,0:T(8,128)(2,1)} custom-call(bf16[48,768]{1,0:T(8,128)(2,1)S(1)} %get-tuple-element.43.scaled_a, bf16[48,768]{1,0:T(8,128)(2,1)S(1)} %get-tuple-element.44.scaled_b, bf16[96,768]{1,0:T(8,128)(2,1)S(1)} %get-tuple-element.53.scaled_c, bf16[48,2048]{1,0:T(8,128)(2,1)S(1)} %get-tuple-element.33.up.up_a, ...), custom_call_target="tpu_custom_call" | custom-call | tf_op jit(solution)/shard_map/pallas_call | solution.py:366
  48.3 0.0 collective-permute-done.7.rows_2
  48.3 0.5 shard_map.94
  48.8 0.0 collective-permute-done.11.rows_1
  48.8 0.3 shard_map.95
  49.1 1.5 %collective-permute-start.12 = (bf16[64,2048]{1,0:T(8,128)(2,1)S(1)}, bf16[64,2048]{1,0:T(8,128)(2,1)S(1)}, u32[]{:S(2)}, u32[]{:S(2)}) collective-permute-start(bf16[64,2048]{1,0:T(8,128)(2,1)S(1)} %get-tuple-element.59), channel_id=1, source_target_pairs={{0,1},{1,0},{2,3},{3,2},{4,5},{5,4},{6,7},{7,6},{8,9},{9,8},{10,11... | collective-permute-start | bytes 786440 | tf_op jit(solution)/shard_map/ppermute | solution.py:144
  50.6 0.0 collective-permute-done.13.rows_6
  50.6 1.9 %collective-permute-done.14.rows_7 = bf16[24,2048]{1,0:T(8,128)(2,1)S(1)} collective-permute-done((bf16[24,2048]{1,0:T(8,128)(2,1)S(1)}, bf16[24,2048]{1,0:T(8,128)(2,1)S(1)}, u32[]{:S(2)}, u32[]{:S(2)}) %collective-permute-start.14) | collective-permute-done | bytes 98336 | tf_op jit(solution)/shard_map/ppermute | solution.py:387
  52.5 0.3 shard_map.96.part
  52.8 0.0 collective-permute-done.12.other
  52.8 0.7 %shard_map.97 = bf16[64,2048]{1,0:T(8,128)(2,1)} custom-call(f32[64,2048]{1,0:T(8,128)S(1)} %get-tuple-element.58.own, bf16[64,2048]{1,0:T(8,128)(2,1)S(1)} %collective-permute-done.12.other, f32[64,2048]{1,0:T(8,128)S(1)} %shard_map.96.part), custom_call_target="tpu_custom_call" | custom-call | tf_op jit(solution)/shard_map/pallas_call | solution.py:366
  (9 shorter events, 0.0 us)
Async XLA Ops:
  0.6 5.7 %collective-permute-start.2 = (bf16[64,2048]{1,0:T(8,128)(2,1)}, bf16[64,2048]{1,0:T(8,128)(2,1)S(1)}, u32[]{:S(2)}, u32[]{:S(2)}) collective-permute-start(bf16[64,2048]{1,0:T(8,128)(2,1)} %bitcast.24), channel_id=1, source_target_pairs={{0,1},{1,0},{2,3},{3,2},{4,5},{5,4},{6,7},{7,6},{8,9},{9,8},{10,11... | collective-permute-start | bytes 786440 | tf_op jit(solution)/shard_map/ppermute | solution.py:144
  1.1 16.8 %collective-permute-start.6 = (bf16[64,2048]{1,0:T(8,128)(2,1)}, bf16[64,2048]{1,0:T(8,128)(2,1)S(1)}, u32[]{:S(2)}, u32[]{:S(2)}) collective-permute-start(bf16[64,2048]{1,0:T(8,128)(2,1)} %bitcast.25), channel_id=1, source_target_pairs={{0,4},{1,5},{2,6},{3,7},{4,0},{5,1},{6,2},{7,3},{8,12},{9,13},{10,... | collective-permute-start | bytes 786440 | tf_op jit(solution)/shard_map/ppermute | solution.py:144
  4.8 1.5 %collective-permute-start = (s32[2,64]{1,0:T(2,128)}, s32[2,64]{1,0:T(2,128)S(1)}, u32[]{:S(2)}, u32[]{:S(2)}) collective-permute-start(s32[2,64]{1,0:T(2,128)} %bitcast.27), channel_id=1, source_target_pairs={{0,1},{1,0},{2,3},{3,2},{4,5},{5,4},{6,7},{7,6},{8,9},{9,8},{10,11... | collective-permute-start | bytes 1544 | tf_op jit(solution)/shard_map/ppermute | solution.py:144
  5.0 1.3 %collective-permute-start.1 = (bf16[2,64]{1,0:T(2,128)(2,1)}, bf16[2,64]{1,0:T(2,128)(2,1)S(1)}, u32[]{:S(2)}, u32[]{:S(2)}) collective-permute-start(bf16[2,64]{1,0:T(2,128)(2,1)} %bitcast.29), channel_id=1, source_target_pairs={{0,1},{1,0},{2,3},{3,2},{4,5},{5,4},{6,7},{7,6},{8,9},{9,8},{10,11... | collective-permute-start | bytes 776 | tf_op jit(solution)/shard_map/ppermute | solution.py:144
  5.3 2.0 %copy-start.3 = (bf16[1,64,2,2,768]{4,3,2,1,0:T(2,128)(2,1)S(1)}, bf16[1,64,2,2,768]{4,3,2,1,0:T(2,128)(2,1)}, u32[]{:S(2)}) copy-start(bf16[1,64,2,2,768]{4,3,2,1,0:T(2,128)(2,1)} %param.8) | copy-start | bytes 1179652
  5.3 2.0 %copy-start.4 = (bf16[1,64,2048]{2,1,0:T(8,128)(2,1)S(1)}, bf16[1,64,2048]{2,1,0:T(8,128)(2,1)}, u32[]{:S(2)}) copy-start(bf16[1,64,2048]{2,1,0:T(8,128)(2,1)} %param.7) | copy-start | bytes 786436
  5.3 2.0 %copy-start.5 = (s32[1,64,2]{1,2,0:T(2,128)S(1)}, s32[1,64,2]{1,2,0:T(2,128)}, u32[]{:S(2)}) copy-start(s32[1,64,2]{1,2,0:T(2,128)} %param.9) | copy-start | bytes 1540
  5.3 2.0 %copy-start.6 = (bf16[1,64,2]{1,2,0:T(2,128)(2,1)S(1)}, bf16[1,64,2]{1,2,0:T(2,128)(2,1)}, u32[]{:S(2)}) copy-start(bf16[1,64,2]{1,2,0:T(2,128)(2,1)} %param.10) | copy-start | bytes 772
  5.3 2.0 %collective-permute-start.3 = (bf16[64,2,2,768]{3,2,1,0:T(2,128)(2,1)}, bf16[64,2,2,768]{3,2,1,0:T(2,128)(2,1)S(1)}, u32[]{:S(2)}, u32[]{:S(2)}) collective-permute-start(bf16[64,2,2,768]{3,2,1,0:T(2,128)(2,1)} %bitcast.22), channel_id=1, source_target_pairs={{0,1},{1,0},{2,3},{3,2},{4,5},{5,4},{6,7},{7,6},{8,9},{9,8},{10,11... | collective-permute-start | bytes 1179656 | tf_op jit(solution)/shard_map/ppermute | solution.py:144
  5.6 6.1 %copy-start = (bf16[1,768,2048]{2,1,0:T(8,128)(2,1)S(1)}, bf16[1,768,2048]{2,1,0:T(8,128)(2,1)}, u32[]{:S(2)}) copy-start(bf16[1,768,2048]{2,1,0:T(8,128)(2,1)} %param.13) | copy-start | bytes 9437188
  5.6 6.1 %copy-start.1 = (bf16[1,2048,768]{2,1,0:T(8,128)(2,1)S(1)}, bf16[1,2048,768]{2,1,0:T(8,128)(2,1)}, u32[]{:S(2)}) copy-start(bf16[1,2048,768]{2,1,0:T(8,128)(2,1)} %param.11) | copy-start | bytes 9437188
  5.6 6.1 %copy-start.2 = (bf16[1,2048,768]{2,1,0:T(8,128)(2,1)S(1)}, bf16[1,2048,768]{2,1,0:T(8,128)(2,1)}, u32[]{:S(2)}) copy-start(bf16[1,2048,768]{2,1,0:T(8,128)(2,1)} %param.12) | copy-start | bytes 9437188
  9.7 24.7 %collective-permute-start.8 = (bf16[48,3712]{1,0:T(8,128)(2,1)S(1)}, bf16[48,3712]{1,0:T(8,128)(2,1)S(1)}, u32[]{:S(2)}, u32[]{:S(2)}) collective-permute-start(bf16[48,3712]{1,0:T(8,128)(2,1)S(1)} %get-tuple-element.45), channel_id=1, source_target_pairs={{0,2},{1,3},{2,0},{3,1},{4,6},{5,7},{6,4},{7,5},{8,10},{9,11},{10,... | collective-permute-start | bytes 1069064 | tf_op jit(solution)/shard_map/ppermute | solution.py:144
  11.4 13.2 %collective-permute-start.5 = (bf16[48,1664]{1,0:T(8,128)(2,1)S(1)}, bf16[48,1664]{1,0:T(8,128)(2,1)S(1)}, u32[]{:S(2)}, u32[]{:S(2)}) collective-permute-start(bf16[48,1664]{1,0:T(8,128)(2,1)S(1)} %get-tuple-element.36.beside), channel_id=1, source_target_pairs={{0,4},{1,5},{2,6},{3,7},{4,0},{5,1},{6,2},{7,3},{8,12},{9,13},{10,... | collective-permute-start | bytes 479240 | tf_op jit(solution)/shard_map/ppermute | solution.py:144
  15.0 10.9 %collective-permute-start.4 = (bf16[48,2176]{1,0:T(8,128)(2,1)S(1)}, bf16[48,2176]{1,0:T(8,128)(2,1)S(1)}, u32[]{:S(2)}, u32[]{:S(2)}) collective-permute-start(bf16[48,2176]{1,0:T(8,128)(2,1)S(1)} %get-tuple-element.37), channel_id=1, source_target_pairs={{0,24},{1,25},{2,26},{3,27},{4,28},{5,29},{6,30},{7,31},{8,0},{9,1... | collective-permute-start | bytes 626696 | tf_op jit(solution)/shard_map/ppermute | solution.py:387
  20.1 14.4 %collective-permute-start.10 = (bf16[48,1536]{1,0:T(8,128)(2,1)S(1)}, bf16[48,1536]{1,0:T(8,128)(2,1)S(1)}, u32[]{:S(2)}, u32[]{:S(2)}) collective-permute-start(bf16[48,1536]{1,0:T(8,128)(2,1)S(1)} %get-tuple-element.48), channel_id=1, source_target_pairs={{0,6},{1,7},{2,4},{3,5},{4,2},{5,3},{6,0},{7,1},{8,14},{9,15},{10,... | collective-permute-start | bytes 442376 | tf_op jit(solution)/shard_map/ppermute | solution.py:144
  25.1 10.7 %collective-permute-start.9 = (bf16[48,2176]{1,0:T(8,128)(2,1)S(1)}, bf16[48,2176]{1,0:T(8,128)(2,1)S(1)}, u32[]{:S(2)}, u32[]{:S(2)}) collective-permute-start(bf16[48,2176]{1,0:T(8,128)(2,1)S(1)} %get-tuple-element.46), channel_id=1, source_target_pairs={{0,2},{1,3},{2,0},{3,1},{4,6},{5,7},{6,4},{7,5},{8,10},{9,11},{10,... | collective-permute-start | bytes 626696 | tf_op jit(solution)/shard_map/ppermute | solution.py:144
  29.2 19.1 %collective-permute-start.7 = (bf16[48,2048]{1,0:T(8,128)(2,1)S(1)}, bf16[48,2048]{1,0:T(8,128)(2,1)S(1)}, u32[]{:S(2)}, u32[]{:S(2)}) collective-permute-start(bf16[48,2048]{1,0:T(8,128)(2,1)S(1)} %get-tuple-element.42), channel_id=1, source_target_pairs={{0,28},{1,29},{2,30},{3,31},{4,24},{5,25},{6,26},{7,27},{8,4},{9,5... | collective-permute-start | bytes 589832 | tf_op jit(solution)/shard_map/ppermute | solution.py:387
  39.2 9.6 %collective-permute-start.11 = (bf16[48,2048]{1,0:T(8,128)(2,1)S(1)}, bf16[48,2048]{1,0:T(8,128)(2,1)S(1)}, u32[]{:S(2)}, u32[]{:S(2)}) collective-permute-start(bf16[48,2048]{1,0:T(8,128)(2,1)S(1)} %get-tuple-element.57), channel_id=1, source_target_pairs={{0,26},{1,27},{2,24},{3,25},{4,30},{5,31},{6,28},{7,29},{8,2},{9,3... | collective-permute-start | bytes 589832 | tf_op jit(solution)/shard_map/ppermute | solution.py:387
  41.6 9.0 %collective-permute-start.13 = (bf16[24,2048]{1,0:T(8,128)(2,1)S(1)}, bf16[24,2048]{1,0:T(8,128)(2,1)S(1)}, u32[]{:S(2)}, u32[]{:S(2)}) collective-permute-start(bf16[24,2048]{1,0:T(8,128)(2,1)S(1)} %get-tuple-element.61), channel_id=1, source_target_pairs={{0,30},{1,31},{2,28},{3,29},{4,26},{5,27},{6,24},{7,25},{8,6},{9,7... | collective-permute-start | bytes 294920 | tf_op jit(solution)/shard_map/ppermute | solution.py:387
  44.8 7.7 %collective-permute-start.14 = (bf16[24,2048]{1,0:T(8,128)(2,1)S(1)}, bf16[24,2048]{1,0:T(8,128)(2,1)S(1)}, u32[]{:S(2)}, u32[]{:S(2)}) collective-permute-start(bf16[24,2048]{1,0:T(8,128)(2,1)S(1)} %get-tuple-element.63), channel_id=1, source_target_pairs={{0,31},{1,30},{2,29},{3,28},{4,27},{5,26},{6,25},{7,24},{8,7},{9,6... | collective-permute-start | bytes 294920 | tf_op jit(solution)/shard_map/ppermute | solution.py:387
  49.1 3.7 %collective-permute-start.12 = (bf16[64,2048]{1,0:T(8,128)(2,1)S(1)}, bf16[64,2048]{1,0:T(8,128)(2,1)S(1)}, u32[]{:S(2)}, u32[]{:S(2)}) collective-permute-start(bf16[64,2048]{1,0:T(8,128)(2,1)S(1)} %get-tuple-element.59), channel_id=1, source_target_pairs={{0,1},{1,0},{2,3},{3,2},{4,5},{5,4},{6,7},{7,6},{8,9},{9,8},{10,11... | collective-permute-start | bytes 786440 | tf_op jit(solution)/shard_map/ppermute | solution.py:144

commit v7 on v5

--- a/solution.py
+++ b/solution.py
@@ -135,7 +135,7 @@
 BF16 = jnp.bfloat16
 GATE_LANES = 128
 FACTORS_COST = 8*10**8
-THREE_COST = 2*10**9
+THREE_COST = 5 * 10**9
 K0_COST = 10 ** 10
 
 

time: 54.4 us -> 54.4 us (level)
  starting transfers between devices: 26.1 us -> 24.7 us
  waiting for transfers between devices: 6.41 us -> 7.81 us
    ppermute x5, waiting for transfers between devices: 1.9 us -> 3.3 us  [before_section(): return lax.ppermute(value, ('section', 'expert'), pairs)]
    ppermute x10, starting transfers between devices: 12.5 us -> 11.1 us  [swapped(): return lax.ppermute(value, 'expert', [(i, i ^ mask) for i in range(count)])]
  transfers between devices with their start and end apart: 15 -> 15, of which waited for: 6 -> 7; matrix products, arithmetic and copies ran while one was open for 0% -> 0% of each run, Pallas kernels for 32% -> 32%
where the time goes in v7:
time: 54.4 us; the launch traced here: 53.6 us
  starting transfers between devices  24.7 us (45%)
  Pallas kernels  18.1 us (33%)
  waiting for transfers between devices  7.81 us (14%)
  blocking collectives  2.17 us (4%)
  between operations  0.78 us (1%)
    pallas_call x12, Pallas kernels, local_call(): pl.pallas_call(kernel, out_shape=outs, scratch_shapes=scratch, compiler_p...  18.1 us
    ppermute x5, starting transfers between devices, before_section(): return lax.ppermute(value, ('section', 'expert'), pairs)  13.6 us
    ppermute x10, starting transfers between devices, swapped(): return lax.ppermute(value, 'expert', [(i, i ^ mask) for i in range(count)])  11.1 us
    ppermute x10, waiting for transfers between devices, swapped(): return lax.ppermute(value, 'expert', [(i, i ^ mask) for i in range(count)])  4.51 us
    ppermute x5, waiting for transfers between devices, before_section(): return lax.ppermute(value, ('section', 'expert'), pairs)  3.3 us
    all_gather x1, blocking collectives, on_device_pairs(): lax.all_gather(far_up, 'expert', axis=0, tiled=True, axis_index_groups=[[...  2.17 us
  transfers between devices with their start and end apart: 15, of which 7 were waited for; matrix products, arithmetic and copies ran while one was open for 0% of the time, Pallas kernels for 32%

profile of v7, /device:TPU:0, one launch (start us, length us, event | category | flops | bytes accessed | tf_op | source)
XLA Modules:
  0.0 53.6 jit_solution(5583938781385167173)
XLA Ops:
  0.6 0.5 collective-permute-start.2
  1.1 3.7 %collective-permute-start.6 = (bf16[64,2048]{1,0:T(8,128)(2,1)}, bf16[64,2048]{1,0:T(8,128)(2,1)S(1)}, u32[]{:S(2)}, u32[]{:S(2)}) collective-permute-start(bf16[64,2048]{1,0:T(8,128)(2,1)} %bitcast.25), channel_id=1, source_target_pairs={{0,4},{1,5},{2,6},{3,7},{4,0},{5,1},{6,2},{7,3},{8,12},{9,13},{10,... | collective-permute-start | bytes 786440 | tf_op jit(solution)/shard_map/ppermute | solution.py:144
  4.8 0.2 collective-permute-start
  5.0 0.3 collective-permute-start.1
  5.3 0.2 collective-permute-start.3
  5.6 0.7 %collective-permute-done.1.pair_gate = bf16[2,64]{1,0:T(2,128)(2,1)S(1)} collective-permute-done((bf16[2,64]{1,0:T(2,128)(2,1)}, bf16[2,64]{1,0:T(2,128)(2,1)S(1)}, u32[]{:S(2)}, u32[]{:S(2)}) %collective-permute-start.1) | collective-permute-done | bytes 288 | tf_op jit(solution)/shard_map/ppermute | solution.py:144
  6.3 0.0 collective-permute-done.pair_ids
  6.3 0.0 collective-permute-done.2.pair_up
  6.3 1.1 %collective-permute-done.3.pair_act = bf16[64,2,2,768]{3,2,1,0:T(2,128)(2,1)S(1)} collective-permute-done((bf16[64,2,2,768]{3,2,1,0:T(2,128)(2,1)}, bf16[64,2,2,768]{3,2,1,0:T(2,128)(2,1)S(1)}, u32[]{:S(2)}, u32[]{:S(2)}) %collective-permute-start.3) | collective-permute-done | bytes 393248 | tf_op jit(solution)/shard_map/ppermute | solution.py:144
  7.3 0.0 copy-done.3
  7.3 0.0 copy-done.4
  7.3 0.0 copy-done.5
  7.3 0.0 copy-done.6
  7.4 2.3 %shard_map.87 = (bf16[48,2048]{1,0:T(8,128)(2,1)S(1)}, bf16[48,3712]{1,0:T(8,128)(2,1)S(1)}, bf16[48,1536]{1,0:T(8,128)(2,1)S(1)}, bf16[48,1664]{1,0:T(8,128)(2,...) custom-call(bf16[128,128]{1,0:T(8,128)(2,1)S(1)} %shard_map.86.upto, s32[2,64]{1,0:T(2,128)S(1)} %bitcast.28, ...), custom_call_target="tpu_custom_call" | custom-call | tf_op jit(solution)/shard_map/pallas_call | solution.py:356
  9.7 1.6 %collective-permute-start.8 = (bf16[48,3712]{1,0:T(8,128)(2,1)S(1)}, bf16[48,3712]{1,0:T(8,128)(2,1)S(1)}, u32[]{:S(2)}, u32[]{:S(2)}) collective-permute-start(bf16[48,3712]{1,0:T(8,128)(2,1)S(1)} %get-tuple-element.45), channel_id=1, source_target_pairs={{0,2},{1,3},{2,0},{3,1},{4,6},{5,7},{6,4},{7,5},{8,10},{9,11},{10,... | collective-permute-start | bytes 1069064 | tf_op jit(solution)/shard_map/ppermute | solution.py:144
  11.4 0.3 collective-permute-start.5
  11.7 0.0 copy-done
  11.7 0.0 copy-done.1
  11.7 3.3 %shard_map.88 = (bf16[48,2176]{1,0:T(8,128)(2,1)S(1)}, bf16[48,768]{1,0:T(8,128)(2,1)S(1)}) custom-call(bf16[48,2048]{1,0:T(8,128)(2,1)S(1)} %get-tuple-element.33.up.up_a, bf16[48,1536]{1,0:T(8,128)(2,1)S(1)} %get-tuple-element.34.saved, bf16[48,128]{1,0:T(8,128)(2,1)S(1)} %get-tuple-element.35.gate, bf16[48,1664]{1,0:T(8,128)(2,1)S(1)} %get-tuple-element.36.beside, ...), custom_call_target="tpu_custom_call" | custom-call | tf_op jit(solution)/shard_map/pallas_call | solution.py:356
  15.0 2.5 %collective-permute-start.4 = (bf16[48,2176]{1,0:T(8,128)(2,1)S(1)}, bf16[48,2176]{1,0:T(8,128)(2,1)S(1)}, u32[]{:S(2)}, u32[]{:S(2)}) collective-permute-start(bf16[48,2176]{1,0:T(8,128)(2,1)S(1)} %get-tuple-element.37), channel_id=1, source_target_pairs={{0,24},{1,25},{2,26},{3,27},{4,28},{5,29},{6,30},{7,31},{8,0},{9,1... | collective-permute-start | bytes 626696 | tf_op jit(solution)/shard_map/ppermute | solution.py:377
  17.5 0.4 collective-permute-done.6
  17.9 2.2 %all_gather.3.both_up = bf16[128,2048]{1,0:T(8,128)(2,1)S(1)} all-gather(bf16[64,2048]{1,0:T(8,128)(2,1)S(1)} %collective-permute-done.6), channel_id=1, replica_groups={{0,1},{2,3},{4,5},{6,7},{8,9},{10,11},{12,13},{14,15},{16,17},{18,19},{..., dimensions={0}, use_global_device_ids=true | all-gather | bytes 786432 | tf_op jit(solution)/shard_map/all_gather | solution.py:411
  20.1 3.3 %collective-permute-start.10 = (bf16[48,1536]{1,0:T(8,128)(2,1)S(1)}, bf16[48,1536]{1,0:T(8,128)(2,1)S(1)}, u32[]{:S(2)}, u32[]{:S(2)}) collective-permute-start(bf16[48,1536]{1,0:T(8,128)(2,1)S(1)} %get-tuple-element.48), channel_id=1, source_target_pairs={{0,6},{1,7},{2,4},{3,5},{4,2},{5,3},{6,0},{7,1},{8,14},{9,15},{10,... | collective-permute-start | bytes 442376 | tf_op jit(solution)/shard_map/ppermute | solution.py:144
  23.4 1.2 %collective-permute-done.5.saved_2.saved = bf16[48,1664]{1,0:T(8,128)(2,1)S(1)} collective-permute-done((bf16[48,1664]{1,0:T(8,128)(2,1)S(1)}, bf16[48,1664]{1,0:T(8,128)(2,1)S(1)}, u32[]{:S(2)}, u32[]{:S(2)}) %collective-permute-start.5) | collective-permute-done | bytes 159776 | tf_op jit(solution)/shard_map/ppermute | solution.py:144
  24.6 0.5 shard_map.89
  25.1 0.8 %collective-permute-start.9 = (bf16[48,2176]{1,0:T(8,128)(2,1)S(1)}, bf16[48,2176]{1,0:T(8,128)(2,1)S(1)}, u32[]{:S(2)}, u32[]{:S(2)}) collective-permute-start(bf16[48,2176]{1,0:T(8,128)(2,1)S(1)} %get-tuple-element.46), channel_id=1, source_target_pairs={{0,2},{1,3},{2,0},{3,1},{4,6},{5,7},{6,4},{7,5},{8,10},{9,11},{10,... | collective-permute-start | bytes 626696 | tf_op jit(solution)/shard_map/ppermute | solution.py:144
  25.9 0.0 collective-permute-done.4.rows_0
  25.9 3.3 %shard_map.90 = (bf16[48,2048]{1,0:T(8,128)(2,1)S(1)}, bf16[48,768]{1,0:T(8,128)(2,1)S(1)}) custom-call(bf16[48,2048]{1,0:T(8,128)(2,1)S(1)} %get-tuple-element.40.up.up_b, bf16[48,1664]{1,0:T(8,128)(2,1)S(1)} %collective-permute-done.5.saved_2.saved, bf16[48,128]{1,0:T(8,128)(2,1)S(1)} %get-tuple-element.41.gate, bf16[768,2048]{1,0:T(8,128)(2,1)S(1)} %bitcast.14, ...), custom_call_target="tpu_custom_call" | custom-call | tf_op jit(solution)/shard_map/pallas_call | solution.py:356
  29.2 5.3 %collective-permute-start.7 = (bf16[48,2048]{1,0:T(8,128)(2,1)S(1)}, bf16[48,2048]{1,0:T(8,128)(2,1)S(1)}, u32[]{:S(2)}, u32[]{:S(2)}) collective-permute-start(bf16[48,2048]{1,0:T(8,128)(2,1)S(1)} %get-tuple-element.42), channel_id=1, source_target_pairs={{0,28},{1,29},{2,30},{3,31},{4,24},{5,25},{6,26},{7,27},{8,4},{9,5... | collective-permute-start | bytes 589832 | tf_op jit(solution)/shard_map/ppermute | solution.py:377
  34.4 0.0 collective-permute-done.10.saved
  34.4 0.0 collective-permute-done.8.near.up_c
  34.4 0.2 shard_map.91
  34.6 1.2 %collective-permute-done.9.up_3.up_d = bf16[48,2176]{1,0:T(8,128)(2,1)S(1)} collective-permute-done((bf16[48,2176]{1,0:T(8,128)(2,1)S(1)}, bf16[48,2176]{1,0:T(8,128)(2,1)S(1)}, u32[]{:S(2)}, u32[]{:S(2)}) %collective-permute-start.9) | collective-permute-done | bytes 208928 | tf_op jit(solution)/shard_map/ppermute | solution.py:144
  35.8 3.5 %shard_map.92 = (bf16[48,2048]{1,0:T(8,128)(2,1)S(1)}, bf16[24,2048]{1,0:T(8,128)(2,1)S(1)}, bf16[24,2048]{1,0:T(8,128)(2,1)S(1)}, bf16[96,768]{1,0:T(8,128)(2,1)S(1)}) custom-call(bf16[48,3712]{1,0:T(8,128)(2,1)S(1)} %collective-permute-done.8.near.up_c, bf16[48,2176]{1,0:T(8,128)(2,1)S(1)} %collective-permute-done.9.up_3.up_d, ...), custom_call_target="tpu_custom_call" | custom-call | tf_op jit(solution)/shard_map/pallas_call | solution.py:356
  39.2 2.4 %collective-permute-start.11 = (bf16[48,2048]{1,0:T(8,128)(2,1)S(1)}, bf16[48,2048]{1,0:T(8,128)(2,1)S(1)}, u32[]{:S(2)}, u32[]{:S(2)}) collective-permute-start(bf16[48,2048]{1,0:T(8,128)(2,1)S(1)} %get-tuple-element.57), channel_id=1, source_target_pairs={{0,26},{1,27},{2,24},{3,25},{4,30},{5,31},{6,28},{7,29},{8,2},{9,3... | collective-permute-start | bytes 589832 | tf_op jit(solution)/shard_map/ppermute | solution.py:377
  41.6 3.2 %collective-permute-start.13 = (bf16[24,2048]{1,0:T(8,128)(2,1)S(1)}, bf16[24,2048]{1,0:T(8,128)(2,1)S(1)}, u32[]{:S(2)}, u32[]{:S(2)}) collective-permute-start(bf16[24,2048]{1,0:T(8,128)(2,1)S(1)} %get-tuple-element.61), channel_id=1, source_target_pairs={{0,30},{1,31},{2,28},{3,29},{4,26},{5,27},{6,24},{7,25},{8,6},{9,7... | collective-permute-start | bytes 294920 | tf_op jit(solution)/shard_map/ppermute | solution.py:377
  44.8 0.2 collective-permute-start.14
  45.0 3.3 %shard_map.93 = bf16[768,2048]{1,0:T(8,128)(2,1)} custom-call(bf16[48,768]{1,0:T(8,128)(2,1)S(1)} %get-tuple-element.43.scaled_a, bf16[48,768]{1,0:T(8,128)(2,1)S(1)} %get-tuple-element.44.scaled_b, bf16[96,768]{1,0:T(8,128)(2,1)S(1)} %get-tuple-element.53.scaled_c, bf16[48,2048]{1,0:T(8,128)(2,1)S(1)} %get-tuple-element.33.up.up_a, ...), custom_call_target="tpu_custom_call" | custom-call | tf_op jit(solution)/shard_map/pallas_call | solution.py:356
  48.3 0.0 collective-permute-done.7.rows_2
  48.3 0.5 shard_map.94
  48.8 1.6 %collective-permute-done.13.rows_6 = bf16[24,2048]{1,0:T(8,128)(2,1)S(1)} collective-permute-done((bf16[24,2048]{1,0:T(8,128)(2,1)S(1)}, bf16[24,2048]{1,0:T(8,128)(2,1)S(1)}, u32[]{:S(2)}, u32[]{:S(2)}) %collective-permute-start.13) | collective-permute-done | bytes 98336 | tf_op jit(solution)/shard_map/ppermute | solution.py:377
  50.4 0.0 collective-permute-done.11.rows_1
  50.4 0.3 shard_map.95
  50.7 0.1 collective-permute-start.12
  50.8 1.7 %collective-permute-done.14.rows_7 = bf16[24,2048]{1,0:T(8,128)(2,1)S(1)} collective-permute-done((bf16[24,2048]{1,0:T(8,128)(2,1)S(1)}, bf16[24,2048]{1,0:T(8,128)(2,1)S(1)}, u32[]{:S(2)}, u32[]{:S(2)}) %collective-permute-start.14) | collective-permute-done | bytes 98336 | tf_op jit(solution)/shard_map/ppermute | solution.py:377
  52.5 0.3 shard_map.96.part
  52.8 0.0 collective-permute-done.12.other
  52.8 0.8 %shard_map.97 = bf16[64,2048]{1,0:T(8,128)(2,1)} custom-call(f32[64,2048]{1,0:T(8,128)S(1)} %get-tuple-element.58.own, bf16[64,2048]{1,0:T(8,128)(2,1)S(1)} %collective-permute-done.12.other, f32[64,2048]{1,0:T(8,128)S(1)} %shard_map.96.part), custom_call_target="tpu_custom_call" | custom-call | tf_op jit(solution)/shard_map/pallas_call | solution.py:356
  (9 shorter events, 0.0 us)
Async XLA Ops:
  0.6 5.7 %collective-permute-start.2 = (bf16[64,2048]{1,0:T(8,128)(2,1)}, bf16[64,2048]{1,0:T(8,128)(2,1)S(1)}, u32[]{:S(2)}, u32[]{:S(2)}) collective-permute-start(bf16[64,2048]{1,0:T(8,128)(2,1)} %bitcast.24), channel_id=1, source_target_pairs={{0,1},{1,0},{2,3},{3,2},{4,5},{5,4},{6,7},{7,6},{8,9},{9,8},{10,11... | collective-permute-start | bytes 786440 | tf_op jit(solution)/shard_map/ppermute | solution.py:144
  1.1 16.8 %collective-permute-start.6 = (bf16[64,2048]{1,0:T(8,128)(2,1)}, bf16[64,2048]{1,0:T(8,128)(2,1)S(1)}, u32[]{:S(2)}, u32[]{:S(2)}) collective-permute-start(bf16[64,2048]{1,0:T(8,128)(2,1)} %bitcast.25), channel_id=1, source_target_pairs={{0,4},{1,5},{2,6},{3,7},{4,0},{5,1},{6,2},{7,3},{8,12},{9,13},{10,... | collective-permute-start | bytes 786440 | tf_op jit(solution)/shard_map/ppermute | solution.py:144
  4.8 1.5 %collective-permute-start = (s32[2,64]{1,0:T(2,128)}, s32[2,64]{1,0:T(2,128)S(1)}, u32[]{:S(2)}, u32[]{:S(2)}) collective-permute-start(s32[2,64]{1,0:T(2,128)} %bitcast.27), channel_id=1, source_target_pairs={{0,1},{1,0},{2,3},{3,2},{4,5},{5,4},{6,7},{7,6},{8,9},{9,8},{10,11... | collective-permute-start | bytes 1544 | tf_op jit(solution)/shard_map/ppermute | solution.py:144
  5.0 1.3 %collective-permute-start.1 = (bf16[2,64]{1,0:T(2,128)(2,1)}, bf16[2,64]{1,0:T(2,128)(2,1)S(1)}, u32[]{:S(2)}, u32[]{:S(2)}) collective-permute-start(bf16[2,64]{1,0:T(2,128)(2,1)} %bitcast.29), channel_id=1, source_target_pairs={{0,1},{1,0},{2,3},{3,2},{4,5},{5,4},{6,7},{7,6},{8,9},{9,8},{10,11... | collective-permute-start | bytes 776 | tf_op jit(solution)/shard_map/ppermute | solution.py:144
  5.3 2.0 %copy-start.3 = (bf16[1,64,2,2,768]{4,3,2,1,0:T(2,128)(2,1)S(1)}, bf16[1,64,2,2,768]{4,3,2,1,0:T(2,128)(2,1)}, u32[]{:S(2)}) copy-start(bf16[1,64,2,2,768]{4,3,2,1,0:T(2,128)(2,1)} %param.8) | copy-start | bytes 1179652
  5.3 2.0 %copy-start.4 = (bf16[1,64,2048]{2,1,0:T(8,128)(2,1)S(1)}, bf16[1,64,2048]{2,1,0:T(8,128)(2,1)}, u32[]{:S(2)}) copy-start(bf16[1,64,2048]{2,1,0:T(8,128)(2,1)} %param.7) | copy-start | bytes 786436
  5.3 2.0 %copy-start.5 = (s32[1,64,2]{1,2,0:T(2,128)S(1)}, s32[1,64,2]{1,2,0:T(2,128)}, u32[]{:S(2)}) copy-start(s32[1,64,2]{1,2,0:T(2,128)} %param.9) | copy-start | bytes 1540
  5.3 2.0 %copy-start.6 = (bf16[1,64,2]{1,2,0:T(2,128)(2,1)S(1)}, bf16[1,64,2]{1,2,0:T(2,128)(2,1)}, u32[]{:S(2)}) copy-start(bf16[1,64,2]{1,2,0:T(2,128)(2,1)} %param.10) | copy-start | bytes 772
  5.3 2.0 %collective-permute-start.3 = (bf16[64,2,2,768]{3,2,1,0:T(2,128)(2,1)}, bf16[64,2,2,768]{3,2,1,0:T(2,128)(2,1)S(1)}, u32[]{:S(2)}, u32[]{:S(2)}) collective-permute-start(bf16[64,2,2,768]{3,2,1,0:T(2,128)(2,1)} %bitcast.22), channel_id=1, source_target_pairs={{0,1},{1,0},{2,3},{3,2},{4,5},{5,4},{6,7},{7,6},{8,9},{9,8},{10,11... | collective-permute-start | bytes 1179656 | tf_op jit(solution)/shard_map/ppermute | solution.py:144
  5.6 6.1 %copy-start = (bf16[1,768,2048]{2,1,0:T(8,128)(2,1)S(1)}, bf16[1,768,2048]{2,1,0:T(8,128)(2,1)}, u32[]{:S(2)}) copy-start(bf16[1,768,2048]{2,1,0:T(8,128)(2,1)} %param.13) | copy-start | bytes 9437188
  5.6 6.1 %copy-start.1 = (bf16[1,2048,768]{2,1,0:T(8,128)(2,1)S(1)}, bf16[1,2048,768]{2,1,0:T(8,128)(2,1)}, u32[]{:S(2)}) copy-start(bf16[1,2048,768]{2,1,0:T(8,128)(2,1)} %param.11) | copy-start | bytes 9437188
  5.6 6.1 %copy-start.2 = (bf16[1,2048,768]{2,1,0:T(8,128)(2,1)S(1)}, bf16[1,2048,768]{2,1,0:T(8,128)(2,1)}, u32[]{:S(2)}) copy-start(bf16[1,2048,768]{2,1,0:T(8,128)(2,1)} %param.12) | copy-start | bytes 9437188
  9.7 24.7 %collective-permute-start.8 = (bf16[48,3712]{1,0:T(8,128)(2,1)S(1)}, bf16[48,3712]{1,0:T(8,128)(2,1)S(1)}, u32[]{:S(2)}, u32[]{:S(2)}) collective-permute-start(bf16[48,3712]{1,0:T(8,128)(2,1)S(1)} %get-tuple-element.45), channel_id=1, source_target_pairs={{0,2},{1,3},{2,0},{3,1},{4,6},{5,7},{6,4},{7,5},{8,10},{9,11},{10,... | collective-permute-start | bytes 1069064 | tf_op jit(solution)/shard_map/ppermute | solution.py:144
  11.4 13.2 %collective-permute-start.5 = (bf16[48,1664]{1,0:T(8,128)(2,1)S(1)}, bf16[48,1664]{1,0:T(8,128)(2,1)S(1)}, u32[]{:S(2)}, u32[]{:S(2)}) collective-permute-start(bf16[48,1664]{1,0:T(8,128)(2,1)S(1)} %get-tuple-element.36.beside), channel_id=1, source_target_pairs={{0,4},{1,5},{2,6},{3,7},{4,0},{5,1},{6,2},{7,3},{8,12},{9,13},{10,... | collective-permute-start | bytes 479240 | tf_op jit(solution)/shard_map/ppermute | solution.py:144
  15.0 10.9 %collective-permute-start.4 = (bf16[48,2176]{1,0:T(8,128)(2,1)S(1)}, bf16[48,2176]{1,0:T(8,128)(2,1)S(1)}, u32[]{:S(2)}, u32[]{:S(2)}) collective-permute-start(bf16[48,2176]{1,0:T(8,128)(2,1)S(1)} %get-tuple-element.37), channel_id=1, source_target_pairs={{0,24},{1,25},{2,26},{3,27},{4,28},{5,29},{6,30},{7,31},{8,0},{9,1... | collective-permute-start | bytes 626696 | tf_op jit(solution)/shard_map/ppermute | solution.py:377
  20.1 14.4 %collective-permute-start.10 = (bf16[48,1536]{1,0:T(8,128)(2,1)S(1)}, bf16[48,1536]{1,0:T(8,128)(2,1)S(1)}, u32[]{:S(2)}, u32[]{:S(2)}) collective-permute-start(bf16[48,1536]{1,0:T(8,128)(2,1)S(1)} %get-tuple-element.48), channel_id=1, source_target_pairs={{0,6},{1,7},{2,4},{3,5},{4,2},{5,3},{6,0},{7,1},{8,14},{9,15},{10,... | collective-permute-start | bytes 442376 | tf_op jit(solution)/shard_map/ppermute | solution.py:144
  25.1 10.7 %collective-permute-start.9 = (bf16[48,2176]{1,0:T(8,128)(2,1)S(1)}, bf16[48,2176]{1,0:T(8,128)(2,1)S(1)}, u32[]{:S(2)}, u32[]{:S(2)}) collective-permute-start(bf16[48,2176]{1,0:T(8,128)(2,1)S(1)} %get-tuple-element.46), channel_id=1, source_target_pairs={{0,2},{1,3},{2,0},{3,1},{4,6},{5,7},{6,4},{7,5},{8,10},{9,11},{10,... | collective-permute-start | bytes 626696 | tf_op jit(solution)/shard_map/ppermute | solution.py:144
  29.2 19.1 %collective-permute-start.7 = (bf16[48,2048]{1,0:T(8,128)(2,1)S(1)}, bf16[48,2048]{1,0:T(8,128)(2,1)S(1)}, u32[]{:S(2)}, u32[]{:S(2)}) collective-permute-start(bf16[48,2048]{1,0:T(8,128)(2,1)S(1)} %get-tuple-element.42), channel_id=1, source_target_pairs={{0,28},{1,29},{2,30},{3,31},{4,24},{5,25},{6,26},{7,27},{8,4},{9,5... | collective-permute-start | bytes 589832 | tf_op jit(solution)/shard_map/ppermute | solution.py:377
  39.2 11.2 %collective-permute-start.11 = (bf16[48,2048]{1,0:T(8,128)(2,1)S(1)}, bf16[48,2048]{1,0:T(8,128)(2,1)S(1)}, u32[]{:S(2)}, u32[]{:S(2)}) collective-permute-start(bf16[48,2048]{1,0:T(8,128)(2,1)S(1)} %get-tuple-element.57), channel_id=1, source_target_pairs={{0,26},{1,27},{2,24},{3,25},{4,30},{5,31},{6,28},{7,29},{8,2},{9,3... | collective-permute-start | bytes 589832 | tf_op jit(solution)/shard_map/ppermute | solution.py:377
  41.6 8.8 %collective-permute-start.13 = (bf16[24,2048]{1,0:T(8,128)(2,1)S(1)}, bf16[24,2048]{1,0:T(8,128)(2,1)S(1)}, u32[]{:S(2)}, u32[]{:S(2)}) collective-permute-start(bf16[24,2048]{1,0:T(8,128)(2,1)S(1)} %get-tuple-element.61), channel_id=1, source_target_pairs={{0,30},{1,31},{2,28},{3,29},{4,26},{5,27},{6,24},{7,25},{8,6},{9,7... | collective-permute-start | bytes 294920 | tf_op jit(solution)/shard_map/ppermute | solution.py:377
  44.8 7.7 %collective-permute-start.14 = (bf16[24,2048]{1,0:T(8,128)(2,1)S(1)}, bf16[24,2048]{1,0:T(8,128)(2,1)S(1)}, u32[]{:S(2)}, u32[]{:S(2)}) collective-permute-start(bf16[24,2048]{1,0:T(8,128)(2,1)S(1)} %get-tuple-element.63), channel_id=1, source_target_pairs={{0,31},{1,30},{2,29},{3,28},{4,27},{5,26},{6,25},{7,24},{8,7},{9,6... | collective-permute-start | bytes 294920 | tf_op jit(solution)/shard_map/ppermute | solution.py:377
  50.7 2.1 %collective-permute-start.12 = (bf16[64,2048]{1,0:T(8,128)(2,1)S(1)}, bf16[64,2048]{1,0:T(8,128)(2,1)S(1)}, u32[]{:S(2)}, u32[]{:S(2)}) collective-permute-start(bf16[64,2048]{1,0:T(8,128)(2,1)S(1)} %get-tuple-element.59), channel_id=1, source_target_pairs={{0,1},{1,0},{2,3},{3,2},{4,5},{5,4},{6,7},{7,6},{8,9},{9,8},{10,11... | collective-permute-start | bytes 786440 | tf_op jit(solution)/shard_map/ppermute | solution.py:144
